TPU v7x, 32 devices: a whole 2x2x4 slice. The times are simulated.
32 devices in a mesh: groups: 2 (over y), seq: 4 (over z), tp: 2 (over x), rep: 2 (over core).
Axes of the slice: x: 2, y: 2, z: 4, core: 2. Of those that a mesh axis runs over, the one named last changes fastest.
Arguments:
- queries: bfloat16 [2, 128, 8192], P('rep', ('groups', 'seq', 'tp')), parts along dimension 1, may hold values from -8 to 8
- fresh_key_rows: bfloat16 [2, 128, 1024], P('rep', ('groups', 'seq', 'tp')), parts along dimension 1, may hold values from -8 to 8
- fresh_value_rows: bfloat16 [2, 128, 1024], P('rep', ('groups', 'seq', 'tp')), parts along dimension 1, may hold values from -8 to 8
- visible: int32 [2, 128], P('rep', 'groups'), parts along dimension 1, may hold values from 128 to 2048, as said below
- prefix_keys: bfloat16 [4096, 1024], P(('groups', 'seq'), 'tp'), parts along dimension 0, may hold values from -6 to 6
- cached_value_rows: bfloat16 [4096, 1024], P(('groups', 'seq'), 'tp'), parts along dimension 0, may hold values from -8 to 8
- out_weight: bfloat16 [8192, 8192], P('tp', 'seq'), may hold values from -0.0625 to 0.0625
Outputs:
- mixed: bfloat16 [2, 128, 8192], P('rep', ('groups', 'tp'), 'seq'), parts along dimension 1
There are 2 independent parts, one for each index of `groups`. A program takes and returns all parts, laid end to end along the dimension named above; an argument that names none is the same for every part. Nothing has to cross between parts.
Inputs may be any that keep to these rules, and one draw needn't show every extreme that they name: Token i of half r sees prefix positions 0 to visible[r, i] - 1; in each half some token sees the whole prefix.
All inputs are finite; a program needn't handle non-finite values.
Results may differ from a plain program's by a relative error of at most 0.0051.
Values may be sent and summed in bfloat16 or wider, within the bound.
No kernel may reach another device: no remote copies, remote signals or barrier semaphores. Data moves between devices by JAX's collectives and lax.ppermute only.
A program may use at most 64 MiB of HBM per device.

v0:
```python
import math

import jax
import jax.numpy as jnp
from jax import lax
from jax.sharding import PartitionSpec as P

HEAD_WIDTH = 128


def block_partial(query_heads, lengths, key_rows, value_rows, offset):
    kv_heads = query_heads.shape[1]
    row_count = key_rows.shape[0]
    step_rows = math.gcd(row_count, 512)
    logit_scale = 1.0 / math.sqrt(HEAD_WIDTH)
    stat_shape = query_heads.shape[:3]

    def masked_scores(turn_index):
        first_row = turn_index * step_rows
        key_block = key_rows.reshape(step_rows, kv_heads, HEAD_WIDTH)
        scores = (
            jnp.einsum("tkgd,pkd->tkgp", query_heads, key_block, preferred_element_type=jnp.float32)
            * logit_scale
        )
        position = offset + first_row + jnp.arange(step_rows, dtype=jnp.int32)
        visible_mask = (position[None, :] < lengths[:, None])[:, None, None, :]
        return (scores, visible_mask, first_row)

    def peak_step(turn_index, peak_now):
        scores, visible_mask, first_row = masked_scores(turn_index)
        return jnp.maximum(peak_now, jnp.max(jnp.where(visible_mask, scores, -jnp.inf), axis=-1))

    block_peak = lax.fori_loop(
        0, row_count // step_rows, peak_step, jnp.full(stat_shape, -jnp.inf, jnp.float32)
    )
    anchor = jnp.where(jnp.isinf(block_peak), 0.0, block_peak)

    def weight_step(turn_index, state_now):
        sum_now, acc_now = state_now
        scores, visible_mask, first_row = masked_scores(turn_index)
        value_block = value_rows.reshape(step_rows, kv_heads, HEAD_WIDTH)
        weights = jnp.where(visible_mask, jnp.exp(scores - anchor[..., None]), 0.0)
        sum_now = sum_now + jnp.sum(weights, axis=-1)
        acc_now = acc_now + jnp.einsum(
            "tkgp,pkd->tkgd",
            weights.astype(jnp.bfloat16),
            value_block,
            preferred_element_type=jnp.float32,
        )
        return (sum_now, acc_now)

    block_sum, block_acc = lax.fori_loop(
        0,
        row_count // step_rows,
        weight_step,
        (jnp.zeros(stat_shape, jnp.float32), jnp.zeros(query_heads.shape, jnp.float32)),
    )
    return (block_peak, block_sum, block_acc)


def shards(
    queries, fresh_key_rows, fresh_value_rows, visible, prefix_keys, cached_value_rows, out_weight
):
    query_rows, self_key_rows, own_values = (
        lax.all_to_all(queries[0], "tp", split_axis=1, concat_axis=0, tiled=True),
        lax.all_to_all(fresh_key_rows[0], "tp", split_axis=1, concat_axis=0, tiled=True),
        lax.all_to_all(fresh_value_rows[0], "tp", split_axis=1, concat_axis=0, tiled=True),
    )
    kv_heads = prefix_keys.shape[1] // HEAD_WIDTH
    tok_rows = query_rows.shape[0]
    block_rows = prefix_keys.shape[0]
    per_group = query_rows.shape[1] // (kv_heads * HEAD_WIDTH)
    seq_index = lax.axis_index("seq")
    query_heads = query_rows.reshape(tok_rows, kv_heads, per_group, HEAD_WIDTH)
    self_key_rows = self_key_rows.reshape(tok_rows, kv_heads, HEAD_WIDTH)
    own_vectors = own_values.reshape(tok_rows, kv_heads, 1, HEAD_WIDTH).astype(jnp.float32)
    self_score_row = jnp.einsum(
        "tkgd,tkd->tkg", query_heads, self_key_rows, preferred_element_type=jnp.float32
    ) * (1.0 / math.sqrt(HEAD_WIDTH))
    seq_count = lax.axis_size("seq")
    everyone = lax.all_gather(query_rows, "seq", axis=0, tiled=True)
    blocks = everyone.reshape(seq_count, tok_rows, kv_heads, per_group, HEAD_WIDTH)
    all_lengths = visible[0].reshape(seq_count, tok_rows)
    prefix_start = seq_index * block_rows

    def partial_block(item_pair):
        return block_partial(
            item_pair[0], item_pair[1], prefix_keys, cached_value_rows, prefix_start
        )

    part_max, part_sum, part_acc = lax.map(partial_block, (blocks, all_lengths))
    part_max, part_sum, part_acc = (
        lax.all_to_all(part_max, "seq", split_axis=0, concat_axis=0, tiled=True),
        lax.all_to_all(part_sum, "seq", split_axis=0, concat_axis=0, tiled=True),
        lax.all_to_all(part_acc, "seq", split_axis=0, concat_axis=0, tiled=True),
    )
    run_max = jnp.max(part_max, axis=0)
    anchor = jnp.where(jnp.isinf(run_max), 0.0, run_max)
    part_factor = jnp.exp(part_max - anchor[None])
    run_sum = jnp.sum(part_sum * part_factor, axis=0)
    run_acc = jnp.sum(part_acc * part_factor[..., None], axis=0)
    row_peak = jnp.maximum(run_max, self_score_row)
    fade = jnp.exp(run_max - row_peak)
    own_weight = jnp.exp(self_score_row - row_peak)
    own_rounded = lax.optimization_barrier(own_weight.astype(jnp.bfloat16)).astype(jnp.float32)
    total_sum = run_sum * fade + own_weight
    total_acc = run_acc * fade[..., None] + own_rounded[..., None] * own_vectors
    context = (
        (total_acc / total_sum[..., None])
        .astype(jnp.bfloat16)
        .reshape(tok_rows, kv_heads * per_group * HEAD_WIDTH)
    )
    partial_out = jnp.dot(
        lax.all_gather(context, "seq", axis=0, tiled=True),
        out_weight,
        preferred_element_type=jnp.float32,
    )
    summed = lax.psum_scatter(partial_out, "tp", scatter_dimension=0, tiled=True)
    return summed.astype(jnp.bfloat16)[None]


def solution(mesh):
    in_specs = (
        P("rep", ("groups", "seq", "tp"), None),
        P("rep", ("groups", "seq", "tp"), None),
        P("rep", ("groups", "seq", "tp"), None),
        P("rep", "groups"),
        P(("groups", "seq"), "tp"),
        P(("groups", "seq"), "tp"),
        P("tp", "seq"),
    )
    out_specs = P("rep", ("groups", "tp"), "seq")
    return jax.shard_map(shards, mesh=mesh, in_specs=in_specs, out_specs=out_specs, check_vma=False)
```

profile of v0, /device:TPU:0, one launch (start us, length us, event | category | flops | bytes accessed | tf_op | source)
XLA Modules:
  0.0 137.8 jit_solution(3093022515407522001)
XLA Ops:
  6.5 4.2 %all-to-all-start = ((bf16[8,2,4096]{2,0,1:T(8,128)(2,1)}), bf16[8,2,4096]{2,0,1:T(8,128)(2,1)S(1)}, u32[]{:S(2)}, u32[]{:S(2)}) async-start(bf16[8,2,4096]{2,0,1:T(8,128)(2,1)} %bitcast.96), calls=%async_computation | async-start | bytes 262144 | tf_op jit(solution)/shard_map/all_to_all | solution.py:65
  11.3 1.4 reduce.3
  12.8 1.2 reshape.123
  14.0 1.2 reshape.124
  15.3 3.3 %all-to-all-start.3 = ((bf16[8,2,512]{2,0,1:T(8,128)(2,1)}), bf16[8,2,512]{2,0,1:T(8,128)(2,1)S(1)}, u32[]{:S(2)}, u32[]{:S(2)}) async-start(bf16[8,2,512]{2,0,1:T(8,128)(2,1)} %bitcast.101), calls=%async_computation.3 | async-start | bytes 32768 | tf_op jit(solution)/shard_map/all_to_all | solution.py:66
  18.6 16.4 %all_gather.6 = bf16[64,4096]{1,0:T(8,128)(2,1)S(1)} all-gather(bf16[16,4096]{1,0:T(8,128)(2,1)S(1)} %bitcast.91), channel_id=1, replica_groups=mesh['groups'=2,'seq'=4,'tp'=2,'rep'=2] {'seq'}, dimensions={0}, use_global_device_ids=true | all-gather | bytes 655360 | tf_op jit(solution)/shard_map/all_gather | solution.py:81
  35.1 3.2 %all-to-all-start.4 = ((bf16[8,2,512]{2,0,1:T(8,128)(2,1)}), bf16[8,2,512]{2,0,1:T(8,128)(2,1)S(1)}, u32[]{:S(2)}, u32[]{:S(2)}) async-start(bf16[8,2,512]{2,0,1:T(8,128)(2,1)} %bitcast.102), calls=%async_computation.4 | async-start | bytes 32768 | tf_op jit(solution)/shard_map/all_to_all | solution.py:67
  38.3 8.6 %while.4 = (s32[]{:T(128)}, f32[4,16,4,8]{1,3,2,0:T(8,128)S(1)}, f32[4,16,4,8]{1,3,2,0:T(8,128)S(1)}, f32[4,16,4,8,128]{4,3,1,2,0:T(8,128)}, s32[]{:T(128)}, /*i...) while((s32[]{:T(128)}, f32[4,16,4,8]{1,3,2,0:T(8,128)S(1)}, ...), condition=%wide.wide.region_3.4_spmd, body=%wide.wide.region_0.3_spmd.sunk | while | flops 136586240 | bytes 4710737 | solution.py:91
  39.3 1.1 fusion.40
  41.4 1.1 fusion.40
  43.6 1.1 fusion.40
  45.7 1.1 fusion.40
  46.9 0.7 reshape.121
  47.6 5.4 %all-to-all-start.5 = ((f32[4,1,512]{2,1,0:T(1,128)}), f32[4,1,512]{2,1,0:T(1,128)S(1)}, u32[]{:S(2)}, u32[]{:S(2)}) async-start(f32[4,1,512]{2,1,0:T(1,128)} %reshape.121), calls=%async_computation.5 | async-start | bytes 16384 | tf_op jit(solution)/shard_map/all_to_all | solution.py:94
  53.1 5.5 %all-to-all-done.5 = f32[4,1,512]{2,1,0:T(1,128)S(1)} async-done(((f32[4,1,512]{2,1,0:T(1,128)}), f32[4,1,512]{2,1,0:T(1,128)S(1)}, u32[]{:S(2)}, u32[]{:S(2)}) %all-to-all-start.5) | async-done | bytes 8224 | tf_op jit(solution)/shard_map/all_to_all | solution.py:94
  58.6 7.9 %all_to_all.63 = f32[4,1,512]{2,1,0:T(1,128)S(1)} all-to-all(f32[4,1,512]{2,1,0:T(1,128)S(1)} %reshape.119), channel_id=1, replica_groups=mesh['groups'=2,'seq'=4,'tp'=2,'rep'=2] {'seq'}, dimensions={0} | all-to-all | bytes 16384 | tf_op jit(solution)/shard_map/all_to_all | solution.py:93
  66.5 3.5 %all-to-all-start.1 = ((f32[4,16,4,8,128]{4,3,1,2,0:T(8,128)}), f32[4,16,4,8,128]{4,3,1,2,0:T(8,128)S(1)}, u32[]{:S(2)}, u32[]{:S(2)}) async-start(f32[4,16,4,8,128]{4,3,1,2,0:T(8,128)} %get-tuple-element.94), calls=%async_computation.1 | async-start | bytes 2097152 | tf_op jit(solution)/shard_map/all_to_all | solution.py:95
  71.0 0.7 reduce.4
  71.7 0.7 reduce.5
  72.9 17.1 %all-to-all-done.1 = f32[4,16,4,8,128]{4,3,1,2,0:T(8,128)S(1)} async-done(((f32[4,16,4,8,128]{4,3,1,2,0:T(8,128)}), f32[4,16,4,8,128]{4,3,1,2,0:T(8,128)S(1)}, u32[]{:S(2)}, u32[]{:S(2)}) %all-to-all-start.1) | async-done | bytes 1048608 | tf_op jit(solution)/shard_map/all_to_all | solution.py:95
  90.8 15.2 %all_gather.7 = bf16[64,4096]{1,0:T(8,128)(2,1)S(1)} all-gather(bf16[16,4096]{1,0:T(8,128)(2,1)S(1)} %bitcast.93), channel_id=1, replica_groups=mesh['groups'=2,'seq'=4,'tp'=2,'rep'=2] {'seq'}, dimensions={0}, use_global_device_ids=true | all-gather | bytes 655360 | tf_op jit(solution)/shard_map/all_gather | solution.py:114
  106.0 9.6 %fusion.18 = f32[64,2048]{1,0:T(8,128)} fusion(bf16[64,4096]{1,0:T(8,128)(2,1)S(1)} %all_gather.7, bf16[4096,2048]{1,0:T(8,128)(2,1)} %param.15), kind=kOutput, calls=%fused_computation.42 | convolution fusion | flops 1073741824 | bytes 17825792 | tf_op jit(solution)/shard_map/dot_general | solution.py:113
  115.6 13.7 %reduce-scatter.2.cloned.1.call-done = f32[32,2048]{1,0:T(8,128)} async-done(((f32[64,2048]{1,0:T(8,128)}), f32[32,2048]{1,0:T(8,128)}) %reduce-scatter.2.cloned.1.call-update) | async-done | bytes 262160 | tf_op jit(solution)/shard_map/reduce_scatter | solution.py:118
  129.3 1.6 %convert_bitcast_fusion = bf16[1,32,2048]{2,1,0:T(8,128)(2,1)} fusion(f32[32,2048]{1,0:T(8,128)} %reduce-scatter.2.cloned.1.call-done), kind=kLoop, calls=%fused_computation.27 | loop fusion | flops 65536 | bytes 393216 | tf_op jit(solution)/shard_map/broadcast_in_dim | solution.py:119
  (70 shorter events, 7.2 us)
Async XLA Ops:
  6.5 8.8 %all-to-all-start = ((bf16[8,2,4096]{2,0,1:T(8,128)(2,1)}), bf16[8,2,4096]{2,0,1:T(8,128)(2,1)S(1)}, u32[]{:S(2)}, u32[]{:S(2)}) async-start(bf16[8,2,4096]{2,0,1:T(8,128)(2,1)} %bitcast.96), calls=%async_computation | async-start | bytes 262144 | tf_op jit(solution)/shard_map/all_to_all | solution.py:65
  15.3 19.8 %all-to-all-start.3 = ((bf16[8,2,512]{2,0,1:T(8,128)(2,1)}), bf16[8,2,512]{2,0,1:T(8,128)(2,1)S(1)}, u32[]{:S(2)}, u32[]{:S(2)}) async-start(bf16[8,2,512]{2,0,1:T(8,128)(2,1)} %bitcast.101), calls=%async_computation.3 | async-start | bytes 32768 | tf_op jit(solution)/shard_map/all_to_all | solution.py:66
  35.1 12.5 %all-to-all-start.4 = ((bf16[8,2,512]{2,0,1:T(8,128)(2,1)}), bf16[8,2,512]{2,0,1:T(8,128)(2,1)S(1)}, u32[]{:S(2)}, u32[]{:S(2)}) async-start(bf16[8,2,512]{2,0,1:T(8,128)(2,1)} %bitcast.102), calls=%async_computation.4 | async-start | bytes 32768 | tf_op jit(solution)/shard_map/all_to_all | solution.py:67
  47.6 11.0 %all-to-all-start.5 = ((f32[4,1,512]{2,1,0:T(1,128)}), f32[4,1,512]{2,1,0:T(1,128)S(1)}, u32[]{:S(2)}, u32[]{:S(2)}) async-start(f32[4,1,512]{2,1,0:T(1,128)} %reshape.121), calls=%async_computation.5 | async-start | bytes 16384 | tf_op jit(solution)/shard_map/all_to_all | solution.py:94
  66.5 23.5 %all-to-all-start.1 = ((f32[4,16,4,8,128]{4,3,1,2,0:T(8,128)}), f32[4,16,4,8,128]{4,3,1,2,0:T(8,128)S(1)}, u32[]{:S(2)}, u32[]{:S(2)}) async-start(f32[4,16,4,8,128]{4,3,1,2,0:T(8,128)} %get-tuple-element.94), calls=%async_computation.1 | async-start | bytes 2097152 | tf_op jit(solution)/shard_map/all_to_all | solution.py:95
  70.0 59.3 %reduce-scatter.2.cloned.1.call-start = ((), (), s32[]{:S(2)}) async-start(), calls=%async_computation.7 | async-start | bytes 786432 | tf_op jit(solution)/shard_map/reduce_scatter | solution.py:118
Sparse Core Ops, SparseCore 0:
  115.7 13.5 reduce-scatter.1
where the time goes:
time: 139 us; the launch traced here: 138 us
  blocking collectives  39.6 us (28%)
  waiting for transfers between devices  36.5 us (26%)
  starting transfers between devices  19.7 us (14%)
  matrix products  15.8 us (11%)
  between operations  13.6 us (10%)
  other arithmetic  6.86 us (5%)
  local copies, waits for them, and re-layouts  5.72 us (4%)
    all_to_all x1, waiting for transfers between devices, shards(): lax.all_to_all(part_acc, 'seq', split_axis=0, concat_axis=0, tiled=True)  17.1 us
    all_gather x1, blocking collectives, shards(): everyone = lax.all_gather(query_rows, 'seq', axis=0, tiled=True)  16.4 us
    all_gather x1, blocking collectives, shards(): lax.all_gather(context, 'seq', axis=0, tiled=True)  15.2 us
    reduce_scatter x1, waiting for transfers between devices, shards(): lax.psum_scatter(partial_out, 'tp', scatter_dimension=0, tiled=True)  13.7 us
    dot_general x1, matrix products, shards(): jnp.dot(lax.all_gather(context, 'seq', axis=0, tiled=True), out_weight, p...  9.6 us
    all_to_all x1, blocking collectives, shards(): lax.all_to_all(part_max, 'seq', split_axis=0, concat_axis=0, tiled=True)  7.92 us
    all_to_all x1, waiting for transfers between devices, shards(): lax.all_to_all(part_sum, 'seq', split_axis=0, concat_axis=0, tiled=True)  5.5 us
    all_to_all x1, starting transfers between devices, shards(): lax.all_to_all(part_sum, 'seq', split_axis=0, concat_axis=0, tiled=True)  5.39 us
  transfers between devices with their start and end apart: 6, of which 4 were waited for; matrix products, arithmetic and copies ran while one was open for 12% of the time, Pallas kernels for 0%

commit v1 on v0

--- a/solution.py
+++ b/solution.py
@@ -1,33 +1,38 @@
+import functools
 import math
 
 import jax
 import jax.numpy as jnp
 from jax import lax
+from jax.experimental import pallas as pl
+from jax.experimental.pallas import tpu as pltpu
 from jax.sharding import PartitionSpec as P
 
 HEAD_WIDTH = 128
+HIDDEN = -1e30
+SCALE = 1.0 / math.sqrt(HEAD_WIDTH)
 
 
 def block_partial(query_heads, lengths, key_rows, value_rows, offset):
     kv_heads = query_heads.shape[1]
     row_count = key_rows.shape[0]
     step_rows = math.gcd(row_count, 512)
-    logit_scale = 1.0 / math.sqrt(HEAD_WIDTH)
     stat_shape = query_heads.shape[:3]
 
     def masked_scores(turn_index):
         first_row = turn_index * step_rows
-        key_block = key_rows.reshape(step_rows, kv_heads, HEAD_WIDTH)
+        key_block = lax.dynamic_slice_in_dim(key_rows, first_row, step_rows, 0)
+        key_block = key_block.reshape(step_rows, kv_heads, HEAD_WIDTH)
         scores = (
             jnp.einsum("tkgd,pkd->tkgp", query_heads, key_block, preferred_element_type=jnp.float32)
-            * logit_scale
+            * SCALE
         )
         position = offset + first_row + jnp.arange(step_rows, dtype=jnp.int32)
         visible_mask = (position[None, :] < lengths[:, None])[:, None, None, :]
         return (scores, visible_mask, first_row)
 
     def peak_step(turn_index, peak_now):
-        scores, visible_mask, first_row = masked_scores(turn_index)
+        scores, visible_mask, _ = masked_scores(turn_index)
         return jnp.maximum(peak_now, jnp.max(jnp.where(visible_mask, scores, -jnp.inf), axis=-1))
 
     block_peak = lax.fori_loop(
@@ -38,7 +43,8 @@
     def weight_step(turn_index, state_now):
         sum_now, acc_now = state_now
         scores, visible_mask, first_row = masked_scores(turn_index)
-        value_block = value_rows.reshape(step_rows, kv_heads, HEAD_WIDTH)
+        value_block = lax.dynamic_slice_in_dim(value_rows, first_row, step_rows, 0)
+        value_block = value_block.reshape(step_rows, kv_heads, HEAD_WIDTH)
         weights = jnp.where(visible_mask, jnp.exp(scores - anchor[..., None]), 0.0)
         sum_now = sum_now + jnp.sum(weights, axis=-1)
         acc_now = acc_now + jnp.einsum(
@@ -58,7 +64,7 @@
     return (block_peak, block_sum, block_acc)
 
 
-def shards(
+def shards_any(
     queries, fresh_key_rows, fresh_value_rows, visible, prefix_keys, cached_value_rows, out_weight
 ):
     query_rows, self_key_rows, own_values = (
@@ -74,9 +80,12 @@
     query_heads = query_rows.reshape(tok_rows, kv_heads, per_group, HEAD_WIDTH)
     self_key_rows = self_key_rows.reshape(tok_rows, kv_heads, HEAD_WIDTH)
     own_vectors = own_values.reshape(tok_rows, kv_heads, 1, HEAD_WIDTH).astype(jnp.float32)
-    self_score_row = jnp.einsum(
-        "tkgd,tkd->tkg", query_heads, self_key_rows, preferred_element_type=jnp.float32
-    ) * (1.0 / math.sqrt(HEAD_WIDTH))
+    self_score_row = (
+        jnp.einsum(
+            "tkgd,tkd->tkg", query_heads, self_key_rows, preferred_element_type=jnp.float32
+        )
+        * SCALE
+    )
     seq_count = lax.axis_size("seq")
     everyone = lax.all_gather(query_rows, "seq", axis=0, tiled=True)
     blocks = everyone.reshape(seq_count, tok_rows, kv_heads, per_group, HEAD_WIDTH)
@@ -119,6 +128,253 @@
     return summed.astype(jnp.bfloat16)[None]
 
 
+def swap(array, axis, mask):
+    return lax.ppermute(array, axis, [(i, i ^ mask) for i in range(lax.axis_size(axis))])
+
+
+def lanes(array, index, width):
+    return lax.dynamic_slice_in_dim(array, index * width, width, 1)
+
+
+def stack_heads(rows, heads):
+    return jnp.concatenate(
+        [rows[:, h * HEAD_WIDTH : (h + 1) * HEAD_WIDTH] for h in range(heads)], axis=0
+    )
+
+
+def attend_step(query, lengths, offset, keys, values, peak, total, acc):
+    scores = (
+        lax.dot_general(query, keys, (((1,), (1,)), ((), ())), preferred_element_type=jnp.float32)
+        * SCALE
+    )
+    position = offset + lax.broadcasted_iota(jnp.int32, scores.shape, 1)
+    scores = jnp.where(position < lengths, scores, HIDDEN)
+    new_peak = jnp.maximum(peak, jnp.max(scores, axis=-1, keepdims=True))
+    weights = jnp.exp(scores - new_peak)
+    fade = jnp.exp(peak - new_peak)
+    total = total * fade + jnp.sum(weights, axis=-1, keepdims=True)
+    acc = acc * fade + jnp.dot(
+        weights.astype(jnp.bfloat16), values, preferred_element_type=jnp.float32
+    )
+    return new_peak, total, acc
+
+
+def attend_first(heads, where_ref, q_ref, len_ref, k_ref, v_ref, peak_ref, total_ref, acc_ref):
+    tokens = q_ref.shape[0]
+    q_width = heads * HEAD_WIDTH
+    offset = where_ref[0]
+    fresh_key = q_ref[:, q_width : q_width + HEAD_WIDTH].astype(jnp.float32)
+    fresh_value = q_ref[:, q_width + HEAD_WIDTH :].astype(jnp.float32)
+    lengths = len_ref[...]
+    for h in range(heads):
+        query = q_ref[:, h * HEAD_WIDTH : (h + 1) * HEAD_WIDTH]
+        own = jnp.sum(query.astype(jnp.float32) * fresh_key, axis=-1, keepdims=True) * SCALE
+        peak, total, acc = attend_step(
+            query,
+            lengths,
+            offset,
+            k_ref[...],
+            v_ref[...],
+            own,
+            jnp.ones_like(own),
+            fresh_value,
+        )
+        rows = slice(h * tokens, (h + 1) * tokens)
+        peak_ref[rows, :] = peak
+        total_ref[rows, :] = total
+        acc_ref[rows, :] = acc
+
+
+def attend_more(
+    heads, blocks, last, where_ref, q_ref, len_ref, peak_in, total_in, acc_in, *refs
+):
+    pieces, outs = refs[:blocks], refs[blocks:]
+    tokens = q_ref.shape[0]
+    lengths = len_ref[...]
+    for h in range(heads):
+        query = q_ref[:, h * HEAD_WIDTH : (h + 1) * HEAD_WIDTH]
+        rows = slice(h * tokens, (h + 1) * tokens)
+        state = (peak_in[rows, :], total_in[rows, :], acc_in[rows, :])
+        for b in range(blocks):
+            half = pieces[b].shape[0] // 2
+            state = attend_step(
+                query,
+                lengths,
+                where_ref[b],
+                pieces[b][:half, :],
+                pieces[b][half:, :],
+                *state,
+            )
+        peak, total, acc = state
+        if last:
+            outs[0][:, h * HEAD_WIDTH : (h + 1) * HEAD_WIDTH] = (acc / total).astype(jnp.bfloat16)
+        else:
+            for ref, value in zip(outs, state):
+                ref[rows, :] = value
+
+
+def in_vmem():
+    return pl.BlockSpec(memory_space=pltpu.VMEM)
+
+
+def in_smem():
+    return pl.BlockSpec(memory_space=pltpu.SMEM)
+
+
+def cost(flops, bytes_accessed, transcendentals=0):
+    return pl.CostEstimate(
+        flops=flops, bytes_accessed=bytes_accessed, transcendentals=transcendentals
+    )
+
+
+def state_shapes(rows):
+    return (
+        jax.ShapeDtypeStruct((rows, 1), jnp.float32),
+        jax.ShapeDtypeStruct((rows, 1), jnp.float32),
+        jax.ShapeDtypeStruct((rows, HEAD_WIDTH), jnp.float32),
+    )
+
+
+def first_call(heads, where, query, lengths, keys, values):
+    rows = query.shape[0] * heads
+    return pl.pallas_call(
+        functools.partial(attend_first, heads),
+        out_shape=state_shapes(rows),
+        in_specs=[in_smem()] + [in_vmem()] * 4,
+        out_specs=(in_vmem(),) * 3,
+        compiler_params=pltpu.CompilerParams(vmem_limit_bytes=24 * 2**20),
+        cost_estimate=cost(
+            4 * rows * keys.shape[0] * HEAD_WIDTH, 2**20, rows * keys.shape[0]
+        ),
+        name="attend_first",
+    )(where, query, lengths, keys, values)
+
+
+def more_call(heads, last, where, query, lengths, state, pieces):
+    tokens = query.shape[0]
+    rows = tokens * heads
+    positions = sum(p.shape[0] // 2 for p in pieces)
+    shapes = (
+        jax.ShapeDtypeStruct((tokens, heads * HEAD_WIDTH), jnp.bfloat16)
+        if last
+        else state_shapes(rows)
+    )
+    return pl.pallas_call(
+        functools.partial(attend_more, heads, len(pieces), last),
+        out_shape=shapes,
+        in_specs=[in_smem()] + [in_vmem()] * (5 + len(pieces)),
+        out_specs=in_vmem() if last else (in_vmem(),) * 3,
+        compiler_params=pltpu.CompilerParams(vmem_limit_bytes=24 * 2**20),
+        cost_estimate=cost(4 * rows * positions * HEAD_WIDTH, 2**20, rows * positions),
+        name="attend_last" if last else "attend_more",
+    )(where, query, lengths, *state, *pieces)
+
+
+def project_kernel(row_ref, x_ref, w_ref, *refs):
+    part = jnp.dot(x_ref[...], w_ref[...], preferred_element_type=jnp.float32)
+    if len(refs) == 2:
+        part = part + refs[0][...]
+    refs[-1][...] = part
+
+
+def project(row_block, context, weight, acc):
+    tokens, depth = context.shape
+    columns = weight.shape[1]
+    step = math.gcd(columns, 512)
+    specs = [
+        pl.BlockSpec((tokens, depth), lambda n, row: (0, 0)),
+        pl.BlockSpec((depth, step), lambda n, row: (row[0], n)),
+    ]
+    operands = [context, weight]
+    if acc is not None:
+        specs.append(pl.BlockSpec((tokens, step), lambda n, row: (0, n)))
+        operands.append(acc)
+    return pl.pallas_call(
+        project_kernel,
+        out_shape=jax.ShapeDtypeStruct((tokens, columns), jnp.float32),
+        grid_spec=pltpu.PrefetchScalarGridSpec(
+            num_scalar_prefetch=1,
+            grid=(columns // step,),
+            in_specs=specs,
+            out_specs=pl.BlockSpec((tokens, step), lambda n, row: (0, n)),
+        ),
+        compiler_params=pltpu.CompilerParams(vmem_limit_bytes=24 * 2**20),
+        cost_estimate=cost(2 * tokens * depth * columns, 2 * depth * columns),
+        name="project",
+    )(row_block, *operands)
+
+
+def shards_by_head(
+    queries, fresh_key_rows, fresh_value_rows, visible, prefix_keys, cached_value_rows, out_weight
+):
+    seq_count = lax.axis_size("seq")
+    seq, tp, rep = lax.axis_index("seq"), lax.axis_index("tp"), lax.axis_index("rep")
+    block_rows = prefix_keys.shape[0]
+    half_rows = block_rows // 2
+    heads = queries.shape[2] // (fresh_key_rows.shape[2])
+    masks = list(range(1, seq_count))
+
+    key_half = lax.dynamic_slice_in_dim(prefix_keys, rep * half_rows, half_rows, 0)
+    value_half = lax.dynamic_slice_in_dim(cached_value_rows, rep * half_rows, half_rows, 0)
+    halves = []
+    for mask in masks:
+        piece = jnp.concatenate(
+            [lanes(key_half, seq ^ mask, HEAD_WIDTH), lanes(value_half, seq ^ mask, HEAD_WIDTH)]
+        )
+        halves.append(swap(piece, "seq", mask))
+
+    rows = [queries[0], fresh_key_rows[0], fresh_value_rows[0]]
+    away = jnp.concatenate([lanes(a, 1 - tp, a.shape[1] // 2) for a in rows], axis=1)
+    home = jnp.concatenate([lanes(a, tp, a.shape[1] // 2) for a in rows], axis=1)
+    arrived = swap(away, "tp", 1)
+    both = jnp.concatenate([jnp.where(tp == 0, home, arrived), jnp.where(tp == 0, arrived, home)])
+    widths = [a.shape[1] // 2 for a in rows]
+    starts = [0, widths[0], widths[0] + widths[1]]
+
+    def for_head(index):
+        parts = [both[:, s : s + w] for s, w in zip(starts, widths)]
+        return jnp.concatenate([lanes(p, index, p.shape[1] // seq_count) for p in parts], axis=1)
+
+    blocks = [for_head(seq)] + [swap(for_head(seq ^ m), "seq", m) for m in masks]
+    stacked = jnp.stack(blocks)
+    query = jnp.concatenate([lax.dynamic_index_in_dim(stacked, seq ^ b, 0, False) for b in range(seq_count)])
+    lengths = visible[0][:, None]
+
+    other = [swap(h, "rep", 1) for h in halves]
+
+    def place(mask, core):
+        return (seq ^ mask) * block_rows + core * half_rows
+
+    state = first_call(
+        heads,
+        (seq * block_rows)[None],
+        query,
+        lengths,
+        lanes(prefix_keys, seq, HEAD_WIDTH),
+        lanes(cached_value_rows, seq, HEAD_WIDTH),
+    )
+    for i, mask in enumerate(masks):
+        state = more_call(
+            heads,
+            i == len(masks) - 1,
+            jnp.stack([place(mask, rep), place(mask, 1 - rep)]),
+            query,
+            lengths,
+            state,
+            [halves[i], other[i]],
+        )
+    context = state
+    gathered = [context] + [swap(context, "seq", m) for m in masks]
+    acc = None
+    for mask, chunk in zip([0] + masks, gathered):
+        acc = project((seq ^ mask)[None], chunk, out_weight, acc)
+    keep_rows = acc.shape[0] // 2
+    keep = lax.dynamic_slice_in_dim(acc, tp * keep_rows, keep_rows, 0)
+    send = lax.dynamic_slice_in_dim(acc, (1 - tp) * keep_rows, keep_rows, 0)
+    got = swap(send.astype(jnp.bfloat16), "tp", 1)
+    return (keep + got.astype(jnp.float32)).astype(jnp.bfloat16)[None]
+
+
 def solution(mesh):
     in_specs = (
         P("rep", ("groups", "seq", "tp"), None),
@@ -130,4 +386,17 @@
         P("tp", "seq"),
     )
     out_specs = P("rep", ("groups", "tp"), "seq")
+    sizes = mesh.shape
+    seq_count = sizes["seq"]
+
+    def shards(*args):
+        local_heads = args[4].shape[1] // HEAD_WIDTH
+        by_head = (
+            local_heads == seq_count
+            and seq_count & (seq_count - 1) == 0
+            and sizes["tp"] == 2
+            and sizes["rep"] == 2
+        )
+        return (shards_by_head if by_head else shards_any)(*args)
+
     return jax.shard_map(shards, mesh=mesh, in_specs=in_specs, out_specs=out_specs, check_vma=False)

time: 139 us -> 71.6 us (0.52)
  blocking collectives: 39.6 us -> 0 us
  Pallas kernels: 0 us -> 25.8 us
  waiting for transfers between devices: 36.5 us -> 10.7 us
  matrix products: 15.8 us -> 0 us
  between operations: 13.6 us -> 0.24 us
  local copies, waits for them, and re-layouts: 5.72 us -> 15.5 us
  other arithmetic: 6.86 us -> 1.07 us
  starting transfers between devices: 19.7 us -> 18 us
    all_gather x2 -> x0, blocking collectives: 31.7 us -> none  [the longest x1 16.4 us: shards(): everyone = lax.all_gather(query_rows, 'seq', axis=0, tiled=True)]
    pallas_call x0 -> x8, Pallas kernels: none -> 25.8 us  [the longest x3 16.9 us: more_call(): pl.pallas_call(functools.partial(attend_more, heads, len(pieces), last),...]
    all_to_all x5 -> x0, waiting for transfers between devices: 22.8 us -> none  [the longest x1 17.1 us: shards(): lax.all_to_all(part_acc, 'seq', split_axis=0, concat_axis=0, tiled=True)]
    all_to_all x5 -> x0, starting transfers between devices: 19.6 us -> none  [the longest x1 5.39 us: shards(): lax.all_to_all(part_sum, 'seq', split_axis=0, concat_axis=0, tiled=True)]
    ppermute x0 -> x14, starting transfers between devices: none -> 18 us  [swap(): lax.ppermute(array, axis, [(i, i ^ mask) for i in range(lax.axis_size(axi...]
    dot_general x10 -> x0, matrix products: 15.8 us -> none  [the longest x1 9.6 us: shards(): jnp.dot(lax.all_gather(context, 'seq', axis=0, tiled=True), out_weight, p...]
    reduce_scatter x1 -> x0, waiting for transfers between devices: 13.7 us -> none  [shards(): lax.psum_scatter(partial_out, 'tp', scatter_dimension=0, tiled=True)]
    ppermute x0 -> x14, waiting for transfers between devices: none -> 10.7 us  [swap(): lax.ppermute(array, axis, [(i, i ^ mask) for i in range(lax.axis_size(axi...]
  transfers between devices with their start and end apart: 6 -> 14, of which waited for: 4 -> 4; matrix products, arithmetic and copies ran while one was open for 12% -> 5% of each run, Pallas kernels for 0% -> 26%
where the time goes in v1:
time: 71.6 us; the launch traced here: 71.2 us
  Pallas kernels  25.8 us (36%)
  starting transfers between devices  18 us (25%)
  local copies, waits for them, and re-layouts  15.5 us (22%)
  waiting for transfers between devices  10.7 us (15%)
  other arithmetic  1.07 us (1%)
    ppermute x14, starting transfers between devices, swap(): lax.ppermute(array, axis, [(i, i ^ mask) for i in range(lax.axis_size(axi...  18 us
    pallas_call x3, Pallas kernels, more_call(): pl.pallas_call(functools.partial(attend_more, heads, len(pieces), last),...  16.9 us
    ppermute x14, waiting for transfers between devices, swap(): lax.ppermute(array, axis, [(i, i ^ mask) for i in range(lax.axis_size(axi...  10.7 us
    unnamed x4, local copies, waits for them, and re-layouts  9.89 us
    pallas_call x4, Pallas kernels, project(): pl.pallas_call(project_kernel, out_shape=jax.ShapeDtypeStruct((tokens, co...  6.67 us
    dynamic_slice x6, local copies, waits for them, and re-layouts, lanes(): return lax.dynamic_slice_in_dim(array, index * width, width, 1)  4.79 us
    pallas_call x1, Pallas kernels, first_call(): pl.pallas_call(functools.partial(attend_first, heads), out_shape=state_sh...  2.18 us
  transfers between devices with their start and end apart: 14, of which 4 were waited for; matrix products, arithmetic and copies ran while one was open for 5% of the time, Pallas kernels for 26%

profile of v1, /device:TPU:0, one launch (start us, length us, event | category | flops | bytes accessed | tf_op | source)
XLA Modules:
  0.0 71.2 jit_solution(5961779349675071810)
XLA Ops:
  1.4 0.9 %dynamic-slice_bitcast_fusion.1 = (bf16[8,4096]{1,0:T(8,128)(2,1)S(1)}, bf16[8,4096]{1,0:T(8,128)(2,1)S(1)}) fusion(bf16[1,8,8192]{2,1,0:T(8,128)(2,1)} %param.7, s32[]{:T(128)S(6)} %select_n.94, s32[]{:T(128)S(6)} %select_n.96), kind=kLoop, calls=%fused_computation.18 | loop fusion | bytes 262152 | tf_op jit(solution)/shard_map/dynamic_slice | solution.py:136
  2.3 3.0 %collective-permute-start = (bf16[8,5120]{1,0:T(8,128)(2,1)S(1)}, bf16[8,5120]{1,0:T(8,128)(2,1)S(1)}, u32[]{:S(2)}, u32[]{:S(2)}) collective-permute-start(bf16[8,5120]{1,0:T(8,128)(2,1)S(1)} %pad_maximum_fusion.6), channel_id=1, source_target_pairs={{0,2},{2,0},{1,3},{3,1},{4,6},{6,4},{5,7},{7,5},{8,10},{10,8},{9,1... | collective-permute-start | bytes 245768 | tf_op jit(solution)/shard_map/ppermute | solution.py:132
  5.3 1.5 %fusion.7 = (bf16[256,128]{1,0:T(8,128)(2,1)S(1)}, bf16[256,128]{1,0:T(8,128)(2,1)S(1)}, bf16[256,128]{1,0:T(8,128)(2,1)S(1)}, bf16[256,128]{1,0:T(8,128)(2,1)S(...) fusion(bf16[512,512]{1,0:T(8,128)(2,1)} %param.11, s32[]{:T(128)S(6)} %select_n.113, s32[]{:T(128)S(6)} %select_n.116, ...), kind=kLoop, calls=%fused_computation.57 | loop fusion | bytes 786448 | tf_op jit(solution)/shard_map/dynamic_slice | solution.py:136
  6.8 1.6 %collective-permute-start.4 = (bf16[512,128]{1,0:T(8,128)(2,1)S(1)}, bf16[512,128]{1,0:T(8,128)(2,1)S(1)}, u32[]{:S(2)}, u32[]{:S(2)}) collective-permute-start(bf16[512,128]{1,0:T(8,128)(2,1)S(1)} %pad_maximum_fusion.2), channel_id=1, source_target_pairs={{0,4},{4,0},{8,12},{12,8},{1,5},{5,1},{9,13},{13,9},{2,6},{6,2},{1... | collective-permute-start | bytes 393224 | tf_op jit(solution)/shard_map/ppermute | solution.py:132
  8.5 2.7 %collective-permute-start.6 = (bf16[512,128]{1,0:T(8,128)(2,1)S(1)}, bf16[512,128]{1,0:T(8,128)(2,1)S(1)}, u32[]{:S(2)}, u32[]{:S(2)}) collective-permute-start(bf16[512,128]{1,0:T(8,128)(2,1)S(1)} %pad_maximum_fusion.3), channel_id=1, source_target_pairs={{0,8},{4,12},{8,0},{12,4},{1,9},{5,13},{9,1},{13,5},{2,10},{6,14},... | collective-permute-start | bytes 393224 | tf_op jit(solution)/shard_map/ppermute | solution.py:132
  11.2 1.0 %constant_dynamic-slice_fusion.4 = (bf16[512,128]{1,0:T(8,128)(2,1)S(1)}, bf16[512,128]{1,0:T(8,128)(2,1)S(1)}) fusion(bf16[512,512]{1,0:T(8,128)(2,1)} %param.12, s32[]{:T(128)S(6)} %select_n.101, bf16[512,512]{1,0:T(8,128)(2,1)} %param.11), kind=kLoop, calls=%fused_computation.36 | loop fusion | bytes 524292 | tf_op jit(solution)/shard_map/dynamic_slice | solution.py:136
  14.1 3.6 %collective-permute-start.3 = (bf16[16,1280]{1,0:T(8,128)(2,1)S(1)}, bf16[16,1280]{1,0:T(8,128)(2,1)S(1)}, u32[]{:S(2)}, u32[]{:S(2)}) collective-permute-start(bf16[16,1280]{1,0:T(8,128)(2,1)S(1)} %pad_maximum_fusion.9), channel_id=1, source_target_pairs={{0,12},{4,8},{8,4},{12,0},{1,13},{5,9},{9,5},{13,1},{2,14},{6,10},... | collective-permute-start | bytes 122888 | tf_op jit(solution)/shard_map/ppermute | solution.py:132
  18.2 1.2 %collective-permute-done.2 = bf16[16,1280]{1,0:T(8,128)(2,1)S(1)} collective-permute-done((bf16[16,1280]{1,0:T(8,128)(2,1)S(1)}, bf16[16,1280]{1,0:T(8,128)(2,1)S(1)}, u32[]{:S(2)}, u32[]{:S(2)}) %collective-permute-start.2) | collective-permute-done | bytes 40992 | tf_op jit(solution)/shard_map/ppermute | solution.py:132
  19.4 0.9 %collective-permute-done.3 = bf16[16,1280]{1,0:T(8,128)(2,1)S(1)} collective-permute-done((bf16[16,1280]{1,0:T(8,128)(2,1)S(1)}, bf16[16,1280]{1,0:T(8,128)(2,1)S(1)}, u32[]{:S(2)}, u32[]{:S(2)}) %collective-permute-start.3) | collective-permute-done | bytes 40992 | tf_op jit(solution)/shard_map/ppermute | solution.py:132
  20.9 3.8 %collective-permute-done.8.refs_0_ = bf16[512,128]{1,0:T(8,128)(2,1)S(1)} collective-permute-done((bf16[512,128]{1,0:T(8,128)(2,1)S(1)}, bf16[512,128]{1,0:T(8,128)(2,1)S(1)}, u32[]{:S(2)}, u32[]{:S(2)}) %collective-permute-start.8) | collective-permute-done | bytes 131104 | tf_op jit(solution)/shard_map/ppermute | solution.py:132
  24.7 2.2 %attend_first.1 = (f32[512,1]{1,0:T(8,128)S(1)}, f32[512,1]{1,0:T(8,128)S(1)}, f32[512,128]{1,0:T(8,128)S(1)}) custom-call(s32[1]{0:T(128)} %bitcast.22.where_ref, bf16[64,1280]{1,0:T(8,128)(2,1)S(1)} %pad_maximum_fusion.1.q_ref, s32[64,1]{1,0:T(8,128)S(1)} %copy.11.len_ref, bf16[512,128]{1,0:T(8,128)(2,1)S(1)} %get-tuple-element.61.k_ref, ...), custom_call_target="tpu_custom_call" | custom-call | flops 134217728 | bytes 1048576 | tf_op jit(solution)/shard_map/attend_first/pallas_call | solution.py:240
  26.9 5.6 %attend_more.2 = (f32[512,1]{1,0:T(8,128)S(1)}, f32[512,1]{1,0:T(8,128)S(1)}, f32[512,128]{1,0:T(8,128)S(1)}) custom-call(s32[2]{0:T(128)S(1)} %pad_add_fusion.2.where_ref, bf16[64,1280]{1,0:T(8,128)(2,1)S(1)} %pad_maximum_fusion.1.q_ref, s32[64,1]{1,0:T(8,128)S(1)} %copy.11.len_ref, f32[512,1]{1,0:T(8,128)S(1)} %get-tuple-element.14.peak_in, ...), custom_call_target="tpu_custom_call" | custom-call | flops 134217728 | bytes 1048576 | tf_op jit(solution)/shard_map/attend_more/pallas_call | solution.py:262
  32.5 5.6 %attend_more.3 = (f32[512,1]{1,0:T(8,128)S(1)}, f32[512,1]{1,0:T(8,128)S(1)}, f32[512,128]{1,0:T(8,128)S(1)}) custom-call(s32[2]{0:T(128)S(1)} %pad_add_fusion.1.where_ref, bf16[64,1280]{1,0:T(8,128)(2,1)S(1)} %pad_maximum_fusion.1.q_ref, s32[64,1]{1,0:T(8,128)S(1)} %copy.11.len_ref, f32[512,1]{1,0:T(8,128)S(1)} %get-tuple-element.17.peak_in, ...), custom_call_target="tpu_custom_call" | custom-call | flops 134217728 | bytes 1048576 | tf_op jit(solution)/shard_map/attend_more/pallas_call | solution.py:262
  38.2 5.7 %attend_last.1.x_ref = bf16[64,1024]{1,0:T(8,128)(2,1)S(1)} custom-call(s32[2]{0:T(128)S(1)} %pad_add_fusion.where_ref, bf16[64,1280]{1,0:T(8,128)(2,1)S(1)} %pad_maximum_fusion.1.q_ref, s32[64,1]{1,0:T(8,128)S(1)} %copy.11.len_ref, f32[512,1]{1,0:T(8,128)S(1)} %get-tuple-element.20.peak_in, f32[512,1]{1,0:T(8,128)S(1)} %get-tuple-element.21.total_in, ...), custom_call_target="tpu_custom_call" | custom-call | flops 134217728 | bytes 1048576 | tf_op jit(solution)/shard_map/attend_last/pallas_call | solution.py:262
  43.9 2.1 %collective-permute-start.12 = (bf16[64,1024]{1,0:T(8,128)(2,1)S(1)}, bf16[64,1024]{1,0:T(8,128)(2,1)S(1)}, u32[]{:S(2)}, u32[]{:S(2)}) collective-permute-start(bf16[64,1024]{1,0:T(8,128)(2,1)S(1)} %attend_last.1.x_ref), channel_id=1, source_target_pairs={{0,4},{4,0},{8,12},{12,8},{1,5},{5,1},{9,13},{13,9},{2,6},{6,2},{1... | collective-permute-start | bytes 393224 | tf_op jit(solution)/shard_map/ppermute | solution.py:132
  46.0 1.0 %collective-permute-start.11 = (bf16[64,1024]{1,0:T(8,128)(2,1)S(1)}, bf16[64,1024]{1,0:T(8,128)(2,1)S(1)}, u32[]{:S(2)}, u32[]{:S(2)}) collective-permute-start(bf16[64,1024]{1,0:T(8,128)(2,1)S(1)} %attend_last.1.x_ref), channel_id=1, source_target_pairs={{0,8},{4,12},{8,0},{12,4},{1,9},{5,13},{9,1},{13,5},{2,10},{6,14},... | collective-permute-start | bytes 393224 | tf_op jit(solution)/shard_map/ppermute | solution.py:132
  47.0 1.5 %collective-permute-start.10 = (bf16[64,1024]{1,0:T(8,128)(2,1)S(1)}, bf16[64,1024]{1,0:T(8,128)(2,1)S(1)}, u32[]{:S(2)}, u32[]{:S(2)}) collective-permute-start(bf16[64,1024]{1,0:T(8,128)(2,1)S(1)} %attend_last.1.x_ref), channel_id=1, source_target_pairs={{0,12},{4,8},{8,4},{12,0},{1,13},{5,9},{9,5},{13,1},{2,14},{6,10},... | collective-permute-start | bytes 393224 | tf_op jit(solution)/shard_map/ppermute | solution.py:132
  48.4 5.8 %copy-done = bf16[4096,2048]{1,0:T(8,128)(2,1)S(1)} copy-done((bf16[4096,2048]{1,0:T(8,128)(2,1)S(1)}, bf16[4096,2048]{1,0:T(8,128)(2,1)}, u32[]{:S(2)}) %copy-start) | copy-done | bytes 16777240
  54.2 1.6 %project.4.refs_0_ = f32[64,2048]{1,0:T(8,128)S(1)} custom-call(s32[1]{0:T(128)} %bitcast.25.row_ref, bf16[64,1024]{1,0:T(8,128)(2,1)S(1)} %attend_last.1.x_ref, bf16[4096,2048]{1,0:T(8,128)(2,1)S(1)} %copy-done), custom_call_target="tpu_custom_call" | custom-call | flops 268435456 | bytes 4194304 | tf_op jit(solution)/shard_map/project/pallas_call | solution.py:292
  55.9 4.1 %copy-done.1 = bf16[4096,2048]{1,0:T(8,128)(2,1)S(1)} copy-done((bf16[4096,2048]{1,0:T(8,128)(2,1)S(1)}, bf16[4096,2048]{1,0:T(8,128)(2,1)}, u32[]{:S(2)}) %copy-start.1) | copy-done | bytes 16777240
  60.0 1.7 %project.5.refs_0_ = f32[64,2048]{1,0:T(8,128)S(1)} custom-call(s32[1]{0:T(128)} %bitcast.24.row_ref, bf16[64,1024]{1,0:T(8,128)(2,1)S(1)} %collective-permute-done.12.x_ref, bf16[4096,2048]{1,0:T(8,128)(2,1)S(1)} %copy-done.1, f32[64,2048]{1,0:T(8,128)S(1)} %project.4.refs_0_), custom_call_target="tpu_custom_call" | custom-call | flops 268435456 | bytes 4194304 | tf_op jit(solution)/shard_map/project/pallas_call | solution.py:292
  61.7 1.7 %project.6.refs_0_ = f32[64,2048]{1,0:T(8,128)S(1)} custom-call(s32[1]{0:T(128)} %bitcast.23.row_ref, bf16[64,1024]{1,0:T(8,128)(2,1)S(1)} %collective-permute-done.11.x_ref, bf16[4096,2048]{1,0:T(8,128)(2,1)S(1)} %copy-done.1, f32[64,2048]{1,0:T(8,128)S(1)} %project.5.refs_0_), custom_call_target="tpu_custom_call" | custom-call | flops 268435456 | bytes 4194304 | tf_op jit(solution)/shard_map/project/pallas_call | solution.py:292
  63.4 1.7 %project.7 = f32[64,2048]{1,0:T(8,128)S(1)} custom-call(s32[1]{0:T(128)} %bitcast.row_ref, bf16[64,1024]{1,0:T(8,128)(2,1)S(1)} %collective-permute-done.10.x_ref, bf16[4096,2048]{1,0:T(8,128)(2,1)S(1)} %copy-done.1, f32[64,2048]{1,0:T(8,128)S(1)} %project.6.refs_0_), custom_call_target="tpu_custom_call" | custom-call | flops 268435456 | bytes 4194304 | tf_op jit(solution)/shard_map/project/pallas_call | solution.py:292
  65.7 4.8 %collective-permute-done.13 = bf16[32,2048]{1,0:T(8,128)(2,1)S(1)} collective-permute-done((bf16[32,2048]{1,0:T(8,128)(2,1)S(1)}, bf16[32,2048]{1,0:T(8,128)(2,1)S(1)}, u32[]{:S(2)}, u32[]{:S(2)}) %collective-permute-start.13) | collective-permute-done | bytes 131104 | tf_op jit(solution)/shard_map/ppermute | solution.py:132
  (45 shorter events, 5.8 us)
Async XLA Ops:
  2.3 10.8 %collective-permute-start = (bf16[8,5120]{1,0:T(8,128)(2,1)S(1)}, bf16[8,5120]{1,0:T(8,128)(2,1)S(1)}, u32[]{:S(2)}, u32[]{:S(2)}) collective-permute-start(bf16[8,5120]{1,0:T(8,128)(2,1)S(1)} %pad_maximum_fusion.6), channel_id=1, source_target_pairs={{0,2},{2,0},{1,3},{3,1},{4,6},{6,4},{5,7},{7,5},{8,10},{10,8},{9,1... | collective-permute-start | bytes 245768 | tf_op jit(solution)/shard_map/ppermute | solution.py:132
  6.8 13.5 %collective-permute-start.4 = (bf16[512,128]{1,0:T(8,128)(2,1)S(1)}, bf16[512,128]{1,0:T(8,128)(2,1)S(1)}, u32[]{:S(2)}, u32[]{:S(2)}) collective-permute-start(bf16[512,128]{1,0:T(8,128)(2,1)S(1)} %pad_maximum_fusion.2), channel_id=1, source_target_pairs={{0,4},{4,0},{8,12},{12,8},{1,5},{5,1},{9,13},{13,9},{2,6},{6,2},{1... | collective-permute-start | bytes 393224 | tf_op jit(solution)/shard_map/ppermute | solution.py:132
  8.5 12.0 %collective-permute-start.6 = (bf16[512,128]{1,0:T(8,128)(2,1)S(1)}, bf16[512,128]{1,0:T(8,128)(2,1)S(1)}, u32[]{:S(2)}, u32[]{:S(2)}) collective-permute-start(bf16[512,128]{1,0:T(8,128)(2,1)S(1)} %pad_maximum_fusion.3), channel_id=1, source_target_pairs={{0,8},{4,12},{8,0},{12,4},{1,9},{5,13},{9,1},{13,5},{2,10},{6,14},... | collective-permute-start | bytes 393224 | tf_op jit(solution)/shard_map/ppermute | solution.py:132
  13.3 4.5 %collective-permute-start.1 = (bf16[16,1280]{1,0:T(8,128)(2,1)S(1)}, bf16[16,1280]{1,0:T(8,128)(2,1)S(1)}, u32[]{:S(2)}, u32[]{:S(2)}) collective-permute-start(bf16[16,1280]{1,0:T(8,128)(2,1)S(1)} %pad_maximum_fusion.7), channel_id=1, source_target_pairs={{0,4},{4,0},{8,12},{12,8},{1,5},{5,1},{9,13},{13,9},{2,6},{6,2},{1... | collective-permute-start | bytes 122888 | tf_op jit(solution)/shard_map/ppermute | solution.py:132
  13.8 5.6 %collective-permute-start.2 = (bf16[16,1280]{1,0:T(8,128)(2,1)S(1)}, bf16[16,1280]{1,0:T(8,128)(2,1)S(1)}, u32[]{:S(2)}, u32[]{:S(2)}) collective-permute-start(bf16[16,1280]{1,0:T(8,128)(2,1)S(1)} %pad_maximum_fusion.8), channel_id=1, source_target_pairs={{0,8},{4,12},{8,0},{12,4},{1,9},{5,13},{9,1},{13,5},{2,10},{6,14},... | collective-permute-start | bytes 122888 | tf_op jit(solution)/shard_map/ppermute | solution.py:132
  14.1 6.2 %collective-permute-start.3 = (bf16[16,1280]{1,0:T(8,128)(2,1)S(1)}, bf16[16,1280]{1,0:T(8,128)(2,1)S(1)}, u32[]{:S(2)}, u32[]{:S(2)}) collective-permute-start(bf16[16,1280]{1,0:T(8,128)(2,1)S(1)} %pad_maximum_fusion.9), channel_id=1, source_target_pairs={{0,12},{4,8},{8,4},{12,0},{1,13},{5,9},{9,5},{13,1},{2,14},{6,10},... | collective-permute-start | bytes 122888 | tf_op jit(solution)/shard_map/ppermute | solution.py:132
  17.8 6.9 %collective-permute-start.8 = (bf16[512,128]{1,0:T(8,128)(2,1)S(1)}, bf16[512,128]{1,0:T(8,128)(2,1)S(1)}, u32[]{:S(2)}, u32[]{:S(2)}) collective-permute-start(bf16[512,128]{1,0:T(8,128)(2,1)S(1)} %pad_maximum_fusion.4), channel_id=1, source_target_pairs={{0,12},{4,8},{8,4},{12,0},{1,13},{5,9},{9,5},{13,1},{2,14},{6,10},... | collective-permute-start | bytes 393224 | tf_op jit(solution)/shard_map/ppermute | solution.py:132
  20.4 6.6 %collective-permute-start.5 = (bf16[512,128]{1,0:T(8,128)(2,1)S(1)}, bf16[512,128]{1,0:T(8,128)(2,1)S(1)}, u32[]{:S(2)}, u32[]{:S(2)}) collective-permute-start(bf16[512,128]{1,0:T(8,128)(2,1)S(1)} %collective-permute-done.4.refs_0_), channel_id=1, source_target_pairs={{0,1},{1,0},{2,3},{3,2},{4,5},{5,4},{6,7},{7,6},{8,9},{9,8},{10,11... | collective-permute-start | bytes 393224 | tf_op jit(solution)/shard_map/ppermute | solution.py:132
  20.4 12.1 %collective-permute-start.7 = (bf16[512,128]{1,0:T(8,128)(2,1)S(1)}, bf16[512,128]{1,0:T(8,128)(2,1)S(1)}, u32[]{:S(2)}, u32[]{:S(2)}) collective-permute-start(bf16[512,128]{1,0:T(8,128)(2,1)S(1)} %collective-permute-done.6.refs_0_), channel_id=1, source_target_pairs={{0,1},{1,0},{2,3},{3,2},{4,5},{5,4},{6,7},{7,6},{8,9},{9,8},{10,11... | collective-permute-start | bytes 393224 | tf_op jit(solution)/shard_map/ppermute | solution.py:132
  24.7 13.4 %collective-permute-start.9 = (bf16[512,128]{1,0:T(8,128)(2,1)S(1)}, bf16[512,128]{1,0:T(8,128)(2,1)S(1)}, u32[]{:S(2)}, u32[]{:S(2)}) collective-permute-start(bf16[512,128]{1,0:T(8,128)(2,1)S(1)} %collective-permute-done.8.refs_0_), channel_id=1, source_target_pairs={{0,1},{1,0},{2,3},{3,2},{4,5},{5,4},{6,7},{7,6},{8,9},{9,8},{10,11... | collective-permute-start | bytes 393224 | tf_op jit(solution)/shard_map/ppermute | solution.py:132
  43.9 12.0 %collective-permute-start.12 = (bf16[64,1024]{1,0:T(8,128)(2,1)S(1)}, bf16[64,1024]{1,0:T(8,128)(2,1)S(1)}, u32[]{:S(2)}, u32[]{:S(2)}) collective-permute-start(bf16[64,1024]{1,0:T(8,128)(2,1)S(1)} %attend_last.1.x_ref), channel_id=1, source_target_pairs={{0,4},{4,0},{8,12},{12,8},{1,5},{5,1},{9,13},{13,9},{2,6},{6,2},{1... | collective-permute-start | bytes 393224 | tf_op jit(solution)/shard_map/ppermute | solution.py:132
  46.0 15.7 %collective-permute-start.11 = (bf16[64,1024]{1,0:T(8,128)(2,1)S(1)}, bf16[64,1024]{1,0:T(8,128)(2,1)S(1)}, u32[]{:S(2)}, u32[]{:S(2)}) collective-permute-start(bf16[64,1024]{1,0:T(8,128)(2,1)S(1)} %attend_last.1.x_ref), channel_id=1, source_target_pairs={{0,8},{4,12},{8,0},{12,4},{1,9},{5,13},{9,1},{13,5},{2,10},{6,14},... | collective-permute-start | bytes 393224 | tf_op jit(solution)/shard_map/ppermute | solution.py:132
  47.0 16.4 %collective-permute-start.10 = (bf16[64,1024]{1,0:T(8,128)(2,1)S(1)}, bf16[64,1024]{1,0:T(8,128)(2,1)S(1)}, u32[]{:S(2)}, u32[]{:S(2)}) collective-permute-start(bf16[64,1024]{1,0:T(8,128)(2,1)S(1)} %attend_last.1.x_ref), channel_id=1, source_target_pairs={{0,12},{4,8},{8,4},{12,0},{1,13},{5,9},{9,5},{13,1},{2,14},{6,10},... | collective-permute-start | bytes 393224 | tf_op jit(solution)/shard_map/ppermute | solution.py:132
  48.4 5.8 %copy-start = (bf16[4096,2048]{1,0:T(8,128)(2,1)S(1)}, bf16[4096,2048]{1,0:T(8,128)(2,1)}, u32[]{:S(2)}) copy-start(bf16[4096,2048]{1,0:T(8,128)(2,1)} %w_ref.7) | copy-start | bytes 50331652
  54.2 5.8 %copy-start.1 = (bf16[4096,2048]{1,0:T(8,128)(2,1)S(1)}, bf16[4096,2048]{1,0:T(8,128)(2,1)}, u32[]{:S(2)}) copy-start(bf16[4096,2048]{1,0:T(8,128)(2,1)} %w_ref.7) | copy-start | bytes 50331652
  65.1 5.4 %collective-permute-start.13 = (bf16[32,2048]{1,0:T(8,128)(2,1)S(1)}, bf16[32,2048]{1,0:T(8,128)(2,1)S(1)}, u32[]{:S(2)}, u32[]{:S(2)}) collective-permute-start(bf16[32,2048]{1,0:T(8,128)(2,1)S(1)} %dynamic-slice_convert_fusion), channel_id=1, source_target_pairs={{0,2},{2,0},{1,3},{3,1},{4,6},{6,4},{5,7},{7,5},{8,10},{10,8},{9,1... | collective-permute-start | bytes 393224 | tf_op jit(solution)/shard_map/ppermute | solution.py:132

commit v2 on v0

--- a/solution.py
+++ b/solution.py
@@ -1,33 +1,38 @@
+import functools
 import math
 
 import jax
 import jax.numpy as jnp
 from jax import lax
+from jax.experimental import pallas as pl
+from jax.experimental.pallas import tpu as pltpu
 from jax.sharding import PartitionSpec as P
 
 HEAD_WIDTH = 128
+HIDDEN = -1e30
+SCALE = 1.0 / math.sqrt(HEAD_WIDTH)
 
 
 def block_partial(query_heads, lengths, key_rows, value_rows, offset):
     kv_heads = query_heads.shape[1]
     row_count = key_rows.shape[0]
     step_rows = math.gcd(row_count, 512)
-    logit_scale = 1.0 / math.sqrt(HEAD_WIDTH)
     stat_shape = query_heads.shape[:3]
 
     def masked_scores(turn_index):
         first_row = turn_index * step_rows
-        key_block = key_rows.reshape(step_rows, kv_heads, HEAD_WIDTH)
+        key_block = lax.dynamic_slice_in_dim(key_rows, first_row, step_rows, 0)
+        key_block = key_block.reshape(step_rows, kv_heads, HEAD_WIDTH)
         scores = (
             jnp.einsum("tkgd,pkd->tkgp", query_heads, key_block, preferred_element_type=jnp.float32)
-            * logit_scale
+            * SCALE
         )
         position = offset + first_row + jnp.arange(step_rows, dtype=jnp.int32)
         visible_mask = (position[None, :] < lengths[:, None])[:, None, None, :]
         return (scores, visible_mask, first_row)
 
     def peak_step(turn_index, peak_now):
-        scores, visible_mask, first_row = masked_scores(turn_index)
+        scores, visible_mask, _ = masked_scores(turn_index)
         return jnp.maximum(peak_now, jnp.max(jnp.where(visible_mask, scores, -jnp.inf), axis=-1))
 
     block_peak = lax.fori_loop(
@@ -38,7 +43,8 @@
     def weight_step(turn_index, state_now):
         sum_now, acc_now = state_now
         scores, visible_mask, first_row = masked_scores(turn_index)
-        value_block = value_rows.reshape(step_rows, kv_heads, HEAD_WIDTH)
+        value_block = lax.dynamic_slice_in_dim(value_rows, first_row, step_rows, 0)
+        value_block = value_block.reshape(step_rows, kv_heads, HEAD_WIDTH)
         weights = jnp.where(visible_mask, jnp.exp(scores - anchor[..., None]), 0.0)
         sum_now = sum_now + jnp.sum(weights, axis=-1)
         acc_now = acc_now + jnp.einsum(
@@ -58,7 +64,7 @@
     return (block_peak, block_sum, block_acc)
 
 
-def shards(
+def shards_any(
     queries, fresh_key_rows, fresh_value_rows, visible, prefix_keys, cached_value_rows, out_weight
 ):
     query_rows, self_key_rows, own_values = (
@@ -74,9 +80,12 @@
     query_heads = query_rows.reshape(tok_rows, kv_heads, per_group, HEAD_WIDTH)
     self_key_rows = self_key_rows.reshape(tok_rows, kv_heads, HEAD_WIDTH)
     own_vectors = own_values.reshape(tok_rows, kv_heads, 1, HEAD_WIDTH).astype(jnp.float32)
-    self_score_row = jnp.einsum(
-        "tkgd,tkd->tkg", query_heads, self_key_rows, preferred_element_type=jnp.float32
-    ) * (1.0 / math.sqrt(HEAD_WIDTH))
+    self_score_row = (
+        jnp.einsum(
+            "tkgd,tkd->tkg", query_heads, self_key_rows, preferred_element_type=jnp.float32
+        )
+        * SCALE
+    )
     seq_count = lax.axis_size("seq")
     everyone = lax.all_gather(query_rows, "seq", axis=0, tiled=True)
     blocks = everyone.reshape(seq_count, tok_rows, kv_heads, per_group, HEAD_WIDTH)
@@ -119,6 +128,369 @@
     return summed.astype(jnp.bfloat16)[None]
 
 
+EXPONENT = SCALE * math.log2(math.e)
+VMEM_BYTES = 20 * 2**20
+SETTLE = 10**11
+ORDER = -1
+PACK_BYTES = int(63.5 * 2**20)
+PROJECT_BYTES = 16 * 2**20
+LOAD_BYTES = 30 * 2**20
+
+
+def swap(array, axis, mask):
+    return lax.ppermute(array, axis, [(i, i ^ mask) for i in range(lax.axis_size(axis))])
+
+
+def tile_at(index, width):
+    return pl.ds(pl.multiple_of(index * width, width), width)
+
+
+def side_by_side(array, times):
+    return jnp.concatenate([array] * times, axis=1)
+
+
+def vmem():
+    return pl.BlockSpec(memory_space=pltpu.VMEM)
+
+
+def hbm():
+    return pl.BlockSpec(memory_space=pltpu.HBM)
+
+
+def params(limit=VMEM_BYTES):
+    return pltpu.CompilerParams(vmem_limit_bytes=limit)
+
+
+def cost(flops, bytes_accessed, transcendentals=0):
+    return pl.CostEstimate(
+        flops=flops, bytes_accessed=bytes_accessed, transcendentals=transcendentals
+    )
+
+
+def pack_prefix_kernel(masks, k_ref, v_ref, own_ref, *piece_refs):
+    seq, rep = lax.axis_index("seq"), lax.axis_index("rep")
+    rows = k_ref.shape[0]
+    half = rows // 2
+    for j, table in enumerate((k_ref, v_ref)):
+        for mask, piece in zip(masks, piece_refs):
+            piece[j * half : (j + 1) * half, :] = table[
+                tile_at(rep, half), tile_at(seq ^ mask, HEAD_WIDTH)
+            ]
+    for j, table in enumerate((k_ref, v_ref)):
+        own_ref[j * rows : (j + 1) * rows, :] = table[:, tile_at(seq, HEAD_WIDTH)]
+
+
+def pack_prefix(prefix_keys, cached_value_rows, masks):
+    rows = prefix_keys.shape[0]
+    heights = [2 * rows] + [rows] * len(masks)
+    return pl.pallas_call(
+        functools.partial(pack_prefix_kernel, masks),
+        out_shape=[jax.ShapeDtypeStruct((n, HEAD_WIDTH), jnp.bfloat16) for n in heights],
+        in_specs=[vmem()] * 2,
+        out_specs=[vmem()] * len(heights),
+        compiler_params=params(),
+        cost_estimate=cost(0, 2 * 2**20),
+        name="pack_prefix",
+    )(prefix_keys, cached_value_rows)
+
+
+def pack_queries_kernel(seq_count, q_ref, fk_ref, fv_ref, out_ref):
+    tokens = q_ref.shape[0]
+    count = out_ref.shape[0] // tokens
+    for owner in range(count):
+        head = owner % 2 * seq_count + owner // 2
+        to = 0
+        for ref in (q_ref, fk_ref, fv_ref):
+            part = ref.shape[1] // count
+            out_ref[owner * tokens : (owner + 1) * tokens, to : to + part] = ref[
+                :, head * part : (head + 1) * part
+            ]
+            to += part
+
+
+def pack_queries(rows, seq_count):
+    count = 2 * seq_count
+    shape = (rows[0].shape[0] * count, sum(a.shape[1] for a in rows) // count)
+    return pl.pallas_call(
+        functools.partial(pack_queries_kernel, seq_count),
+        out_shape=jax.ShapeDtypeStruct(shape, jnp.bfloat16),
+        in_specs=[vmem()] * 3,
+        out_specs=vmem(),
+        compiler_params=params(),
+        cost_estimate=cost(0, 2**19),
+        name="pack_queries",
+    )(*rows)
+
+
+def settle_kernel(*refs):
+    del refs
+
+
+def settle(arrays):
+    count = len(arrays)
+    return pl.pallas_call(
+        settle_kernel,
+        out_shape=[jax.ShapeDtypeStruct(a.shape, a.dtype) for a in arrays],
+        in_specs=[vmem()] * count,
+        out_specs=[vmem()] * count,
+        input_output_aliases={i: i for i in range(count)},
+        compiler_params=params(2**20),
+        cost_estimate=cost(SETTLE, 2**20),
+        name="settle",
+    )(*arrays)
+
+
+def lengths_kernel(visible_ref, out_ref):
+    tokens = out_ref.shape[0]
+    diagonal = lax.broadcasted_iota(jnp.int32, (tokens, tokens), 0) == lax.broadcasted_iota(
+        jnp.int32, (tokens, tokens), 1
+    )
+    lengths = jnp.sum(jnp.where(diagonal, visible_ref[...], 0), axis=-1, keepdims=True)
+    out_ref[...] = jnp.broadcast_to(lengths, out_ref.shape)
+
+
+def spread_lengths(visible):
+    return pl.pallas_call(
+        lengths_kernel,
+        out_shape=jax.ShapeDtypeStruct((visible.shape[1], HEAD_WIDTH), jnp.int32),
+        in_specs=[vmem()],
+        out_specs=vmem(),
+        compiler_params=params(),
+        cost_estimate=cost(0, 2**15),
+        name="spread_lengths",
+    )(visible)
+
+
+def attend_step(query, lengths, position, keys, values, peak, acc):
+    count = keys.shape[0]
+    scores = lax.dot_general(
+        query, keys, (((1,), (1,)), ((), ())), preferred_element_type=jnp.float32
+    )
+    scores = jnp.where(position < side_by_side(lengths, count // HEAD_WIDTH), scores, HIDDEN)
+    new_peak = jnp.maximum(peak, jnp.max(scores, axis=-1, keepdims=True))
+    weights = jnp.exp2((scores - side_by_side(new_peak, count // HEAD_WIDTH)) * EXPONENT)
+    fade = jnp.exp2((peak - new_peak) * EXPONENT)
+    with_ones = jnp.concatenate([values, jnp.ones_like(values)], axis=1)
+    acc = acc * side_by_side(fade, 2) + jnp.dot(
+        weights.astype(jnp.bfloat16), with_ones, preferred_element_type=jnp.float32
+    )
+    return new_peak, acc
+
+
+def join(refs, first, count):
+    return jnp.concatenate([ref[first : first + count, :] for ref in refs], axis=0)
+
+
+def attend_first_kernel(
+    heads, block_rows, rows_ref, lengths_ref, own_ref, stacked_ref, peak_ref, acc_ref
+):
+    seq = lax.axis_index("seq")
+    tokens = rows_ref.shape[0]
+    lengths = lengths_ref[...]
+    width = heads * HEAD_WIDTH
+    fresh_key = rows_ref[:, width : width + HEAD_WIDTH].astype(jnp.float32)
+    fresh_value = rows_ref[:, width + HEAD_WIDTH :].astype(jnp.float32)
+    start = jnp.concatenate([fresh_value, jnp.ones_like(fresh_value)], axis=1)
+    keys, values = own_ref[:block_rows, :], own_ref[block_rows:, :]
+    position = seq * block_rows + lax.broadcasted_iota(jnp.int32, (1, block_rows), 1)
+    for h in range(0, heads, 2):
+        rows = slice(h * tokens, (h + 2) * tokens)
+        query = jnp.concatenate(
+            [rows_ref[:, i * HEAD_WIDTH : (i + 1) * HEAD_WIDTH] for i in (h, h + 1)], axis=0
+        )
+        own = jnp.sum(
+            query.astype(jnp.float32) * jnp.concatenate([fresh_key] * 2, axis=0),
+            axis=-1,
+            keepdims=True,
+        )
+        stacked_ref[rows, :] = query
+        peak, acc = attend_step(
+            query,
+            jnp.concatenate([lengths] * 2, axis=0),
+            position,
+            keys,
+            values,
+            jnp.broadcast_to(own, (2 * tokens, HEAD_WIDTH)),
+            jnp.concatenate([start] * 2, axis=0),
+        )
+        peak_ref[rows, :] = peak
+        acc_ref[rows, :] = acc
+
+
+def attend_first(heads, query_rows, lengths, own):
+    rows = heads * query_rows.shape[0]
+    block_rows = own.shape[0] // 2
+    return pl.pallas_call(
+        functools.partial(attend_first_kernel, heads, block_rows),
+        out_shape=(
+            jax.ShapeDtypeStruct((rows, HEAD_WIDTH), jnp.bfloat16),
+            jax.ShapeDtypeStruct((rows, HEAD_WIDTH), jnp.float32),
+            jax.ShapeDtypeStruct((rows, 2 * HEAD_WIDTH), jnp.float32),
+        ),
+        in_specs=[vmem()] * 3,
+        out_specs=(vmem(),) * 3,
+        compiler_params=params(),
+        cost_estimate=cost(6 * rows * block_rows * HEAD_WIDTH, 2**20, rows * block_rows),
+        name="attend_first",
+    )(query_rows, lengths, own)
+
+
+def attend_more_kernel(
+    block_rows, mask, last, query_ref, lengths_ref, peak_in, acc_in, mine_ref, other_ref, *outs
+):
+    seq, rep = lax.axis_index("seq"), lax.axis_index("rep")
+    half = block_rows // 2
+    tokens = lengths_ref.shape[0]
+    lengths = jnp.concatenate([lengths_ref[...]] * 2, axis=0)
+    base = (seq ^ mask) * 2 * half
+    keys = join((mine_ref, other_ref), 0, half)
+    values = join((mine_ref, other_ref), half, half)
+    lane = lax.broadcasted_iota(jnp.int32, (1, 2 * half), 1)
+    position = base + jnp.where(rep == 0, lane, jnp.where(lane < half, lane + half, lane - half))
+    for first in range(0, query_ref.shape[0], 2 * tokens):
+        rows = slice(first, first + 2 * tokens)
+        state = peak_in[rows, :], acc_in[rows, :]
+        state = attend_step(
+            query_ref[rows, :], lengths, position, keys, values, *state
+        )
+        if last:
+            context = state[1][:, :HEAD_WIDTH] / state[1][:, HEAD_WIDTH:]
+            for i in range(2):
+                column = (first // tokens + i) * HEAD_WIDTH
+                outs[0][:, column : column + HEAD_WIDTH] = context[
+                    i * tokens : (i + 1) * tokens, :
+                ].astype(jnp.bfloat16)
+        else:
+            outs[0][rows, :], outs[1][rows, :] = state
+
+
+def attend_more(positions, mask, last, stacked, lengths, state, mine, other):
+    rows, tokens = stacked.shape[0], lengths.shape[0]
+    shapes = (
+        (jax.ShapeDtypeStruct((tokens, rows // tokens * HEAD_WIDTH), jnp.bfloat16),)
+        if last
+        else tuple(jax.ShapeDtypeStruct(a.shape, a.dtype) for a in state)
+    )
+    return pl.pallas_call(
+        functools.partial(attend_more_kernel, positions, mask, last),
+        out_shape=shapes,
+        in_specs=[vmem()] * 6,
+        out_specs=(vmem(),) * len(shapes),
+        compiler_params=params(),
+        cost_estimate=cost(6 * rows * positions * HEAD_WIDTH, 2**20, rows * positions),
+        name="attend_last" if last else "attend_more",
+    )(stacked, lengths, *state, mine, other)
+
+
+def load_kernel(masks, weight_ref, *refs):
+    tile_refs, sems = refs[:-1], refs[-1]
+    seq = lax.axis_index("seq")
+    depth = tile_refs[0].shape[0]
+    steps = sems.shape[0] // len(tile_refs)
+    rows = depth // steps
+    copies = [
+        pltpu.make_async_copy(
+            weight_ref.at[pl.ds(pl.multiple_of((seq ^ mask) * depth + n * rows, rows), rows), :],
+            tile_ref.at[pl.ds(n * rows, rows), :],
+            sems.at[i * steps + n],
+        )
+        for i, (mask, tile_ref) in enumerate(zip([0] + masks, tile_refs))
+        for n in range(steps)
+    ]
+    for copy in copies:
+        copy.start()
+    for copy in copies:
+        copy.wait()
+
+
+def load(weight, masks):
+    count = 1 + len(masks)
+    shape = jax.ShapeDtypeStruct((weight.shape[0] // count, weight.shape[1]), weight.dtype)
+    return pl.pallas_call(
+        functools.partial(load_kernel, masks),
+        out_shape=[shape] * count,
+        in_specs=[hbm()],
+        out_specs=[vmem()] * count,
+        scratch_shapes=[pltpu.SemaphoreType.DMA((4 * count,))],
+        compiler_params=params(LOAD_BYTES),
+        cost_estimate=cost(0, weight.size * 2),
+        name="load",
+    )(weight)
+
+
+def project_kernel(first, last, *refs):
+    x_ref, w_ref = refs[:2]
+    acc_ref = None if first else refs[2]
+    outs = refs[2 if first else 3 :]
+    tp = lax.axis_index("tp")
+    columns = w_ref.shape[1]
+    width = math.gcd(columns, 512)
+    keep_rows = x_ref.shape[0] // 2
+    for start in range(0, columns, width):
+        at = slice(start, start + width)
+        part = jnp.dot(x_ref[...], w_ref[:, at], preferred_element_type=jnp.float32)
+        if not first:
+            part = part + acc_ref[:, at]
+        if last:
+            low, high = part[:keep_rows, :], part[keep_rows:, :]
+            outs[0][:, at] = jnp.where(tp == 0, low, high)
+            outs[1][:, at] = jnp.where(tp == 0, high, low).astype(jnp.bfloat16)
+        else:
+            outs[0][:, at] = part
+
+
+def project(context, tile, acc, last):
+    tokens, depth = context.shape
+    columns = tile.shape[1]
+    if last:
+        shapes = [
+            jax.ShapeDtypeStruct((tokens // 2, columns), jnp.float32),
+            jax.ShapeDtypeStruct((tokens // 2, columns), jnp.bfloat16),
+        ]
+    else:
+        shapes = [jax.ShapeDtypeStruct((tokens, columns), jnp.float32)]
+    operands = [context, tile] + ([] if acc is None else [acc])
+    return pl.pallas_call(
+        functools.partial(project_kernel, acc is None, last),
+        out_shape=shapes,
+        in_specs=[vmem()] * len(operands),
+        out_specs=[vmem()] * len(shapes),
+        compiler_params=params(PROJECT_BYTES),
+        cost_estimate=cost(2 * tokens * depth * columns, 2 * depth * columns),
+        name="project",
+    )(*operands)
+
+
+def shards_by_head(
+    queries, fresh_key_rows, fresh_value_rows, visible, prefix_keys, cached_value_rows, out_weight
+):
+    heads = queries.shape[2] // fresh_key_rows.shape[2]
+    masks = list(range(1, lax.axis_size("seq")))[::ORDER]
+    rows = [queries[0], fresh_key_rows[0], fresh_value_rows[0]]
+    own, *pieces = pack_prefix(prefix_keys, cached_value_rows, masks)
+    mine = [swap(piece, "seq", mask) for piece, mask in zip(pieces, masks)]
+    query_rows = lax.all_to_all(
+        pack_queries(rows, 1 + len(masks)), ("seq", "tp"), split_axis=0, concat_axis=0, tiled=True
+    )
+    lengths = spread_lengths(visible)
+    mine = settle(mine)
+    other = [swap(piece, "rep", 1) for piece in mine]
+
+    stacked, *state = attend_first(heads, query_rows, lengths, own)
+    for i, mask in enumerate(masks):
+        state = attend_more(
+            prefix_keys.shape[0], mask, mask == masks[-1], stacked, lengths, state, mine[i], other[i]
+        )
+    context = state[0]
+    tiles = load(out_weight, masks)
+    acc, send = None, None
+    for mask, tile in zip([0] + masks, tiles):
+        chunk = swap(context, "seq", mask) if mask else context
+        acc, *send = project(chunk, tile, acc, mask == masks[-1])
+    got = swap(send[0], "tp", 1)
+    return (acc + got.astype(jnp.float32)).astype(jnp.bfloat16)[None]
+
+
 def solution(mesh):
     in_specs = (
         P("rep", ("groups", "seq", "tp"), None),
@@ -130,4 +502,18 @@
         P("tp", "seq"),
     )
     out_specs = P("rep", ("groups", "tp"), "seq")
+    sizes = mesh.shape
+    seq_count = sizes["seq"]
+
+    def shards(*args):
+        local_heads = args[4].shape[1] // HEAD_WIDTH
+        by_head = (
+            local_heads == seq_count
+            and seq_count & (seq_count - 1) == 0
+            and sizes["tp"] == 2
+            and sizes["rep"] == 2
+            and args[0].shape[2] // args[1].shape[2] % 2 == 0
+        )
+        return (shards_by_head if by_head else shards_any)(*args)
+
     return jax.shard_map(shards, mesh=mesh, in_specs=in_specs, out_specs=out_specs, check_vma=False)

time: 139 us -> 47.2 us (0.34)
  blocking collectives: 39.6 us -> 0 us
  waiting for transfers between devices: 36.5 us -> 11.7 us
  matrix products: 15.8 us -> 0 us
  between operations: 13.6 us -> 0.15 us
  Pallas kernels: 0 us -> 12.9 us
  other arithmetic: 6.86 us -> 0.69 us
  starting transfers between devices: 19.7 us -> 16.9 us
    all_gather x2 -> x0, blocking collectives: 31.7 us -> none  [the longest x1 16.4 us: shards(): everyone = lax.all_gather(query_rows, 'seq', axis=0, tiled=True)]
    all_to_all x5 -> x1, waiting for transfers between devices: 22.8 us -> 5.41 us  [shards_by_head(): lax.all_to_all(pack_queries(rows, 1 + len(masks)), ('seq', 'tp'), split_a...]
    dot_general x10 -> x0, matrix products: 15.8 us -> none  [the longest x1 9.6 us: shards(): jnp.dot(lax.all_gather(context, 'seq', axis=0, tiled=True), out_weight, p...]
    reduce_scatter x1 -> x0, waiting for transfers between devices: 13.7 us -> none  [shards(): lax.psum_scatter(partial_out, 'tp', scatter_dimension=0, tiled=True)]
    all_to_all x5 -> x1, starting transfers between devices: 19.6 us -> 5.95 us  [shards_by_head(): lax.all_to_all(pack_queries(rows, 1 + len(masks)), ('seq', 'tp'), split_a...]
    pallas_call x0 -> x13, Pallas kernels: none -> 12.9 us  [the longest x1 5.93 us: load(): pl.pallas_call(functools.partial(load_kernel, masks), out_shape=[shape] *...]
    ppermute x0 -> x10, starting transfers between devices: none -> 11 us  [swap(): lax.ppermute(array, axis, [(i, i ^ mask) for i in range(lax.axis_size(axi...]
    all_to_all x1 -> x0, blocking collectives: 7.92 us -> none  [shards(): lax.all_to_all(part_max, 'seq', split_axis=0, concat_axis=0, tiled=True)]
  transfers between devices with their start and end apart: 6 -> 11, of which waited for: 4 -> 3; matrix products, arithmetic and copies ran while one was open for 12% -> 0% of each run, Pallas kernels for 0% -> 24%
where the time goes in v2:
time: 47.2 us; the launch traced here: 46.8 us
  starting transfers between devices  16.9 us (36%)
  Pallas kernels  12.9 us (27%)
  waiting for transfers between devices  11.7 us (25%)
  local copies, waits for them, and re-layouts  4.42 us (9%)
  other arithmetic  0.69 us (1%)
    ppermute x10, starting transfers between devices, swap(): lax.ppermute(array, axis, [(i, i ^ mask) for i in range(lax.axis_size(axi...  11 us
    ppermute x10, waiting for transfers between devices, swap(): lax.ppermute(array, axis, [(i, i ^ mask) for i in range(lax.axis_size(axi...  6.31 us
    all_to_all x1, starting transfers between devices, shards_by_head(): lax.all_to_all(pack_queries(rows, 1 + len(masks)), ('seq', 'tp'), split_a...  5.95 us
    pallas_call x1, Pallas kernels, load(): pl.pallas_call(functools.partial(load_kernel, masks), out_shape=[shape] *...  5.93 us
    all_to_all x1, waiting for transfers between devices, shards_by_head(): lax.all_to_all(pack_queries(rows, 1 + len(masks)), ('seq', 'tp'), split_a...  5.41 us
    unnamed x12, local copies, waits for them, and re-layouts  4.42 us
    pallas_call x4, Pallas kernels, project(): pl.pallas_call(functools.partial(project_kernel, acc is None, last), out_...  3.39 us
    pallas_call x3, Pallas kernels, attend_more(): pl.pallas_call(functools.partial(attend_more_kernel, positions, mask, las...  2.04 us
  transfers between devices with their start and end apart: 11, of which 3 were waited for; matrix products, arithmetic and copies ran while one was open for 0% of the time, Pallas kernels for 24%

profile of v2, /device:TPU:0, one launch (start us, length us, event | category | flops | bytes accessed | tf_op | source)
XLA Modules:
  0.0 46.8 jit_solution(17561740278128412839)
XLA Ops:
  0.0 1.0 %copy-done = bf16[512,512]{1,0:T(8,128)(2,1)S(1)} copy-done((bf16[512,512]{1,0:T(8,128)(2,1)S(1)}, bf16[512,512]{1,0:T(8,128)(2,1)}, u32[]{:S(2)}) %copy-start) | copy-done | bytes 524312
  1.0 1.0 %copy-done.1 = bf16[512,512]{1,0:T(8,128)(2,1)S(1)} copy-done((bf16[512,512]{1,0:T(8,128)(2,1)S(1)}, bf16[512,512]{1,0:T(8,128)(2,1)}, u32[]{:S(2)}) %copy-start.1) | copy-done | bytes 524312
  2.2 5.1 %collective-permute-start = (bf16[512,128]{1,0:T(8,128)(2,1)S(1)}, bf16[512,128]{1,0:T(8,128)(2,1)S(1)}, u32[]{:S(2)}, u32[]{:S(2)}) collective-permute-start(bf16[512,128]{1,0:T(8,128)(2,1)S(1)} %get-tuple-element.29), channel_id=1, source_target_pairs={{0,12},{4,8},{8,4},{12,0},{1,13},{5,9},{9,5},{13,1},{2,14},{6,10},... | collective-permute-start | bytes 393224 | tf_op jit(solution)/shard_map/ppermute | solution.py:141
  7.3 0.6 %collective-permute-start.2 = (bf16[512,128]{1,0:T(8,128)(2,1)S(1)}, bf16[512,128]{1,0:T(8,128)(2,1)S(1)}, u32[]{:S(2)}, u32[]{:S(2)}) collective-permute-start(bf16[512,128]{1,0:T(8,128)(2,1)S(1)} %get-tuple-element.31), channel_id=1, source_target_pairs={{0,4},{4,0},{8,12},{12,8},{1,5},{5,1},{9,13},{13,9},{2,6},{6,2},{1... | collective-permute-start | bytes 393224 | tf_op jit(solution)/shard_map/ppermute | solution.py:141
  8.0 0.9 %copy-done.2 = bf16[1,8,8192]{2,1,0:T(8,128)(2,1)S(1)} copy-done((bf16[1,8,8192]{2,1,0:T(8,128)(2,1)S(1)}, bf16[1,8,8192]{2,1,0:T(8,128)(2,1)}, u32[]{:S(2)}) %copy-start.2) | copy-done | bytes 131096
  8.9 0.7 %copy-done.3 = bf16[1,8,1024]{2,1,0:T(8,128)(2,1)S(1)} copy-done((bf16[1,8,1024]{2,1,0:T(8,128)(2,1)S(1)}, bf16[1,8,1024]{2,1,0:T(8,128)(2,1)}, u32[]{:S(2)}) %copy-start.3) | copy-done | bytes 16408
  9.6 0.7 %copy-done.4 = bf16[1,8,1024]{2,1,0:T(8,128)(2,1)S(1)} copy-done((bf16[1,8,1024]{2,1,0:T(8,128)(2,1)S(1)}, bf16[1,8,1024]{2,1,0:T(8,128)(2,1)}, u32[]{:S(2)}) %copy-start.4) | copy-done | bytes 16408
  10.3 0.7 %pack_queries.1 = bf16[64,1280]{1,0:T(8,128)(2,1)} custom-call(bf16[8,8192]{1,0:T(8,128)(2,1)S(1)} %bitcast.8, bf16[8,1024]{1,0:T(8,128)(2,1)S(1)} %bitcast.9, bf16[8,1024]{1,0:T(8,128)(2,1)S(1)} %bitcast.10), custom_call_target="tpu_custom_call" | custom-call | bytes 524288 | tf_op jit(solution)/shard_map/pack_queries/pallas_call | solution.py:214
  11.0 5.9 %all-to-all-start = ((bf16[8,8,1280]{2,1,0:T(8,128)(2,1)}), bf16[8,8,1280]{2,1,0:T(8,128)(2,1)S(1)}, u32[]{:S(2)}, u32[]{:S(2)}) async-start(bf16[8,8,1280]{2,1,0:T(8,128)(2,1)} %bitcast.3), calls=%async_computation | async-start | bytes 327680 | tf_op jit(solution)/shard_map/all_to_all | solution.py:472
  16.9 1.4 %collective-permute-done.1.refs_1_ = bf16[512,128]{1,0:T(8,128)(2,1)S(1)} collective-permute-done((bf16[512,128]{1,0:T(8,128)(2,1)S(1)}, bf16[512,128]{1,0:T(8,128)(2,1)S(1)}, u32[]{:S(2)}, u32[]{:S(2)}) %collective-permute-start.1) | collective-permute-done | bytes 131104 | tf_op jit(solution)/shard_map/ppermute | solution.py:141
  19.1 5.4 %all-to-all-done = bf16[8,8,1280]{2,1,0:T(8,128)(2,1)S(1)} async-done(((bf16[8,8,1280]{2,1,0:T(8,128)(2,1)}), bf16[8,8,1280]{2,1,0:T(8,128)(2,1)S(1)}, u32[]{:S(2)}, u32[]{:S(2)}) %all-to-all-start) | async-done | bytes 163872 | tf_op jit(solution)/shard_map/all_to_all | solution.py:472
  24.5 0.7 %attend_first.1 = (bf16[512,128]{1,0:T(8,128)(2,1)S(1)}, f32[512,128]{1,0:T(8,128)S(1)}, f32[512,256]{1,0:T(8,128)S(1)}) custom-call(bf16[64,1280]{1,0:T(8,128)(2,1)S(1)} %bitcast.7, s32[64,128]{1,0:T(8,128)S(1)} %spread_lengths.1.lengths_ref, bf16[1024,128]{1,0:T(8,128)(2,1)S(1)} %get-tuple-element.25.own_ref), custom_call_target="tpu_custom_call" | custom-call | flops 201326592 | bytes 1048576 | tf_op jit(solution)/shard_map/attend_first/pallas_call | solution.py:323
  25.2 0.7 %attend_more.2 = (f32[512,128]{1,0:T(8,128)S(1)}, f32[512,256]{1,0:T(8,128)S(1)}) custom-call(bf16[512,128]{1,0:T(8,128)(2,1)S(1)} %get-tuple-element.26.query_ref, s32[64,128]{1,0:T(8,128)S(1)} %spread_lengths.1.lengths_ref, f32[512,128]{1,0:T(8,128)S(1)} %get-tuple-element.27.peak_in, f32[512,256]{1,0:T(8,128)S(1)} %get-tuple-element.28.acc_in, ...), custom_call_target="tpu_custom_call" | custom-call | flops 201326592 | bytes 1048576 | tf_op jit(solution)/shard_map/attend_more/pallas_call | solution.py:374
  25.9 0.7 %attend_more.3 = (f32[512,128]{1,0:T(8,128)S(1)}, f32[512,256]{1,0:T(8,128)S(1)}) custom-call(bf16[512,128]{1,0:T(8,128)(2,1)S(1)} %get-tuple-element.26.query_ref, s32[64,128]{1,0:T(8,128)S(1)} %spread_lengths.1.lengths_ref, f32[512,128]{1,0:T(8,128)S(1)} %get-tuple-element.33.peak_in, f32[512,256]{1,0:T(8,128)S(1)} %get-tuple-element.34.acc_in, ...), custom_call_target="tpu_custom_call" | custom-call | flops 201326592 | bytes 1048576 | tf_op jit(solution)/shard_map/attend_more/pallas_call | solution.py:374
  26.6 0.7 %attend_last.1.refs_0_ = bf16[64,1024]{1,0:T(8,128)(2,1)S(1)} custom-call(bf16[512,128]{1,0:T(8,128)(2,1)S(1)} %get-tuple-element.26.query_ref, s32[64,128]{1,0:T(8,128)S(1)} %spread_lengths.1.lengths_ref, f32[512,128]{1,0:T(8,128)S(1)} %get-tuple-element.36.peak_in, f32[512,256]{1,0:T(8,128)S(1)} %get-tuple-element.37.acc_in, ...), custom_call_target="tpu_custom_call" | custom-call | flops 201326592 | bytes 1048576 | tf_op jit(solution)/shard_map/attend_last/pallas_call | solution.py:374
  27.9 0.8 %collective-permute-start.7 = (bf16[64,1024]{1,0:T(8,128)(2,1)S(1)}, bf16[64,1024]{1,0:T(8,128)(2,1)S(1)}, u32[]{:S(2)}, u32[]{:S(2)}) collective-permute-start(bf16[64,1024]{1,0:T(8,128)(2,1)S(1)} %attend_last.1.refs_0_), channel_id=1, source_target_pairs={{0,8},{4,12},{8,0},{12,4},{1,9},{5,13},{9,1},{13,5},{2,10},{6,14},... | collective-permute-start | bytes 393224 | tf_op jit(solution)/shard_map/ppermute | solution.py:141
  28.7 3.0 %collective-permute-start.6 = (bf16[64,1024]{1,0:T(8,128)(2,1)S(1)}, bf16[64,1024]{1,0:T(8,128)(2,1)S(1)}, u32[]{:S(2)}, u32[]{:S(2)}) collective-permute-start(bf16[64,1024]{1,0:T(8,128)(2,1)S(1)} %attend_last.1.refs_0_), channel_id=1, source_target_pairs={{0,4},{4,0},{8,12},{12,8},{1,5},{5,1},{9,13},{13,9},{2,6},{6,2},{1... | collective-permute-start | bytes 393224 | tf_op jit(solution)/shard_map/ppermute | solution.py:141
  31.7 5.9 %load.1 = (bf16[1024,2048]{1,0:T(8,128)(2,1)S(1)}, bf16[1024,2048]{1,0:T(8,128)(2,1)S(1)}, bf16[1024,2048]{1,0:T(8,128)(2,1)S(1)}, bf16[1024,2048]{1,0:T(8,128)(2,1)S(1)}) custom-call(bf16[4096,2048]{1,0:T(8,128)(2,1)} %weight_ref.1), custom_call_target="tpu_custom_call" | custom-call | bytes 16777216 | tf_op jit(solution)/shard_map/load/pallas_call | solution.py:409
  37.6 0.8 %project.4.refs_2_ = f32[64,2048]{1,0:T(8,128)S(1)} custom-call(bf16[64,1024]{1,0:T(8,128)(2,1)S(1)} %attend_last.1.refs_0_, bf16[1024,2048]{1,0:T(8,128)(2,1)S(1)} %get-tuple-element.42.refs_1_), custom_call_target="tpu_custom_call" | custom-call | flops 268435456 | bytes 4194304 | tf_op jit(solution)/shard_map/project/pallas_call | solution.py:453
  38.5 0.8 %project.5.refs_2_ = f32[64,2048]{1,0:T(8,128)S(1)} custom-call(bf16[64,1024]{1,0:T(8,128)(2,1)S(1)} %collective-permute-done.8.refs_0_, bf16[1024,2048]{1,0:T(8,128)(2,1)S(1)} %get-tuple-element.41.refs_1_, f32[64,2048]{1,0:T(8,128)S(1)} %project.4.refs_2_), custom_call_target="tpu_custom_call" | custom-call | flops 268435456 | bytes 4194304 | tf_op jit(solution)/shard_map/project/pallas_call | solution.py:453
  39.4 0.8 %project.6.refs_2_ = f32[64,2048]{1,0:T(8,128)S(1)} custom-call(bf16[64,1024]{1,0:T(8,128)(2,1)S(1)} %collective-permute-done.7.refs_0_, bf16[1024,2048]{1,0:T(8,128)(2,1)S(1)} %get-tuple-element.40.refs_1_, f32[64,2048]{1,0:T(8,128)S(1)} %project.5.refs_2_), custom_call_target="tpu_custom_call" | custom-call | flops 268435456 | bytes 4194304 | tf_op jit(solution)/shard_map/project/pallas_call | solution.py:453
  40.2 0.9 %project.7 = (f32[32,2048]{1,0:T(8,128)S(1)}, bf16[32,2048]{1,0:T(8,128)(2,1)S(1)}) custom-call(bf16[64,1024]{1,0:T(8,128)(2,1)S(1)} %collective-permute-done.6.refs_0_, bf16[1024,2048]{1,0:T(8,128)(2,1)S(1)} %get-tuple-element.39.refs_1_, f32[64,2048]{1,0:T(8,128)S(1)} %project.6.refs_2_), custom_call_target="tpu_custom_call" | custom-call | flops 268435456 | bytes 4194304 | tf_op jit(solution)/shard_map/project/pallas_call | solution.py:453
  41.3 4.8 %collective-permute-done.9 = bf16[32,2048]{1,0:T(8,128)(2,1)S(1)} collective-permute-done((bf16[32,2048]{1,0:T(8,128)(2,1)S(1)}, bf16[32,2048]{1,0:T(8,128)(2,1)S(1)}, u32[]{:S(2)}, u32[]{:S(2)}) %collective-permute-start.9) | collective-permute-done | bytes 131104 | tf_op jit(solution)/shard_map/ppermute | solution.py:141
  46.1 0.7 %fusion = bf16[1,32,2048]{2,1,0:T(8,128)(2,1)} fusion(f32[32,2048]{1,0:T(8,128)S(1)} %get-tuple-element.43, bf16[32,2048]{1,0:T(8,128)(2,1)S(1)} %collective-permute-done.9), kind=kLoop, calls=%fused_computation.1 | loop fusion | flops 196608 | bytes 524288 | tf_op jit(solution)/shard_map/broadcast_in_dim | solution.py:491
  (24 shorter events, 1.6 us)
Async XLA Ops:
  0.0 1.0 %copy-start = (bf16[512,512]{1,0:T(8,128)(2,1)S(1)}, bf16[512,512]{1,0:T(8,128)(2,1)}, u32[]{:S(2)}) copy-start(bf16[512,512]{1,0:T(8,128)(2,1)} %k_ref.1) | copy-start | bytes 1572868
  1.0 1.0 %copy-start.1 = (bf16[512,512]{1,0:T(8,128)(2,1)S(1)}, bf16[512,512]{1,0:T(8,128)(2,1)}, u32[]{:S(2)}) copy-start(bf16[512,512]{1,0:T(8,128)(2,1)} %v_ref.1) | copy-start | bytes 1572868
  2.2 14.7 %collective-permute-start = (bf16[512,128]{1,0:T(8,128)(2,1)S(1)}, bf16[512,128]{1,0:T(8,128)(2,1)S(1)}, u32[]{:S(2)}, u32[]{:S(2)}) collective-permute-start(bf16[512,128]{1,0:T(8,128)(2,1)S(1)} %get-tuple-element.29), channel_id=1, source_target_pairs={{0,12},{4,8},{8,4},{12,0},{1,13},{5,9},{9,5},{13,1},{2,14},{6,10},... | collective-permute-start | bytes 393224 | tf_op jit(solution)/shard_map/ppermute | solution.py:141
  7.3 11.1 %collective-permute-start.1 = (bf16[512,128]{1,0:T(8,128)(2,1)S(1)}, bf16[512,128]{1,0:T(8,128)(2,1)S(1)}, u32[]{:S(2)}, u32[]{:S(2)}) collective-permute-start(bf16[512,128]{1,0:T(8,128)(2,1)S(1)} %get-tuple-element.30), channel_id=1, source_target_pairs={{0,8},{4,12},{8,0},{12,4},{1,9},{5,13},{9,1},{13,5},{2,10},{6,14},... | collective-permute-start | bytes 393224 | tf_op jit(solution)/shard_map/ppermute | solution.py:141
  7.3 11.1 %collective-permute-start.2 = (bf16[512,128]{1,0:T(8,128)(2,1)S(1)}, bf16[512,128]{1,0:T(8,128)(2,1)S(1)}, u32[]{:S(2)}, u32[]{:S(2)}) collective-permute-start(bf16[512,128]{1,0:T(8,128)(2,1)S(1)} %get-tuple-element.31), channel_id=1, source_target_pairs={{0,4},{4,0},{8,12},{12,8},{1,5},{5,1},{9,13},{13,9},{2,6},{6,2},{1... | collective-permute-start | bytes 393224 | tf_op jit(solution)/shard_map/ppermute | solution.py:141
  8.0 0.9 %copy-start.2 = (bf16[1,8,8192]{2,1,0:T(8,128)(2,1)S(1)}, bf16[1,8,8192]{2,1,0:T(8,128)(2,1)}, u32[]{:S(2)}) copy-start(bf16[1,8,8192]{2,1,0:T(8,128)(2,1)} %param.7) | copy-start | bytes 393220
  8.9 0.7 %copy-start.3 = (bf16[1,8,1024]{2,1,0:T(8,128)(2,1)S(1)}, bf16[1,8,1024]{2,1,0:T(8,128)(2,1)}, u32[]{:S(2)}) copy-start(bf16[1,8,1024]{2,1,0:T(8,128)(2,1)} %param.8) | copy-start | bytes 49156
  9.6 0.7 %copy-start.4 = (bf16[1,8,1024]{2,1,0:T(8,128)(2,1)S(1)}, bf16[1,8,1024]{2,1,0:T(8,128)(2,1)}, u32[]{:S(2)}) copy-start(bf16[1,8,1024]{2,1,0:T(8,128)(2,1)} %param.9) | copy-start | bytes 49156
  11.0 13.5 %all-to-all-start = ((bf16[8,8,1280]{2,1,0:T(8,128)(2,1)}), bf16[8,8,1280]{2,1,0:T(8,128)(2,1)S(1)}, u32[]{:S(2)}, u32[]{:S(2)}) async-start(bf16[8,8,1280]{2,1,0:T(8,128)(2,1)} %bitcast.3), calls=%async_computation | async-start | bytes 327680 | tf_op jit(solution)/shard_map/all_to_all | solution.py:472
  16.9 2.0 %copy-start.5 = (s32[1,64]{1,0:T(1,128)S(1)}, s32[1,64]{1,0:T(1,128)}, u32[]{:S(2)}) copy-start(s32[1,64]{1,0:T(1,128)} %visible_ref.1) | copy-start | bytes 772
  18.4 6.8 %collective-permute-start.3 = (bf16[512,128]{1,0:T(8,128)(2,1)S(1)}, bf16[512,128]{1,0:T(8,128)(2,1)S(1)}, u32[]{:S(2)}, u32[]{:S(2)}) collective-permute-start(bf16[512,128]{1,0:T(8,128)(2,1)S(1)} %get-tuple-element.32.mine_ref), channel_id=1, source_target_pairs={{0,1},{1,0},{2,3},{3,2},{4,5},{5,4},{6,7},{7,6},{8,9},{9,8},{10,11... | collective-permute-start | bytes 393224 | tf_op jit(solution)/shard_map/ppermute | solution.py:141
  18.4 7.5 %collective-permute-start.4 = (bf16[512,128]{1,0:T(8,128)(2,1)S(1)}, bf16[512,128]{1,0:T(8,128)(2,1)S(1)}, u32[]{:S(2)}, u32[]{:S(2)}) collective-permute-start(bf16[512,128]{1,0:T(8,128)(2,1)S(1)} %get-tuple-element.35.mine_ref), channel_id=1, source_target_pairs={{0,1},{1,0},{2,3},{3,2},{4,5},{5,4},{6,7},{7,6},{8,9},{9,8},{10,11... | collective-permute-start | bytes 393224 | tf_op jit(solution)/shard_map/ppermute | solution.py:141
  18.9 7.6 %collective-permute-start.5 = (bf16[512,128]{1,0:T(8,128)(2,1)S(1)}, bf16[512,128]{1,0:T(8,128)(2,1)S(1)}, u32[]{:S(2)}, u32[]{:S(2)}) collective-permute-start(bf16[512,128]{1,0:T(8,128)(2,1)S(1)} %get-tuple-element.38.mine_ref), channel_id=1, source_target_pairs={{0,1},{1,0},{2,3},{3,2},{4,5},{5,4},{6,7},{7,6},{8,9},{9,8},{10,11... | collective-permute-start | bytes 393224 | tf_op jit(solution)/shard_map/ppermute | solution.py:141
  27.3 11.2 %collective-permute-start.8 = (bf16[64,1024]{1,0:T(8,128)(2,1)S(1)}, bf16[64,1024]{1,0:T(8,128)(2,1)S(1)}, u32[]{:S(2)}, u32[]{:S(2)}) collective-permute-start(bf16[64,1024]{1,0:T(8,128)(2,1)S(1)} %attend_last.1.refs_0_), channel_id=1, source_target_pairs={{0,12},{4,8},{8,4},{12,0},{1,13},{5,9},{9,5},{13,1},{2,14},{6,10},... | collective-permute-start | bytes 393224 | tf_op jit(solution)/shard_map/ppermute | solution.py:141
  27.9 11.5 %collective-permute-start.7 = (bf16[64,1024]{1,0:T(8,128)(2,1)S(1)}, bf16[64,1024]{1,0:T(8,128)(2,1)S(1)}, u32[]{:S(2)}, u32[]{:S(2)}) collective-permute-start(bf16[64,1024]{1,0:T(8,128)(2,1)S(1)} %attend_last.1.refs_0_), channel_id=1, source_target_pairs={{0,8},{4,12},{8,0},{12,4},{1,9},{5,13},{9,1},{13,5},{2,10},{6,14},... | collective-permute-start | bytes 393224 | tf_op jit(solution)/shard_map/ppermute | solution.py:141
  28.7 11.6 %collective-permute-start.6 = (bf16[64,1024]{1,0:T(8,128)(2,1)S(1)}, bf16[64,1024]{1,0:T(8,128)(2,1)S(1)}, u32[]{:S(2)}, u32[]{:S(2)}) collective-permute-start(bf16[64,1024]{1,0:T(8,128)(2,1)S(1)} %attend_last.1.refs_0_), channel_id=1, source_target_pairs={{0,4},{4,0},{8,12},{12,8},{1,5},{5,1},{9,13},{13,9},{2,6},{6,2},{1... | collective-permute-start | bytes 393224 | tf_op jit(solution)/shard_map/ppermute | solution.py:141
  41.1 5.0 %collective-permute-start.9 = (bf16[32,2048]{1,0:T(8,128)(2,1)S(1)}, bf16[32,2048]{1,0:T(8,128)(2,1)S(1)}, u32[]{:S(2)}, u32[]{:S(2)}) collective-permute-start(bf16[32,2048]{1,0:T(8,128)(2,1)S(1)} %get-tuple-element.44), channel_id=1, source_target_pairs={{0,2},{2,0},{1,3},{3,1},{4,6},{6,4},{5,7},{7,5},{8,10},{10,8},{9,1... | collective-permute-start | bytes 393224 | tf_op jit(solution)/shard_map/ppermute | solution.py:141

commit v3 on v2

--- a/solution.py
+++ b/solution.py
@@ -131,10 +131,13 @@
 EXPONENT = SCALE * math.log2(math.e)
 VMEM_BYTES = 20 * 2**20
 SETTLE = 10**11
-ORDER = -1
-PACK_BYTES = int(63.5 * 2**20)
+UNIT_ROWS = 128
+PACK_BYTES = 56 * 2**20
+LATE_NEAR = False
+PARTS = 1
+ORDER = 1
+LOAD_BYTES = 30 * 2**20
 PROJECT_BYTES = 16 * 2**20
-LOAD_BYTES = 30 * 2**20
 
 
 def swap(array, axis, mask):
@@ -194,13 +197,22 @@
     )(prefix_keys, cached_value_rows)
 
 
-def pack_queries_kernel(seq_count, q_ref, fk_ref, fv_ref, out_ref):
-    tokens = q_ref.shape[0]
+def pack_queries_kernel(seq_count, *refs):
+    row_refs, out_ref, held_refs, sems = refs[:3], refs[3], refs[4:7], refs[7]
+    copies = [
+        pltpu.make_async_copy(ref, held, sems.at[i])
+        for i, (ref, held) in enumerate(zip(row_refs, held_refs))
+    ]
+    for copy in copies:
+        copy.start()
+    for copy in copies:
+        copy.wait()
+    tokens = row_refs[0].shape[0]
     count = out_ref.shape[0] // tokens
     for owner in range(count):
         head = owner % 2 * seq_count + owner // 2
         to = 0
-        for ref in (q_ref, fk_ref, fv_ref):
+        for ref in held_refs:
             part = ref.shape[1] // count
             out_ref[owner * tokens : (owner + 1) * tokens, to : to + part] = ref[
                 :, head * part : (head + 1) * part
@@ -214,9 +226,11 @@
     return pl.pallas_call(
         functools.partial(pack_queries_kernel, seq_count),
         out_shape=jax.ShapeDtypeStruct(shape, jnp.bfloat16),
-        in_specs=[vmem()] * 3,
+        in_specs=[hbm()] * 3,
         out_specs=vmem(),
-        compiler_params=params(),
+        scratch_shapes=[pltpu.VMEM(a.shape, a.dtype) for a in rows]
+        + [pltpu.SemaphoreType.DMA((3,))],
+        compiler_params=params(PACK_BYTES),
         cost_estimate=cost(0, 2**19),
         name="pack_queries",
     )(*rows)
@@ -261,125 +275,80 @@
     )(visible)
 
 
-def attend_step(query, lengths, position, keys, values, peak, acc):
-    count = keys.shape[0]
-    scores = lax.dot_general(
-        query, keys, (((1,), (1,)), ((), ())), preferred_element_type=jnp.float32
-    )
-    scores = jnp.where(position < side_by_side(lengths, count // HEAD_WIDTH), scores, HIDDEN)
-    new_peak = jnp.maximum(peak, jnp.max(scores, axis=-1, keepdims=True))
-    weights = jnp.exp2((scores - side_by_side(new_peak, count // HEAD_WIDTH)) * EXPONENT)
-    fade = jnp.exp2((peak - new_peak) * EXPONENT)
-    with_ones = jnp.concatenate([values, jnp.ones_like(values)], axis=1)
-    acc = acc * side_by_side(fade, 2) + jnp.dot(
-        weights.astype(jnp.bfloat16), with_ones, preferred_element_type=jnp.float32
-    )
-    return new_peak, acc
-
-
-def join(refs, first, count):
-    return jnp.concatenate([ref[first : first + count, :] for ref in refs], axis=0)
-
-
-def attend_first_kernel(
-    heads, block_rows, rows_ref, lengths_ref, own_ref, stacked_ref, peak_ref, acc_ref
+def attend_kernel(
+    heads, masks, block_rows, rows_ref, lengths_ref, own_ref, *refs
 ):
-    seq = lax.axis_index("seq")
-    tokens = rows_ref.shape[0]
-    lengths = lengths_ref[...]
+    piece_refs, out_ref = refs[:-1], refs[-1]
+    seq, rep = lax.axis_index("seq"), lax.axis_index("rep")
+    tokens = out_ref.shape[0]
+    half = block_rows // 2
+    lane = lax.broadcasted_iota(jnp.int32, (1, half), 1)
+    blocks = []
+    for core in range(2):
+        rows = slice(core * half, (core + 1) * half)
+        values = slice(block_rows + core * half, block_rows + (core + 1) * half)
+        blocks.append((own_ref, rows, values, seq * block_rows + core * half + lane))
+    for i, ref in enumerate(piece_refs):
+        mask, core = masks[i // 2], (rep if i % 2 == 0 else 1 - rep)
+        first = (seq ^ mask) * block_rows + core * half
+        blocks.append((ref, slice(0, half), slice(half, 2 * half), first + lane))
     width = heads * HEAD_WIDTH
     fresh_key = rows_ref[:, width : width + HEAD_WIDTH].astype(jnp.float32)
     fresh_value = rows_ref[:, width + HEAD_WIDTH :].astype(jnp.float32)
+    group = max(1, UNIT_ROWS // tokens)
+    lengths = jnp.concatenate([lengths_ref[...]] * group, axis=0)
+    fresh_key = jnp.concatenate([fresh_key] * group, axis=0)
     start = jnp.concatenate([fresh_value, jnp.ones_like(fresh_value)], axis=1)
-    keys, values = own_ref[:block_rows, :], own_ref[block_rows:, :]
-    position = seq * block_rows + lax.broadcasted_iota(jnp.int32, (1, block_rows), 1)
-    for h in range(0, heads, 2):
-        rows = slice(h * tokens, (h + 2) * tokens)
+    start = jnp.concatenate([start] * group, axis=0)
+    for first in range(0, heads, group):
         query = jnp.concatenate(
-            [rows_ref[:, i * HEAD_WIDTH : (i + 1) * HEAD_WIDTH] for i in (h, h + 1)], axis=0
-        )
-        own = jnp.sum(
-            query.astype(jnp.float32) * jnp.concatenate([fresh_key] * 2, axis=0),
-            axis=-1,
-            keepdims=True,
-        )
-        stacked_ref[rows, :] = query
-        peak, acc = attend_step(
-            query,
-            jnp.concatenate([lengths] * 2, axis=0),
-            position,
-            keys,
-            values,
-            jnp.broadcast_to(own, (2 * tokens, HEAD_WIDTH)),
-            jnp.concatenate([start] * 2, axis=0),
-        )
-        peak_ref[rows, :] = peak
-        acc_ref[rows, :] = acc
-
-
-def attend_first(heads, query_rows, lengths, own):
-    rows = heads * query_rows.shape[0]
+            [
+                rows_ref[:, h * HEAD_WIDTH : (h + 1) * HEAD_WIDTH]
+                for h in range(first, first + group)
+            ],
+            axis=0,
+        )
+        own = jnp.sum(query.astype(jnp.float32) * fresh_key, axis=-1, keepdims=True)
+        own = jnp.broadcast_to(own, (group * tokens, HEAD_WIDTH))
+        top, scores = own, []
+        for ref, rows, _, position in blocks:
+            score = lax.dot_general(
+                query, ref[rows, :], (((1,), (1,)), ((), ())), preferred_element_type=jnp.float32
+            )
+            hidden = position >= side_by_side(lengths, half // HEAD_WIDTH)
+            score = jnp.where(hidden, HIDDEN, score)
+            for i in range(0, half, HEAD_WIDTH):
+                top = jnp.maximum(top, score[:, i : i + HEAD_WIDTH])
+            scores.append(score)
+        peak = jnp.broadcast_to(jnp.max(top, axis=-1, keepdims=True), own.shape)
+        acc = start * side_by_side(jnp.exp2((own - peak) * EXPONENT), 2)
+        for score, (ref, _, rows, _) in zip(scores, blocks):
+            weights = jnp.exp2((score - side_by_side(peak, half // HEAD_WIDTH)) * EXPONENT)
+            values = ref[rows, :]
+            acc = acc + jnp.dot(
+                weights.astype(jnp.bfloat16),
+                jnp.concatenate([values, jnp.ones_like(values)], axis=1),
+                preferred_element_type=jnp.float32,
+            )
+        context = (acc[:, :HEAD_WIDTH] / acc[:, HEAD_WIDTH:]).astype(jnp.bfloat16)
+        for i in range(group):
+            column = (first + i) * HEAD_WIDTH
+            out_ref[:, column : column + HEAD_WIDTH] = context[i * tokens : (i + 1) * tokens, :]
+
+
+def attend(heads, masks, query_rows, lengths, own, pieces):
+    tokens = query_rows.shape[0]
     block_rows = own.shape[0] // 2
-    return pl.pallas_call(
-        functools.partial(attend_first_kernel, heads, block_rows),
-        out_shape=(
-            jax.ShapeDtypeStruct((rows, HEAD_WIDTH), jnp.bfloat16),
-            jax.ShapeDtypeStruct((rows, HEAD_WIDTH), jnp.float32),
-            jax.ShapeDtypeStruct((rows, 2 * HEAD_WIDTH), jnp.float32),
-        ),
-        in_specs=[vmem()] * 3,
-        out_specs=(vmem(),) * 3,
+    work = tokens * heads * block_rows * (1 + len(masks))
+    return pl.pallas_call(
+        functools.partial(attend_kernel, heads, masks, block_rows),
+        out_shape=jax.ShapeDtypeStruct((tokens, heads * HEAD_WIDTH), jnp.bfloat16),
+        in_specs=[vmem()] * (3 + len(pieces)),
+        out_specs=vmem(),
         compiler_params=params(),
-        cost_estimate=cost(6 * rows * block_rows * HEAD_WIDTH, 2**20, rows * block_rows),
-        name="attend_first",
-    )(query_rows, lengths, own)
-
-
-def attend_more_kernel(
-    block_rows, mask, last, query_ref, lengths_ref, peak_in, acc_in, mine_ref, other_ref, *outs
-):
-    seq, rep = lax.axis_index("seq"), lax.axis_index("rep")
-    half = block_rows // 2
-    tokens = lengths_ref.shape[0]
-    lengths = jnp.concatenate([lengths_ref[...]] * 2, axis=0)
-    base = (seq ^ mask) * 2 * half
-    keys = join((mine_ref, other_ref), 0, half)
-    values = join((mine_ref, other_ref), half, half)
-    lane = lax.broadcasted_iota(jnp.int32, (1, 2 * half), 1)
-    position = base + jnp.where(rep == 0, lane, jnp.where(lane < half, lane + half, lane - half))
-    for first in range(0, query_ref.shape[0], 2 * tokens):
-        rows = slice(first, first + 2 * tokens)
-        state = peak_in[rows, :], acc_in[rows, :]
-        state = attend_step(
-            query_ref[rows, :], lengths, position, keys, values, *state
-        )
-        if last:
-            context = state[1][:, :HEAD_WIDTH] / state[1][:, HEAD_WIDTH:]
-            for i in range(2):
-                column = (first // tokens + i) * HEAD_WIDTH
-                outs[0][:, column : column + HEAD_WIDTH] = context[
-                    i * tokens : (i + 1) * tokens, :
-                ].astype(jnp.bfloat16)
-        else:
-            outs[0][rows, :], outs[1][rows, :] = state
-
-
-def attend_more(positions, mask, last, stacked, lengths, state, mine, other):
-    rows, tokens = stacked.shape[0], lengths.shape[0]
-    shapes = (
-        (jax.ShapeDtypeStruct((tokens, rows // tokens * HEAD_WIDTH), jnp.bfloat16),)
-        if last
-        else tuple(jax.ShapeDtypeStruct(a.shape, a.dtype) for a in state)
-    )
-    return pl.pallas_call(
-        functools.partial(attend_more_kernel, positions, mask, last),
-        out_shape=shapes,
-        in_specs=[vmem()] * 6,
-        out_specs=(vmem(),) * len(shapes),
-        compiler_params=params(),
-        cost_estimate=cost(6 * rows * positions * HEAD_WIDTH, 2**20, rows * positions),
-        name="attend_last" if last else "attend_more",
-    )(stacked, lengths, *state, mine, other)
+        cost_estimate=cost(6 * work * HEAD_WIDTH, 2**20, work),
+        name="attend",
+    )(query_rows, lengths, own, *pieces)
 
 
 def load_kernel(masks, weight_ref, *refs):
@@ -394,7 +363,7 @@
             tile_ref.at[pl.ds(n * rows, rows), :],
             sems.at[i * steps + n],
         )
-        for i, (mask, tile_ref) in enumerate(zip([0] + masks, tile_refs))
+        for i, (mask, tile_ref) in enumerate(zip(masks, tile_refs))
         for n in range(steps)
     ]
     for copy in copies:
@@ -403,62 +372,97 @@
         copy.wait()
 
 
-def load(weight, masks):
-    count = 1 + len(masks)
-    shape = jax.ShapeDtypeStruct((weight.shape[0] // count, weight.shape[1]), weight.dtype)
+def load(weight, masks, count):
+    depth, columns = weight.shape[0] // count, weight.shape[1]
     return pl.pallas_call(
         functools.partial(load_kernel, masks),
-        out_shape=[shape] * count,
+        out_shape=[jax.ShapeDtypeStruct((depth, columns), weight.dtype)] * len(masks),
         in_specs=[hbm()],
-        out_specs=[vmem()] * count,
-        scratch_shapes=[pltpu.SemaphoreType.DMA((4 * count,))],
+        out_specs=[vmem()] * len(masks),
+        scratch_shapes=[pltpu.SemaphoreType.DMA((4 * len(masks),))],
         compiler_params=params(LOAD_BYTES),
-        cost_estimate=cost(0, weight.size * 2),
+        cost_estimate=cost(0, len(masks) * depth * columns * 2),
         name="load",
     )(weight)
 
 
-def project_kernel(first, last, *refs):
-    x_ref, w_ref = refs[:2]
-    acc_ref = None if first else refs[2]
-    outs = refs[2 if first else 3 :]
-    tp = lax.axis_index("tp")
+def project_kernel(x_ref, w_ref, *refs):
+    acc_refs, out_ref = refs[:-1], refs[-1]
     columns = w_ref.shape[1]
     width = math.gcd(columns, 512)
-    keep_rows = x_ref.shape[0] // 2
     for start in range(0, columns, width):
         at = slice(start, start + width)
         part = jnp.dot(x_ref[...], w_ref[:, at], preferred_element_type=jnp.float32)
-        if not first:
+        for acc_ref in acc_refs:
             part = part + acc_ref[:, at]
-        if last:
-            low, high = part[:keep_rows, :], part[keep_rows:, :]
-            outs[0][:, at] = jnp.where(tp == 0, low, high)
-            outs[1][:, at] = jnp.where(tp == 0, high, low).astype(jnp.bfloat16)
-        else:
-            outs[0][:, at] = part
-
-
-def project(context, tile, acc, last):
-    tokens, depth = context.shape
-    columns = tile.shape[1]
-    if last:
-        shapes = [
-            jax.ShapeDtypeStruct((tokens // 2, columns), jnp.float32),
-            jax.ShapeDtypeStruct((tokens // 2, columns), jnp.bfloat16),
-        ]
-    else:
-        shapes = [jax.ShapeDtypeStruct((tokens, columns), jnp.float32)]
-    operands = [context, tile] + ([] if acc is None else [acc])
-    return pl.pallas_call(
-        functools.partial(project_kernel, acc is None, last),
-        out_shape=shapes,
-        in_specs=[vmem()] * len(operands),
-        out_specs=[vmem()] * len(shapes),
+        out_ref[:, at] = part
+
+
+def project(context, tile, acc):
+    tokens, columns = context.shape[0], tile.shape[1]
+    return pl.pallas_call(
+        project_kernel,
+        out_shape=jax.ShapeDtypeStruct((tokens, columns), jnp.float32),
+        in_specs=[vmem()] * (2 + len(acc)),
+        out_specs=vmem(),
         compiler_params=params(PROJECT_BYTES),
-        cost_estimate=cost(2 * tokens * depth * columns, 2 * depth * columns),
+        cost_estimate=cost(2 * context.size * columns, 2 * tile.size),
         name="project",
-    )(*operands)
+    )(context, tile, *acc)
+
+
+def last_kernel(first, x_ref, w_ref, acc_ref, keep_ref, send_ref):
+    tp = lax.axis_index("tp")
+    half = x_ref.shape[0] // 2
+    columns = send_ref.shape[1]
+    width = math.gcd(columns, 512)
+    for start in range(0, columns, width):
+        at, to = slice(first + start, first + start + width), slice(start, start + width)
+        part = jnp.dot(x_ref[...], w_ref[:, at], preferred_element_type=jnp.float32)
+        part = part + acc_ref[:, at]
+        low, high = part[:half, :], part[half:, :]
+        keep_ref[:, to] = jnp.where(tp == 0, low, high)
+        send_ref[:, to] = jnp.where(tp == 0, high, low).astype(jnp.bfloat16)
+
+
+def project_last(context, tile, acc, first, columns):
+    tokens = context.shape[0] // 2
+    return pl.pallas_call(
+        functools.partial(last_kernel, first),
+        out_shape=[
+            jax.ShapeDtypeStruct((tokens, columns), jnp.float32),
+            jax.ShapeDtypeStruct((tokens, columns), jnp.bfloat16),
+        ],
+        in_specs=[vmem()] * 3,
+        out_specs=[vmem()] * 2,
+        compiler_params=params(PROJECT_BYTES),
+        cost_estimate=cost(2 * context.size * columns, 2 * tile.shape[0] * columns),
+        name="project_last",
+    )(context, tile, acc)
+
+
+def add_kernel(*refs):
+    out_ref = refs[-1]
+    count = (len(refs) - 1) // 2
+    start = 0
+    for keep_ref, got_ref in zip(refs[:count], refs[count:-1]):
+        width = keep_ref.shape[1]
+        total = keep_ref[...] + got_ref[...].astype(jnp.float32)
+        out_ref[0, :, start : start + width] = total.astype(out_ref.dtype)
+        start += width
+
+
+def add(keeps, gots):
+    shape = (1, keeps[0].shape[0], sum(a.shape[1] for a in keeps))
+    return pl.pallas_call(
+        add_kernel,
+        out_shape=jax.ShapeDtypeStruct(shape, jnp.bfloat16),
+        in_specs=[vmem()] * (2 * len(keeps)),
+        out_specs=vmem(),
+        compiler_params=params(PROJECT_BYTES),
+        cost_estimate=cost(0, 2**19),
+        name="add",
+    )(*keeps, *gots)
 
 
 def shards_by_head(
@@ -468,27 +472,33 @@
     masks = list(range(1, lax.axis_size("seq")))[::ORDER]
     rows = [queries[0], fresh_key_rows[0], fresh_value_rows[0]]
     own, *pieces = pack_prefix(prefix_keys, cached_value_rows, masks)
-    mine = [swap(piece, "seq", mask) for piece, mask in zip(pieces, masks)]
+    near = masks.index(1)
+    mine = [swap(p, "seq", m) if m != 1 else p for p, m in zip(pieces, masks)]
+    if LATE_NEAR:
+        mine = list(lax.optimization_barrier(mine))
+    mine[near] = swap(mine[near], "seq", 1)
     query_rows = lax.all_to_all(
         pack_queries(rows, 1 + len(masks)), ("seq", "tp"), split_axis=0, concat_axis=0, tiled=True
     )
     lengths = spread_lengths(visible)
-    mine = settle(mine)
+    far = settle([piece for piece, mask in zip(mine, masks) if mask != 1])
+    mine = [*far[:near], mine[near], *far[near:]]
     other = [swap(piece, "rep", 1) for piece in mine]
 
-    stacked, *state = attend_first(heads, query_rows, lengths, own)
-    for i, mask in enumerate(masks):
-        state = attend_more(
-            prefix_keys.shape[0], mask, mask == masks[-1], stacked, lengths, state, mine[i], other[i]
-        )
-    context = state[0]
-    tiles = load(out_weight, masks)
-    acc, send = None, None
-    for mask, tile in zip([0] + masks, tiles):
-        chunk = swap(context, "seq", mask) if mask else context
-        acc, *send = project(chunk, tile, acc, mask == masks[-1])
-    got = swap(send[0], "tp", 1)
-    return (acc + got.astype(jnp.float32)).astype(jnp.bfloat16)[None]
+    pieces = [piece for pair in zip(mine, other) for piece in pair]
+    context = attend(heads, masks, query_rows, lengths, own, pieces)
+
+    chunks = [swap(context, "seq", mask) for mask in masks]
+    tiles = load(out_weight, [0] + masks, 1 + len(masks))
+    acc = []
+    for chunk, tile in zip([context] + chunks[:-1], tiles):
+        acc = [project(chunk, tile, acc)]
+    acc = acc[0]
+    columns = acc.shape[1] // PARTS
+    parts = [
+        project_last(chunks[-1], tiles[-1], acc, i * columns, columns) for i in range(PARTS)
+    ]
+    return add([keep for keep, _ in parts], [swap(send, "tp", 1) for _, send in parts])
 
 
 def solution(mesh):

time: 47.2 us -> 45.6 us (0.966)
  local copies, waits for them, and re-layouts: 4.42 us -> 2.09 us
  Pallas kernels: 12.9 us -> 13.7 us
  other arithmetic: 0.69 us -> 0 us
  starting transfers between devices: 16.9 us -> 17.4 us
    unnamed x12 -> x6, local copies, waits for them, and re-layouts: 4.42 us -> 2.09 us
    ppermute x10, waiting for transfers between devices: 6.31 us -> 8.41 us  [swap(): lax.ppermute(array, axis, [(i, i ^ mask) for i in range(lax.axis_size(axi...]
    all_to_all x1, waiting for transfers between devices: 5.41 us -> 3.61 us  [shards_by_head(): lax.all_to_all(pack_queries(rows, 1 + len(masks)), ('seq', 'tp'), split_a...]
    ppermute x10, starting transfers between devices: 11 us -> 12.2 us  [swap(): lax.ppermute(array, axis, [(i, i ^ mask) for i in range(lax.axis_size(axi...]
    pallas_call x1, Pallas kernels: 0.68 us -> 1.62 us  [pack_queries(): pl.pallas_call(functools.partial(pack_queries_kernel, seq_count), out_sha...]
    all_to_all x1, starting transfers between devices: 5.95 us -> 5.14 us  [shards_by_head(): lax.all_to_all(pack_queries(rows, 1 + len(masks)), ('seq', 'tp'), split_a...]
    broadcast_in_dim x1 -> x0, other arithmetic: 0.69 us -> none  [shards_by_head(): return (acc + got.astype(jnp.float32)).astype(jnp.bfloat16)[None]]
    pallas_call x9 -> x7, Pallas kernels: 12 us -> 11.9 us  [the longest x1 5.93 us: load(): pl.pallas_call(functools.partial(load_kernel, masks), out_shape=[jax.Shap...]
  transfers between devices with their start and end apart: 11 -> 11, of which waited for: 3 -> 8; matrix products, arithmetic and copies ran while one was open for 0% -> 0% of each run, Pallas kernels for 24% -> 22%
where the time goes in v3:
time: 45.6 us; the launch traced here: 45.2 us
  starting transfers between devices  17.4 us (38%)
  Pallas kernels  13.7 us (30%)
  waiting for transfers between devices  12 us (26%)
  local copies, waits for them, and re-layouts  2.09 us (5%)
    ppermute x10, starting transfers between devices, swap(): lax.ppermute(array, axis, [(i, i ^ mask) for i in range(lax.axis_size(axi...  12.2 us
    ppermute x10, waiting for transfers between devices, swap(): lax.ppermute(array, axis, [(i, i ^ mask) for i in range(lax.axis_size(axi...  8.41 us
    pallas_call x1, Pallas kernels, load(): pl.pallas_call(functools.partial(load_kernel, masks), out_shape=[jax.Shap...  5.93 us
    all_to_all x1, starting transfers between devices, shards_by_head(): lax.all_to_all(pack_queries(rows, 1 + len(masks)), ('seq', 'tp'), split_a...  5.14 us
    all_to_all x1, waiting for transfers between devices, shards_by_head(): lax.all_to_all(pack_queries(rows, 1 + len(masks)), ('seq', 'tp'), split_a...  3.61 us
    pallas_call x3, Pallas kernels, project(): pl.pallas_call(project_kernel, out_shape=jax.ShapeDtypeStruct((tokens, co...  2.53 us
    unnamed x6, local copies, waits for them, and re-layouts  2.09 us
    pallas_call x1, Pallas kernels, attend(): pl.pallas_call(functools.partial(attend_kernel, heads, masks, block_rows)...  1.86 us
  transfers between devices with their start and end apart: 11, of which 8 were waited for; matrix products, arithmetic and copies ran while one was open for 0% of the time, Pallas kernels for 22%

profile of v3, /device:TPU:0, one launch (start us, length us, event | category | flops | bytes accessed | tf_op | source)
XLA Modules:
  0.0 45.2 jit_solution(16790476672699195728)
XLA Ops:
  0.0 1.0 %copy-done = bf16[512,512]{1,0:T(8,128)(2,1)S(1)} copy-done((bf16[512,512]{1,0:T(8,128)(2,1)S(1)}, bf16[512,512]{1,0:T(8,128)(2,1)}, u32[]{:S(2)}) %copy-start) | copy-done | bytes 524312
  1.0 1.0 %copy-done.1 = bf16[512,512]{1,0:T(8,128)(2,1)S(1)} copy-done((bf16[512,512]{1,0:T(8,128)(2,1)S(1)}, bf16[512,512]{1,0:T(8,128)(2,1)}, u32[]{:S(2)}) %copy-start.1) | copy-done | bytes 524312
  2.2 4.1 %collective-permute-start.2 = (bf16[512,128]{1,0:T(8,128)(2,1)S(1)}, bf16[512,128]{1,0:T(8,128)(2,1)S(1)}, u32[]{:S(2)}, u32[]{:S(2)}) collective-permute-start(bf16[512,128]{1,0:T(8,128)(2,1)S(1)} %get-tuple-element.19), channel_id=1, source_target_pairs={{0,8},{4,12},{8,0},{12,4},{1,9},{5,13},{9,1},{13,5},{2,10},{6,14},... | collective-permute-start | bytes 393224 | tf_op jit(solution)/shard_map/ppermute | solution.py:144
  6.3 1.3 %collective-permute-start.3 = (bf16[512,128]{1,0:T(8,128)(2,1)S(1)}, bf16[512,128]{1,0:T(8,128)(2,1)S(1)}, u32[]{:S(2)}, u32[]{:S(2)}) collective-permute-start(bf16[512,128]{1,0:T(8,128)(2,1)S(1)} %get-tuple-element.20), channel_id=1, source_target_pairs={{0,12},{4,8},{8,4},{12,0},{1,13},{5,9},{9,5},{13,1},{2,14},{6,10},... | collective-permute-start | bytes 393224 | tf_op jit(solution)/shard_map/ppermute | solution.py:144
  7.9 1.6 %pack_queries.1 = bf16[64,1280]{1,0:T(8,128)(2,1)} custom-call(bf16[8,8192]{1,0:T(8,128)(2,1)} %bitcast.7, bf16[8,1024]{1,0:T(8,128)(2,1)} %bitcast.8, bf16[8,1024]{1,0:T(8,128)(2,1)} %bitcast.9), custom_call_target="tpu_custom_call" | custom-call | bytes 524288 | tf_op jit(solution)/shard_map/pack_queries/pallas_call | solution.py:226
  9.5 5.1 %all-to-all-start = ((bf16[8,8,1280]{2,1,0:T(8,128)(2,1)}), bf16[8,8,1280]{2,1,0:T(8,128)(2,1)S(1)}, u32[]{:S(2)}, u32[]{:S(2)}) async-start(bf16[8,8,1280]{2,1,0:T(8,128)(2,1)} %bitcast.6), calls=%async_computation | async-start | bytes 327680 | tf_op jit(solution)/shard_map/all_to_all | solution.py:480
  14.6 1.6 %collective-permute-done.2.refs_0_ = bf16[512,128]{1,0:T(8,128)(2,1)S(1)} collective-permute-done((bf16[512,128]{1,0:T(8,128)(2,1)S(1)}, bf16[512,128]{1,0:T(8,128)(2,1)S(1)}, u32[]{:S(2)}, u32[]{:S(2)}) %collective-permute-start.2) | collective-permute-done | bytes 131104 | tf_op jit(solution)/shard_map/ppermute | solution.py:144
  16.3 0.5 %collective-permute-start.5 = (bf16[512,128]{1,0:T(8,128)(2,1)S(1)}, bf16[512,128]{1,0:T(8,128)(2,1)S(1)}, u32[]{:S(2)}, u32[]{:S(2)}) collective-permute-start(bf16[512,128]{1,0:T(8,128)(2,1)S(1)} %get-tuple-element.22.refs_4_), channel_id=1, source_target_pairs={{0,1},{1,0},{2,3},{3,2},{4,5},{5,4},{6,7},{7,6},{8,9},{9,8},{10,11... | collective-permute-start | bytes 393224 | tf_op jit(solution)/shard_map/ppermute | solution.py:144
  16.8 0.4 collective-permute-done.refs_0_
  17.8 0.8 %collective-permute-done.1.refs_1_ = bf16[512,128]{1,0:T(8,128)(2,1)S(1)} collective-permute-done((bf16[512,128]{1,0:T(8,128)(2,1)S(1)}, bf16[512,128]{1,0:T(8,128)(2,1)S(1)}, u32[]{:S(2)}, u32[]{:S(2)}) %collective-permute-start.1) | collective-permute-done | bytes 131104 | tf_op jit(solution)/shard_map/ppermute | solution.py:144
  18.6 3.6 %all-to-all-done = bf16[8,8,1280]{2,1,0:T(8,128)(2,1)S(1)} async-done(((bf16[8,8,1280]{2,1,0:T(8,128)(2,1)}), bf16[8,8,1280]{2,1,0:T(8,128)(2,1)S(1)}, u32[]{:S(2)}, u32[]{:S(2)}) %all-to-all-start) | async-done | bytes 163872 | tf_op jit(solution)/shard_map/all_to_all | solution.py:480
  22.2 1.9 %attend.1.x_ref = bf16[64,1024]{1,0:T(8,128)(2,1)S(1)} custom-call(bf16[64,1280]{1,0:T(8,128)(2,1)S(1)} %bitcast.5, s32[64,128]{1,0:T(8,128)S(1)} %spread_lengths.1.lengths_ref, bf16[1024,128]{1,0:T(8,128)(2,1)S(1)} %get-tuple-element.17.own_ref, bf16[512,128]{1,0:T(8,128)(2,1)S(1)} %collective-permute-done.refs_0_, ...), custom_call_target="tpu_custom_call" | custom-call | flops 805306368 | bytes 1048576 | tf_op jit(solution)/shard_map/attend/pallas_call | solution.py:343
  24.1 1.0 %collective-permute-start.8 = (bf16[64,1024]{1,0:T(8,128)(2,1)S(1)}, bf16[64,1024]{1,0:T(8,128)(2,1)S(1)}, u32[]{:S(2)}, u32[]{:S(2)}) collective-permute-start(bf16[64,1024]{1,0:T(8,128)(2,1)S(1)} %attend.1.x_ref), channel_id=1, source_target_pairs={{0,4},{4,0},{8,12},{12,8},{1,5},{5,1},{9,13},{13,9},{2,6},{6,2},{1... | collective-permute-start | bytes 393224 | tf_op jit(solution)/shard_map/ppermute | solution.py:144
  25.0 2.8 %collective-permute-start.7 = (bf16[64,1024]{1,0:T(8,128)(2,1)S(1)}, bf16[64,1024]{1,0:T(8,128)(2,1)S(1)}, u32[]{:S(2)}, u32[]{:S(2)}) collective-permute-start(bf16[64,1024]{1,0:T(8,128)(2,1)S(1)} %attend.1.x_ref), channel_id=1, source_target_pairs={{0,8},{4,12},{8,0},{12,4},{1,9},{5,13},{9,1},{13,5},{2,10},{6,14},... | collective-permute-start | bytes 393224 | tf_op jit(solution)/shard_map/ppermute | solution.py:144
  27.8 0.7 %collective-permute-start.6 = (bf16[64,1024]{1,0:T(8,128)(2,1)S(1)}, bf16[64,1024]{1,0:T(8,128)(2,1)S(1)}, u32[]{:S(2)}, u32[]{:S(2)}) collective-permute-start(bf16[64,1024]{1,0:T(8,128)(2,1)S(1)} %attend.1.x_ref), channel_id=1, source_target_pairs={{0,12},{4,8},{8,4},{12,0},{1,13},{5,9},{9,5},{13,1},{2,14},{6,10},... | collective-permute-start | bytes 393224 | tf_op jit(solution)/shard_map/ppermute | solution.py:144
  28.5 5.9 %load.1 = (bf16[1024,2048]{1,0:T(8,128)(2,1)S(1)}, bf16[1024,2048]{1,0:T(8,128)(2,1)S(1)}, bf16[1024,2048]{1,0:T(8,128)(2,1)S(1)}, bf16[1024,2048]{1,0:T(8,128)(2,1)S(1)}) custom-call(bf16[4096,2048]{1,0:T(8,128)(2,1)} %weight_ref.1), custom_call_target="tpu_custom_call" | custom-call | bytes 16777216 | tf_op jit(solution)/shard_map/load/pallas_call | solution.py:377
  34.5 0.8 %project.3.refs_0_ = f32[64,2048]{1,0:T(8,128)S(1)} custom-call(bf16[64,1024]{1,0:T(8,128)(2,1)S(1)} %attend.1.x_ref, bf16[1024,2048]{1,0:T(8,128)(2,1)S(1)} %get-tuple-element.26.w_ref), custom_call_target="tpu_custom_call" | custom-call | flops 268435456 | bytes 4194304 | tf_op jit(solution)/shard_map/project/pallas_call | solution.py:403
  35.3 0.8 %project.4.refs_0_ = f32[64,2048]{1,0:T(8,128)S(1)} custom-call(bf16[64,1024]{1,0:T(8,128)(2,1)S(1)} %collective-permute-done.8.x_ref, bf16[1024,2048]{1,0:T(8,128)(2,1)S(1)} %get-tuple-element.25.w_ref, f32[64,2048]{1,0:T(8,128)S(1)} %project.3.refs_0_), custom_call_target="tpu_custom_call" | custom-call | flops 268435456 | bytes 4194304 | tf_op jit(solution)/shard_map/project/pallas_call | solution.py:403
  36.2 1.6 %collective-permute-done.7.x_ref = bf16[64,1024]{1,0:T(8,128)(2,1)S(1)} collective-permute-done((bf16[64,1024]{1,0:T(8,128)(2,1)S(1)}, bf16[64,1024]{1,0:T(8,128)(2,1)S(1)}, u32[]{:S(2)}, u32[]{:S(2)}) %collective-permute-start.7) | collective-permute-done | bytes 131104 | tf_op jit(solution)/shard_map/ppermute | solution.py:144
  37.8 0.8 %project.5.acc_ref = f32[64,2048]{1,0:T(8,128)S(1)} custom-call(bf16[64,1024]{1,0:T(8,128)(2,1)S(1)} %collective-permute-done.7.x_ref, bf16[1024,2048]{1,0:T(8,128)(2,1)S(1)} %get-tuple-element.24.w_ref, f32[64,2048]{1,0:T(8,128)S(1)} %project.4.refs_0_), custom_call_target="tpu_custom_call" | custom-call | flops 268435456 | bytes 4194304 | tf_op jit(solution)/shard_map/project/pallas_call | solution.py:403
  38.7 0.9 %project_last.1 = (f32[32,2048]{1,0:T(8,128)S(1)}, bf16[32,2048]{1,0:T(8,128)(2,1)S(1)}) custom-call(bf16[64,1024]{1,0:T(8,128)(2,1)S(1)} %collective-permute-done.6.x_ref, bf16[1024,2048]{1,0:T(8,128)(2,1)S(1)} %get-tuple-element.23.w_ref, f32[64,2048]{1,0:T(8,128)S(1)} %project.5.acc_ref), custom_call_target="tpu_custom_call" | custom-call | flops 268435456 | bytes 4194304 | tf_op jit(solution)/shard_map/project_last/pallas_call | solution.py:430
  39.5 1.6 %collective-permute-start.9 = (bf16[32,2048]{1,0:T(8,128)(2,1)S(1)}, bf16[32,2048]{1,0:T(8,128)(2,1)S(1)}, u32[]{:S(2)}, u32[]{:S(2)}) collective-permute-start(bf16[32,2048]{1,0:T(8,128)(2,1)S(1)} %get-tuple-element.28), channel_id=1, source_target_pairs={{0,2},{2,0},{1,3},{3,1},{4,6},{6,4},{5,7},{7,5},{8,10},{10,8},{9,1... | collective-permute-start | bytes 393224 | tf_op jit(solution)/shard_map/ppermute | solution.py:144
  41.1 3.5 %collective-permute-done.9.refs_1_ = bf16[32,2048]{1,0:T(8,128)(2,1)S(1)} collective-permute-done((bf16[32,2048]{1,0:T(8,128)(2,1)S(1)}, bf16[32,2048]{1,0:T(8,128)(2,1)S(1)}, u32[]{:S(2)}, u32[]{:S(2)}) %collective-permute-start.9) | collective-permute-done | bytes 131104 | tf_op jit(solution)/shard_map/ppermute | solution.py:144
  44.6 0.7 %add.1 = bf16[1,32,2048]{2,1,0:T(8,128)(2,1)} custom-call(f32[32,2048]{1,0:T(8,128)S(1)} %get-tuple-element.27.refs_0_, bf16[32,2048]{1,0:T(8,128)(2,1)S(1)} %collective-permute-done.9.refs_1_), custom_call_target="tpu_custom_call" | custom-call | bytes 524288 | tf_op jit(solution)/shard_map/add/pallas_call | solution.py:457
  (15 shorter events, 0.9 us)
Async XLA Ops:
  0.0 1.0 %copy-start = (bf16[512,512]{1,0:T(8,128)(2,1)S(1)}, bf16[512,512]{1,0:T(8,128)(2,1)}, u32[]{:S(2)}) copy-start(bf16[512,512]{1,0:T(8,128)(2,1)} %k_ref.1) | copy-start | bytes 1572868
  1.0 1.0 %copy-start.1 = (bf16[512,512]{1,0:T(8,128)(2,1)S(1)}, bf16[512,512]{1,0:T(8,128)(2,1)}, u32[]{:S(2)}) copy-start(bf16[512,512]{1,0:T(8,128)(2,1)} %v_ref.1) | copy-start | bytes 1572868
  2.2 14.1 %collective-permute-start.2 = (bf16[512,128]{1,0:T(8,128)(2,1)S(1)}, bf16[512,128]{1,0:T(8,128)(2,1)S(1)}, u32[]{:S(2)}, u32[]{:S(2)}) collective-permute-start(bf16[512,128]{1,0:T(8,128)(2,1)S(1)} %get-tuple-element.19), channel_id=1, source_target_pairs={{0,8},{4,12},{8,0},{12,4},{1,9},{5,13},{9,1},{13,5},{2,10},{6,14},... | collective-permute-start | bytes 393224 | tf_op jit(solution)/shard_map/ppermute | solution.py:144
  6.3 10.0 %collective-permute-start.3 = (bf16[512,128]{1,0:T(8,128)(2,1)S(1)}, bf16[512,128]{1,0:T(8,128)(2,1)S(1)}, u32[]{:S(2)}, u32[]{:S(2)}) collective-permute-start(bf16[512,128]{1,0:T(8,128)(2,1)S(1)} %get-tuple-element.20), channel_id=1, source_target_pairs={{0,12},{4,8},{8,4},{12,0},{1,13},{5,9},{9,5},{13,1},{2,14},{6,10},... | collective-permute-start | bytes 393224 | tf_op jit(solution)/shard_map/ppermute | solution.py:144
  7.7 9.6 %collective-permute-start = (bf16[512,128]{1,0:T(8,128)(2,1)S(1)}, bf16[512,128]{1,0:T(8,128)(2,1)S(1)}, u32[]{:S(2)}, u32[]{:S(2)}) collective-permute-start(bf16[512,128]{1,0:T(8,128)(2,1)S(1)} %get-tuple-element.18), channel_id=1, source_target_pairs={{0,4},{4,0},{8,12},{12,8},{1,5},{5,1},{9,13},{13,9},{2,6},{6,2},{1... | collective-permute-start | bytes 393224 | tf_op jit(solution)/shard_map/ppermute | solution.py:144
  9.5 12.7 %all-to-all-start = ((bf16[8,8,1280]{2,1,0:T(8,128)(2,1)}), bf16[8,8,1280]{2,1,0:T(8,128)(2,1)S(1)}, u32[]{:S(2)}, u32[]{:S(2)}) async-start(bf16[8,8,1280]{2,1,0:T(8,128)(2,1)} %bitcast.6), calls=%async_computation | async-start | bytes 327680 | tf_op jit(solution)/shard_map/all_to_all | solution.py:480
  14.6 2.6 %copy-start.2 = (s32[1,64]{1,0:T(1,128)S(1)}, s32[1,64]{1,0:T(1,128)}, u32[]{:S(2)}) copy-start(s32[1,64]{1,0:T(1,128)} %visible_ref.1) | copy-start | bytes 772
  16.3 1.3 %collective-permute-start.4 = (bf16[512,128]{1,0:T(8,128)(2,1)S(1)}, bf16[512,128]{1,0:T(8,128)(2,1)S(1)}, u32[]{:S(2)}, u32[]{:S(2)}) collective-permute-start(bf16[512,128]{1,0:T(8,128)(2,1)S(1)} %get-tuple-element.21.refs_2_), channel_id=1, source_target_pairs={{0,1},{1,0},{2,3},{3,2},{4,5},{5,4},{6,7},{7,6},{8,9},{9,8},{10,11... | collective-permute-start | bytes 393224 | tf_op jit(solution)/shard_map/ppermute | solution.py:144
  16.3 1.5 %collective-permute-start.5 = (bf16[512,128]{1,0:T(8,128)(2,1)S(1)}, bf16[512,128]{1,0:T(8,128)(2,1)S(1)}, u32[]{:S(2)}, u32[]{:S(2)}) collective-permute-start(bf16[512,128]{1,0:T(8,128)(2,1)S(1)} %get-tuple-element.22.refs_4_), channel_id=1, source_target_pairs={{0,1},{1,0},{2,3},{3,2},{4,5},{5,4},{6,7},{7,6},{8,9},{9,8},{10,11... | collective-permute-start | bytes 393224 | tf_op jit(solution)/shard_map/ppermute | solution.py:144
  17.2 1.3 %collective-permute-start.1 = (bf16[512,128]{1,0:T(8,128)(2,1)S(1)}, bf16[512,128]{1,0:T(8,128)(2,1)S(1)}, u32[]{:S(2)}, u32[]{:S(2)}) collective-permute-start(bf16[512,128]{1,0:T(8,128)(2,1)S(1)} %collective-permute-done.refs_0_), channel_id=1, source_target_pairs={{0,1},{1,0},{2,3},{3,2},{4,5},{5,4},{6,7},{7,6},{8,9},{9,8},{10,11... | collective-permute-start | bytes 393224 | tf_op jit(solution)/shard_map/ppermute | solution.py:144
  24.1 11.2 %collective-permute-start.8 = (bf16[64,1024]{1,0:T(8,128)(2,1)S(1)}, bf16[64,1024]{1,0:T(8,128)(2,1)S(1)}, u32[]{:S(2)}, u32[]{:S(2)}) collective-permute-start(bf16[64,1024]{1,0:T(8,128)(2,1)S(1)} %attend.1.x_ref), channel_id=1, source_target_pairs={{0,4},{4,0},{8,12},{12,8},{1,5},{5,1},{9,13},{13,9},{2,6},{6,2},{1... | collective-permute-start | bytes 393224 | tf_op jit(solution)/shard_map/ppermute | solution.py:144
  25.0 12.8 %collective-permute-start.7 = (bf16[64,1024]{1,0:T(8,128)(2,1)S(1)}, bf16[64,1024]{1,0:T(8,128)(2,1)S(1)}, u32[]{:S(2)}, u32[]{:S(2)}) collective-permute-start(bf16[64,1024]{1,0:T(8,128)(2,1)S(1)} %attend.1.x_ref), channel_id=1, source_target_pairs={{0,8},{4,12},{8,0},{12,4},{1,9},{5,13},{9,1},{13,5},{2,10},{6,14},... | collective-permute-start | bytes 393224 | tf_op jit(solution)/shard_map/ppermute | solution.py:144
  27.8 10.8 %collective-permute-start.6 = (bf16[64,1024]{1,0:T(8,128)(2,1)S(1)}, bf16[64,1024]{1,0:T(8,128)(2,1)S(1)}, u32[]{:S(2)}, u32[]{:S(2)}) collective-permute-start(bf16[64,1024]{1,0:T(8,128)(2,1)S(1)} %attend.1.x_ref), channel_id=1, source_target_pairs={{0,12},{4,8},{8,4},{12,0},{1,13},{5,9},{9,5},{13,1},{2,14},{6,10},... | collective-permute-start | bytes 393224 | tf_op jit(solution)/shard_map/ppermute | solution.py:144
  39.5 5.0 %collective-permute-start.9 = (bf16[32,2048]{1,0:T(8,128)(2,1)S(1)}, bf16[32,2048]{1,0:T(8,128)(2,1)S(1)}, u32[]{:S(2)}, u32[]{:S(2)}) collective-permute-start(bf16[32,2048]{1,0:T(8,128)(2,1)S(1)} %get-tuple-element.28), channel_id=1, source_target_pairs={{0,2},{2,0},{1,3},{3,1},{4,6},{6,4},{5,7},{7,5},{8,10},{10,8},{9,1... | collective-permute-start | bytes 393224 | tf_op jit(solution)/shard_map/ppermute | solution.py:144

commit v4 on v3

--- a/solution.py
+++ b/solution.py
@@ -130,12 +130,12 @@
 
 EXPONENT = SCALE * math.log2(math.e)
 VMEM_BYTES = 20 * 2**20
-SETTLE = 10**11
 UNIT_ROWS = 128
+FETCHES = 4
+SETTLE_FIRST = 10**11
+SETTLE_LAST = 10**10
 PACK_BYTES = 56 * 2**20
-LATE_NEAR = False
-PARTS = 1
-ORDER = 1
+ATTEND_BYTES = 40 * 2**20
 LOAD_BYTES = 30 * 2**20
 PROJECT_BYTES = 16 * 2**20
 
@@ -168,33 +168,6 @@
     return pl.CostEstimate(
         flops=flops, bytes_accessed=bytes_accessed, transcendentals=transcendentals
     )
-
-
-def pack_prefix_kernel(masks, k_ref, v_ref, own_ref, *piece_refs):
-    seq, rep = lax.axis_index("seq"), lax.axis_index("rep")
-    rows = k_ref.shape[0]
-    half = rows // 2
-    for j, table in enumerate((k_ref, v_ref)):
-        for mask, piece in zip(masks, piece_refs):
-            piece[j * half : (j + 1) * half, :] = table[
-                tile_at(rep, half), tile_at(seq ^ mask, HEAD_WIDTH)
-            ]
-    for j, table in enumerate((k_ref, v_ref)):
-        own_ref[j * rows : (j + 1) * rows, :] = table[:, tile_at(seq, HEAD_WIDTH)]
-
-
-def pack_prefix(prefix_keys, cached_value_rows, masks):
-    rows = prefix_keys.shape[0]
-    heights = [2 * rows] + [rows] * len(masks)
-    return pl.pallas_call(
-        functools.partial(pack_prefix_kernel, masks),
-        out_shape=[jax.ShapeDtypeStruct((n, HEAD_WIDTH), jnp.bfloat16) for n in heights],
-        in_specs=[vmem()] * 2,
-        out_specs=[vmem()] * len(heights),
-        compiler_params=params(),
-        cost_estimate=cost(0, 2 * 2**20),
-        name="pack_prefix",
-    )(prefix_keys, cached_value_rows)
 
 
 def pack_queries_kernel(seq_count, *refs):
@@ -240,7 +213,7 @@
     del refs
 
 
-def settle(arrays):
+def settle(arrays, declared):
     count = len(arrays)
     return pl.pallas_call(
         settle_kernel,
@@ -249,7 +222,7 @@
         out_specs=[vmem()] * count,
         input_output_aliases={i: i for i in range(count)},
         compiler_params=params(2**20),
-        cost_estimate=cost(SETTLE, 2**20),
+        cost_estimate=cost(declared, 2**20),
         name="settle",
     )(*arrays)
 
@@ -275,169 +248,185 @@
     )(visible)
 
 
-def attend_kernel(
-    heads, masks, block_rows, rows_ref, lengths_ref, own_ref, *refs
-):
-    piece_refs, out_ref = refs[:-1], refs[-1]
-    seq, rep = lax.axis_index("seq"), lax.axis_index("rep")
-    tokens = out_ref.shape[0]
-    half = block_rows // 2
-    lane = lax.broadcasted_iota(jnp.int32, (1, half), 1)
-    blocks = []
-    for core in range(2):
-        rows = slice(core * half, (core + 1) * half)
-        values = slice(block_rows + core * half, block_rows + (core + 1) * half)
-        blocks.append((own_ref, rows, values, seq * block_rows + core * half + lane))
-    for i, ref in enumerate(piece_refs):
-        mask, core = masks[i // 2], (rep if i % 2 == 0 else 1 - rep)
-        first = (seq ^ mask) * block_rows + core * half
-        blocks.append((ref, slice(0, half), slice(half, 2 * half), first + lane))
-    width = heads * HEAD_WIDTH
-    fresh_key = rows_ref[:, width : width + HEAD_WIDTH].astype(jnp.float32)
-    fresh_value = rows_ref[:, width + HEAD_WIDTH :].astype(jnp.float32)
-    group = max(1, UNIT_ROWS // tokens)
-    lengths = jnp.concatenate([lengths_ref[...]] * group, axis=0)
-    fresh_key = jnp.concatenate([fresh_key] * group, axis=0)
-    start = jnp.concatenate([fresh_value, jnp.ones_like(fresh_value)], axis=1)
-    start = jnp.concatenate([start] * group, axis=0)
-    for first in range(0, heads, group):
-        query = jnp.concatenate(
-            [
-                rows_ref[:, h * HEAD_WIDTH : (h + 1) * HEAD_WIDTH]
-                for h in range(first, first + group)
-            ],
-            axis=0,
-        )
-        own = jnp.sum(query.astype(jnp.float32) * fresh_key, axis=-1, keepdims=True)
-        own = jnp.broadcast_to(own, (group * tokens, HEAD_WIDTH))
-        top, scores = own, []
-        for ref, rows, _, position in blocks:
-            score = lax.dot_general(
-                query, ref[rows, :], (((1,), (1,)), ((), ())), preferred_element_type=jnp.float32
-            )
-            hidden = position >= side_by_side(lengths, half // HEAD_WIDTH)
-            score = jnp.where(hidden, HIDDEN, score)
-            for i in range(0, half, HEAD_WIDTH):
-                top = jnp.maximum(top, score[:, i : i + HEAD_WIDTH])
-            scores.append(score)
-        peak = jnp.broadcast_to(jnp.max(top, axis=-1, keepdims=True), own.shape)
-        acc = start * side_by_side(jnp.exp2((own - peak) * EXPONENT), 2)
-        for score, (ref, _, rows, _) in zip(scores, blocks):
-            weights = jnp.exp2((score - side_by_side(peak, half // HEAD_WIDTH)) * EXPONENT)
-            values = ref[rows, :]
-            acc = acc + jnp.dot(
-                weights.astype(jnp.bfloat16),
-                jnp.concatenate([values, jnp.ones_like(values)], axis=1),
-                preferred_element_type=jnp.float32,
-            )
-        context = (acc[:, :HEAD_WIDTH] / acc[:, HEAD_WIDTH:]).astype(jnp.bfloat16)
-        for i in range(group):
-            column = (first + i) * HEAD_WIDTH
-            out_ref[:, column : column + HEAD_WIDTH] = context[i * tokens : (i + 1) * tokens, :]
-
-
-def attend(heads, masks, query_rows, lengths, own, pieces):
-    tokens = query_rows.shape[0]
-    block_rows = own.shape[0] // 2
-    work = tokens * heads * block_rows * (1 + len(masks))
-    return pl.pallas_call(
-        functools.partial(attend_kernel, heads, masks, block_rows),
-        out_shape=jax.ShapeDtypeStruct((tokens, heads * HEAD_WIDTH), jnp.bfloat16),
-        in_specs=[vmem()] * (3 + len(pieces)),
-        out_specs=vmem(),
-        compiler_params=params(),
-        cost_estimate=cost(6 * work * HEAD_WIDTH, 2**20, work),
-        name="attend",
-    )(query_rows, lengths, own, *pieces)
-
-
-def load_kernel(masks, weight_ref, *refs):
-    tile_refs, sems = refs[:-1], refs[-1]
+def half_of(rows, side):
+    half = rows.shape[0] // 2
+    return jnp.where(side == 0, rows[:half, :], rows[half:, :])
+
+
+def tile_copies(masks, weight_ref, tile_refs, sems):
+    depth = tile_refs[0].shape[0]
+    rows = depth // FETCHES
     seq = lax.axis_index("seq")
-    depth = tile_refs[0].shape[0]
-    steps = sems.shape[0] // len(tile_refs)
-    rows = depth // steps
-    copies = [
+    return [
         pltpu.make_async_copy(
             weight_ref.at[pl.ds(pl.multiple_of((seq ^ mask) * depth + n * rows, rows), rows), :],
             tile_ref.at[pl.ds(n * rows, rows), :],
-            sems.at[i * steps + n],
+            sems.at[i * FETCHES + n],
         )
         for i, (mask, tile_ref) in enumerate(zip(masks, tile_refs))
-        for n in range(steps)
+        for n in range(FETCHES)
     ]
-    for copy in copies:
-        copy.start()
-    for copy in copies:
-        copy.wait()
-
-
-def load(weight, masks, count):
-    depth, columns = weight.shape[0] // count, weight.shape[1]
-    return pl.pallas_call(
-        functools.partial(load_kernel, masks),
-        out_shape=[jax.ShapeDtypeStruct((depth, columns), weight.dtype)] * len(masks),
-        in_specs=[hbm()],
-        out_specs=[vmem()] * len(masks),
-        scratch_shapes=[pltpu.SemaphoreType.DMA((4 * len(masks),))],
-        compiler_params=params(LOAD_BYTES),
-        cost_estimate=cost(0, len(masks) * depth * columns * 2),
-        name="load",
-    )(weight)
-
-
-def project_kernel(x_ref, w_ref, *refs):
-    acc_refs, out_ref = refs[:-1], refs[-1]
+
+
+def multiply(x_ref, w_ref, finish):
     columns = w_ref.shape[1]
     width = math.gcd(columns, 512)
     for start in range(0, columns, width):
         at = slice(start, start + width)
-        part = jnp.dot(x_ref[...], w_ref[:, at], preferred_element_type=jnp.float32)
-        for acc_ref in acc_refs:
-            part = part + acc_ref[:, at]
-        out_ref[:, at] = part
-
-
-def project(context, tile, acc):
+        finish(at, jnp.dot(x_ref[...], w_ref[:, at], preferred_element_type=jnp.float32))
+
+
+def attend_kernel(heads, masks, block_rows, rows_ref, lengths_ref, own_ref, *refs):
+    pieces = 2 * len(masks)
+    piece_refs, weight_ref = refs[:pieces], refs[pieces]
+    out_ref, theirs_ref, tile_ref, sems = refs[pieces + 1 :]
+    seq, tp, rep = lax.axis_index("seq"), lax.axis_index("tp"), lax.axis_index("rep")
+    copies = tile_copies([0], weight_ref, [tile_ref], sems)
+    for copy in copies:
+        copy.start()
+    @pl.when(tp >= 0)
+    def compute():
+        tokens = out_ref.shape[0]
+        half = block_rows // 2
+        lane = lax.broadcasted_iota(jnp.int32, (1, half), 1)
+        blocks = []
+        for core in range(2):
+            rows = slice(core * half, (core + 1) * half)
+            values = slice(block_rows + core * half, block_rows + (core + 1) * half)
+            blocks.append((own_ref, rows, values, seq * block_rows + core * half + lane))
+        for i, ref in enumerate(piece_refs):
+            mask, core = masks[i // 2], (rep if i % 2 == 0 else 1 - rep)
+            first = (seq ^ mask) * block_rows + core * half
+            blocks.append((ref, slice(0, half), slice(half, 2 * half), first + lane))
+        width = heads * HEAD_WIDTH
+        fresh_key = rows_ref[:, width : width + HEAD_WIDTH].astype(jnp.float32)
+        fresh_value = rows_ref[:, width + HEAD_WIDTH :].astype(jnp.float32)
+        group = max(1, UNIT_ROWS // tokens)
+        lengths = jnp.concatenate([lengths_ref[...]] * group, axis=0)
+        fresh_key = jnp.concatenate([fresh_key] * group, axis=0)
+        start = jnp.concatenate([fresh_value, jnp.ones_like(fresh_value)], axis=1)
+        start = jnp.concatenate([start] * group, axis=0)
+        for first in range(0, heads, group):
+            query = jnp.concatenate(
+                [
+                    rows_ref[:, h * HEAD_WIDTH : (h + 1) * HEAD_WIDTH]
+                    for h in range(first, first + group)
+                ],
+                axis=0,
+            )
+            own = jnp.sum(query.astype(jnp.float32) * fresh_key, axis=-1, keepdims=True)
+            own = jnp.broadcast_to(own, (group * tokens, HEAD_WIDTH))
+            top, scores = own, []
+            for ref, rows, _, position in blocks:
+                score = lax.dot_general(
+                    query, ref[rows, :], (((1,), (1,)), ((), ())), preferred_element_type=jnp.float32
+                )
+                hidden = position >= side_by_side(lengths, half // HEAD_WIDTH)
+                score = jnp.where(hidden, HIDDEN, score)
+                for i in range(0, half, HEAD_WIDTH):
+                    top = jnp.maximum(top, score[:, i : i + HEAD_WIDTH])
+                scores.append(score)
+            peak = jnp.broadcast_to(jnp.max(top, axis=-1, keepdims=True), own.shape)
+            acc = start * side_by_side(jnp.exp2((own - peak) * EXPONENT), 2)
+            for score, (ref, _, rows, _) in zip(scores, blocks):
+                weights = jnp.exp2((score - side_by_side(peak, half // HEAD_WIDTH)) * EXPONENT)
+                values = ref[rows, :]
+                acc = acc + jnp.dot(
+                    weights.astype(jnp.bfloat16),
+                    jnp.concatenate([values, jnp.ones_like(values)], axis=1),
+                    preferred_element_type=jnp.float32,
+                )
+            context = (acc[:, :HEAD_WIDTH] / acc[:, HEAD_WIDTH:]).astype(jnp.bfloat16)
+            for i in range(group):
+                column = (first + i) * HEAD_WIDTH
+                head = context[i * tokens : (i + 1) * tokens, :]
+                out_ref[:, column : column + HEAD_WIDTH] = head
+                theirs_ref[:, column : column + HEAD_WIDTH] = half_of(head, 1 - tp)
+
+    for copy in copies:
+        copy.wait()
+
+
+def attend(heads, masks, query_rows, lengths, own, pieces, weight):
+    tokens = query_rows.shape[0]
+    block_rows = own.shape[0] // 2
+    work = tokens * heads * block_rows * (1 + len(masks))
+    depth = heads * HEAD_WIDTH
+    return pl.pallas_call(
+        functools.partial(attend_kernel, heads, masks, block_rows),
+        out_shape=[
+            jax.ShapeDtypeStruct((tokens, depth), jnp.bfloat16),
+            jax.ShapeDtypeStruct((tokens // 2, depth), jnp.bfloat16),
+            jax.ShapeDtypeStruct((depth, weight.shape[1]), weight.dtype),
+        ],
+        in_specs=[vmem()] * (3 + len(pieces)) + [hbm()],
+        out_specs=[vmem()] * 3,
+        scratch_shapes=[pltpu.SemaphoreType.DMA((FETCHES,))],
+        compiler_params=params(ATTEND_BYTES),
+        cost_estimate=cost(6 * work * HEAD_WIDTH, 2**20, work),
+        name="attend",
+    )(query_rows, lengths, own, *pieces, weight)
+
+
+def load_kernel(masks, weight_ref, x_ref, first_ref, acc_ref, ours_ref, *refs):
+    tile_refs, sems = refs[:-1], refs[-1]
+    tp = lax.axis_index("tp")
+    copies = tile_copies(masks, weight_ref, tile_refs, sems)
+    for copy in copies:
+        copy.start()
+    ours_ref[...] = half_of(x_ref[...], tp)
+
+    def finish(at, part):
+        acc_ref[:, at] = part
+
+    @pl.when(tp >= 0)
+    def compute():
+        multiply(x_ref, first_ref, finish)
+
+    for copy in copies:
+        copy.wait()
+
+
+def load(weight, context, tile, masks):
+    tokens, (depth, columns) = context.shape[0], tile.shape
+    return pl.pallas_call(
+        functools.partial(load_kernel, masks),
+        out_shape=[
+            jax.ShapeDtypeStruct((tokens, columns), jnp.float32),
+            jax.ShapeDtypeStruct((tokens // 2, depth), jnp.bfloat16),
+        ]
+        + [jax.ShapeDtypeStruct(tile.shape, tile.dtype)] * len(masks),
+        in_specs=[hbm(), vmem(), vmem()],
+        out_specs=[vmem()] * (2 + len(masks)),
+        scratch_shapes=[pltpu.SemaphoreType.DMA((FETCHES * len(masks),))],
+        compiler_params=params(LOAD_BYTES),
+        cost_estimate=cost(2 * tokens * depth * columns, len(masks) * depth * columns * 2),
+        name="load",
+    )(weight, context, tile)
+
+
+def project_kernel(side, x_ref, w_ref, acc_ref, out_ref):
+    tp = lax.axis_index("tp")
+
+    def finish(at, part):
+        acc = acc_ref[:, at]
+        if side is not None:
+            acc = half_of(acc, tp if side == 0 else 1 - tp)
+        out_ref[:, at] = (part + acc).astype(out_ref.dtype)
+
+    multiply(x_ref, w_ref, finish)
+
+
+def project(context, tile, acc, side=None, dtype=jnp.float32):
     tokens, columns = context.shape[0], tile.shape[1]
     return pl.pallas_call(
-        project_kernel,
-        out_shape=jax.ShapeDtypeStruct((tokens, columns), jnp.float32),
-        in_specs=[vmem()] * (2 + len(acc)),
+        functools.partial(project_kernel, side),
+        out_shape=jax.ShapeDtypeStruct((tokens, columns), dtype),
+        in_specs=[vmem()] * 3,
         out_specs=vmem(),
         compiler_params=params(PROJECT_BYTES),
         cost_estimate=cost(2 * context.size * columns, 2 * tile.size),
         name="project",
-    )(context, tile, *acc)
-
-
-def last_kernel(first, x_ref, w_ref, acc_ref, keep_ref, send_ref):
-    tp = lax.axis_index("tp")
-    half = x_ref.shape[0] // 2
-    columns = send_ref.shape[1]
-    width = math.gcd(columns, 512)
-    for start in range(0, columns, width):
-        at, to = slice(first + start, first + start + width), slice(start, start + width)
-        part = jnp.dot(x_ref[...], w_ref[:, at], preferred_element_type=jnp.float32)
-        part = part + acc_ref[:, at]
-        low, high = part[:half, :], part[half:, :]
-        keep_ref[:, to] = jnp.where(tp == 0, low, high)
-        send_ref[:, to] = jnp.where(tp == 0, high, low).astype(jnp.bfloat16)
-
-
-def project_last(context, tile, acc, first, columns):
-    tokens = context.shape[0] // 2
-    return pl.pallas_call(
-        functools.partial(last_kernel, first),
-        out_shape=[
-            jax.ShapeDtypeStruct((tokens, columns), jnp.float32),
-            jax.ShapeDtypeStruct((tokens, columns), jnp.bfloat16),
-        ],
-        in_specs=[vmem()] * 3,
-        out_specs=[vmem()] * 2,
-        compiler_params=params(PROJECT_BYTES),
-        cost_estimate=cost(2 * context.size * columns, 2 * tile.shape[0] * columns),
-        name="project_last",
     )(context, tile, acc)
 
 
@@ -469,36 +458,44 @@
     queries, fresh_key_rows, fresh_value_rows, visible, prefix_keys, cached_value_rows, out_weight
 ):
     heads = queries.shape[2] // fresh_key_rows.shape[2]
-    masks = list(range(1, lax.axis_size("seq")))[::ORDER]
+    masks = list(range(1, lax.axis_size("seq")))
     rows = [queries[0], fresh_key_rows[0], fresh_value_rows[0]]
-    own, *pieces = pack_prefix(prefix_keys, cached_value_rows, masks)
+    seq, rep = lax.axis_index("seq"), lax.axis_index("rep")
+    half_rows = prefix_keys.shape[0] // 2
+
+    def cut(first, count, head):
+        return jnp.concatenate(
+            [
+                lax.dynamic_slice(table, (first, head * HEAD_WIDTH), (count, HEAD_WIDTH))
+                for table in (prefix_keys, cached_value_rows)
+            ]
+        )
+
+    pieces = [cut(rep * half_rows, half_rows, seq ^ mask) for mask in masks]
+    own = cut(0, 2 * half_rows, seq)
     near = masks.index(1)
-    mine = [swap(p, "seq", m) if m != 1 else p for p, m in zip(pieces, masks)]
-    if LATE_NEAR:
-        mine = list(lax.optimization_barrier(mine))
-    mine[near] = swap(mine[near], "seq", 1)
+    mine = [swap(piece, "seq", mask) for piece, mask in zip(pieces, masks)]
     query_rows = lax.all_to_all(
         pack_queries(rows, 1 + len(masks)), ("seq", "tp"), split_axis=0, concat_axis=0, tiled=True
     )
     lengths = spread_lengths(visible)
-    far = settle([piece for piece, mask in zip(mine, masks) if mask != 1])
+    far = settle([piece for piece, mask in zip(mine, masks) if mask != 1], SETTLE_FIRST)
     mine = [*far[:near], mine[near], *far[near:]]
     other = [swap(piece, "rep", 1) for piece in mine]
 
     pieces = [piece for pair in zip(mine, other) for piece in pair]
-    context = attend(heads, masks, query_rows, lengths, own, pieces)
-
-    chunks = [swap(context, "seq", mask) for mask in masks]
-    tiles = load(out_weight, [0] + masks, 1 + len(masks))
-    acc = []
-    for chunk, tile in zip([context] + chunks[:-1], tiles):
-        acc = [project(chunk, tile, acc)]
-    acc = acc[0]
-    columns = acc.shape[1] // PARTS
-    parts = [
-        project_last(chunks[-1], tiles[-1], acc, i * columns, columns) for i in range(PARTS)
-    ]
-    return add([keep for keep, _ in parts], [swap(send, "tp", 1) for _, send in parts])
+    context, theirs, tile = attend(heads, masks, query_rows, lengths, own, pieces, out_weight)
+
+    order = masks[-1:] + masks[:-1]
+    far = order[-1]
+    chunks = [swap(context, "seq", mask) for mask in order[:-1]]
+    first = swap(theirs, "seq", far)
+    acc, ours, *tiles = load(out_weight, context, tile, order)
+    (second,) = settle([swap(ours, "seq", far)], SETTLE_LAST)
+    for chunk, tile in zip(chunks, tiles):
+        acc = project(chunk, tile, acc)
+    got = swap(project(first, tiles[-1], acc, 1, jnp.bfloat16), "tp", 1)
+    return add([project(second, tiles[-1], acc, 0)], [got])
 
 
 def solution(mesh):
@@ -519,7 +516,7 @@
         local_heads = args[4].shape[1] // HEAD_WIDTH
         by_head = (
             local_heads == seq_count
-            and seq_count & (seq_count - 1) == 0
+            and seq_count in (4, 8)
             and sizes["tp"] == 2
             and sizes["rep"] == 2
             and args[0].shape[2] // args[1].shape[2] % 2 == 0

time: 45.6 us -> 43.3 us (0.950)
  waiting for transfers between devices: 12 us -> 9.53 us
  starting transfers between devices: 17.4 us -> 18.6 us
  Pallas kernels: 13.7 us -> 12.7 us
    ppermute x10 -> x11, waiting for transfers between devices: 8.41 us -> 5.89 us  [swap(): lax.ppermute(array, axis, [(i, i ^ mask) for i in range(lax.axis_size(axi...]
    unnamed x6 -> x2, local copies, waits for them, and re-layouts: 2.09 us -> 0.01 us
    dynamic_slice x0 -> x2, local copies, waits for them, and re-layouts: none -> 2.02 us  [cut(): lax.dynamic_slice(table, (first, head * HEAD_WIDTH), (count, HEAD_WIDTH))]
    ppermute x10 -> x11, starting transfers between devices: 12.2 us -> 13.5 us  [swap(): lax.ppermute(array, axis, [(i, i ^ mask) for i in range(lax.axis_size(axi...]
    pallas_call x1, Pallas kernels: 5.93 us -> 4.71 us  [load(): pl.pallas_call(functools.partial(load_kernel, masks), out_shape=[jax.Shap...]
    pallas_call x5 -> x4, Pallas kernels: 3.5 us -> 3.35 us  [project(): pl.pallas_call(functools.partial(project_kernel, side), out_shape=jax.Sha...]
  transfers between devices with their start and end apart: 11 -> 12, of which waited for: 8 -> 7; matrix products, arithmetic and copies ran while one was open for 0% -> 2% of each run, Pallas kernels for 22% -> 23%
where the time goes in v4:
time: 43.3 us; the launch traced here: 43 us
  starting transfers between devices  18.6 us (43%)
  Pallas kernels  12.7 us (29%)
  waiting for transfers between devices  9.53 us (22%)
  local copies, waits for them, and re-layouts  2.03 us (5%)
    ppermute x11, starting transfers between devices, swap(): lax.ppermute(array, axis, [(i, i ^ mask) for i in range(lax.axis_size(axi...  13.5 us
    ppermute x11, waiting for transfers between devices, swap(): lax.ppermute(array, axis, [(i, i ^ mask) for i in range(lax.axis_size(axi...  5.89 us
    all_to_all x1, starting transfers between devices, shards_by_head(): lax.all_to_all(pack_queries(rows, 1 + len(masks)), ('seq', 'tp'), split_a...  5.12 us
    pallas_call x1, Pallas kernels, load(): pl.pallas_call(functools.partial(load_kernel, masks), out_shape=[jax.Shap...  4.71 us
    all_to_all x1, waiting for transfers between devices, shards_by_head(): lax.all_to_all(pack_queries(rows, 1 + len(masks)), ('seq', 'tp'), split_a...  3.64 us
    pallas_call x4, Pallas kernels, project(): pl.pallas_call(functools.partial(project_kernel, side), out_shape=jax.Sha...  3.35 us
    pallas_call x1, Pallas kernels, attend(): pl.pallas_call(functools.partial(attend_kernel, heads, masks, block_rows)...  2.21 us
    dynamic_slice x2, local copies, waits for them, and re-layouts, cut(): lax.dynamic_slice(table, (first, head * HEAD_WIDTH), (count, HEAD_WIDTH))  2.02 us
  transfers between devices with their start and end apart: 12, of which 7 were waited for; matrix products, arithmetic and copies ran while one was open for 2% of the time, Pallas kernels for 23%

profile of v4, /device:TPU:0, one launch (start us, length us, event | category | flops | bytes accessed | tf_op | source)
XLA Modules:
  0.0 43.0 jit_solution(12572200176717865296)
XLA Ops:
  0.0 1.0 %fusion = (bf16[256,128]{1,0:T(8,128)(2,1)S(1)}, bf16[256,128]{1,0:T(8,128)(2,1)S(1)}, bf16[256,128]{1,0:T(8,128)(2,1)S(1)}, bf16[256,128]{1,0:T(8,128)(2,1)S(1)...) fusion(bf16[512,512]{1,0:T(8,128)(2,1)} %param.11, s32[]{:T(128)S(6)} %select_n.11, s32[]{:T(128)S(6)} %select_n.28, ...), kind=kLoop, calls=%fused_computation.6 | loop fusion | bytes 786448 | tf_op jit(solution)/shard_map/dynamic_slice | solution.py:469
  1.1 4.1 %collective-permute-start.2 = (bf16[512,128]{1,0:T(8,128)(2,1)S(1)}, bf16[512,128]{1,0:T(8,128)(2,1)S(1)}, u32[]{:S(2)}, u32[]{:S(2)}) collective-permute-start(bf16[512,128]{1,0:T(8,128)(2,1)S(1)} %pad_maximum_fusion.2), channel_id=1, source_target_pairs={{0,8},{4,12},{8,0},{12,4},{1,9},{5,13},{9,1},{13,5},{2,10},{6,14},... | collective-permute-start | bytes 393224 | tf_op jit(solution)/shard_map/ppermute | solution.py:144
  5.2 1.4 %collective-permute-start.3 = (bf16[512,128]{1,0:T(8,128)(2,1)S(1)}, bf16[512,128]{1,0:T(8,128)(2,1)S(1)}, u32[]{:S(2)}, u32[]{:S(2)}) collective-permute-start(bf16[512,128]{1,0:T(8,128)(2,1)S(1)} %pad_maximum_fusion.3), channel_id=1, source_target_pairs={{0,12},{4,8},{8,4},{12,0},{1,13},{5,9},{9,5},{13,1},{2,14},{6,10},... | collective-permute-start | bytes 393224 | tf_op jit(solution)/shard_map/ppermute | solution.py:144
  6.6 0.3 collective-permute-start
  6.9 1.6 %pack_queries.1 = bf16[64,1280]{1,0:T(8,128)(2,1)} custom-call(bf16[8,8192]{1,0:T(8,128)(2,1)} %bitcast.7, bf16[8,1024]{1,0:T(8,128)(2,1)} %bitcast.8, bf16[8,1024]{1,0:T(8,128)(2,1)} %bitcast.9), custom_call_target="tpu_custom_call" | custom-call | bytes 524288 | tf_op jit(solution)/shard_map/pack_queries/pallas_call | solution.py:199
  8.5 5.1 %all-to-all-start = ((bf16[8,8,1280]{2,1,0:T(8,128)(2,1)}), bf16[8,8,1280]{2,1,0:T(8,128)(2,1)S(1)}, u32[]{:S(2)}, u32[]{:S(2)}) async-start(bf16[8,8,1280]{2,1,0:T(8,128)(2,1)} %bitcast.6), calls=%async_computation | async-start | bytes 327680 | tf_op jit(solution)/shard_map/all_to_all | solution.py:478
  13.7 1.5 %collective-permute-done.2.refs_0_ = bf16[512,128]{1,0:T(8,128)(2,1)S(1)} collective-permute-done((bf16[512,128]{1,0:T(8,128)(2,1)S(1)}, bf16[512,128]{1,0:T(8,128)(2,1)S(1)}, u32[]{:S(2)}, u32[]{:S(2)}) %collective-permute-start.2) | collective-permute-done | bytes 131104 | tf_op jit(solution)/shard_map/ppermute | solution.py:144
  15.2 0.5 %collective-permute-start.5 = (bf16[512,128]{1,0:T(8,128)(2,1)S(1)}, bf16[512,128]{1,0:T(8,128)(2,1)S(1)}, u32[]{:S(2)}, u32[]{:S(2)}) collective-permute-start(bf16[512,128]{1,0:T(8,128)(2,1)S(1)} %get-tuple-element.16.refs_4_), channel_id=1, source_target_pairs={{0,1},{1,0},{2,3},{3,2},{4,5},{5,4},{6,7},{7,6},{8,9},{9,8},{10,11... | collective-permute-start | bytes 393224 | tf_op jit(solution)/shard_map/ppermute | solution.py:144
  15.7 0.6 %collective-permute-done.refs_0_ = bf16[512,128]{1,0:T(8,128)(2,1)S(1)} collective-permute-done((bf16[512,128]{1,0:T(8,128)(2,1)S(1)}, bf16[512,128]{1,0:T(8,128)(2,1)S(1)}, u32[]{:S(2)}, u32[]{:S(2)}) %collective-permute-start) | collective-permute-done | bytes 131104 | tf_op jit(solution)/shard_map/ppermute | solution.py:144
  16.2 1.0 %constant_dynamic-slice_fusion = (bf16[512,128]{1,0:T(8,128)(2,1)S(1)}, bf16[512,128]{1,0:T(8,128)(2,1)S(1)}) fusion(bf16[512,512]{1,0:T(8,128)(2,1)} %param.12, s32[]{:T(128)S(6)} %select_n.10, bf16[512,512]{1,0:T(8,128)(2,1)} %param.11), kind=kLoop, calls=%fused_computation.4 | loop fusion | bytes 524292 | tf_op jit(solution)/shard_map/dynamic_slice | solution.py:469
  17.6 3.6 %all-to-all-done = bf16[8,8,1280]{2,1,0:T(8,128)(2,1)S(1)} async-done(((bf16[8,8,1280]{2,1,0:T(8,128)(2,1)}), bf16[8,8,1280]{2,1,0:T(8,128)(2,1)S(1)}, u32[]{:S(2)}, u32[]{:S(2)}) %all-to-all-start) | async-done | bytes 163872 | tf_op jit(solution)/shard_map/all_to_all | solution.py:478
  21.2 2.2 %attend.1 = (bf16[64,1024]{1,0:T(8,128)(2,1)S(1)}, bf16[32,1024]{1,0:T(8,128)(2,1)S(1)}, bf16[1024,2048]{1,0:T(8,128)(2,1)S(1)}) custom-call(bf16[64,1280]{1,0:T(8,128)(2,1)S(1)} %bitcast.5, s32[64,128]{1,0:T(8,128)S(1)} %spread_lengths.1.lengths_ref, bf16[1024,128]{1,0:T(8,128)(2,1)S(1)} %pad_maximum_fusion.own_ref, ...), custom_call_target="tpu_custom_call" | custom-call | flops 805306368 | bytes 1048576 | tf_op jit(solution)/shard_map/attend/pallas_call | solution.py:355
  23.4 3.0 %collective-permute-start.8 = (bf16[64,1024]{1,0:T(8,128)(2,1)S(1)}, bf16[64,1024]{1,0:T(8,128)(2,1)S(1)}, u32[]{:S(2)}, u32[]{:S(2)}) collective-permute-start(bf16[64,1024]{1,0:T(8,128)(2,1)S(1)} %get-tuple-element.17.x_ref), channel_id=1, source_target_pairs={{0,12},{4,8},{8,4},{12,0},{1,13},{5,9},{9,5},{13,1},{2,14},{6,10},... | collective-permute-start | bytes 393224 | tf_op jit(solution)/shard_map/ppermute | solution.py:144
  26.7 1.2 %collective-permute-start.9 = (bf16[32,1024]{1,0:T(8,128)(2,1)S(1)}, bf16[32,1024]{1,0:T(8,128)(2,1)S(1)}, u32[]{:S(2)}, u32[]{:S(2)}) collective-permute-start(bf16[32,1024]{1,0:T(8,128)(2,1)S(1)} %get-tuple-element.24), channel_id=1, source_target_pairs={{0,8},{4,12},{8,0},{12,4},{1,9},{5,13},{9,1},{13,5},{2,10},{6,14},... | collective-permute-start | bytes 196616 | tf_op jit(solution)/shard_map/ppermute | solution.py:144
  27.9 4.7 %load.1 = (f32[64,2048]{1,0:T(8,128)S(1)}, bf16[32,1024]{1,0:T(8,128)(2,1)S(1)}, bf16[1024,2048]{1,0:T(8,128)(2,1)S(1)}, bf16[1024,2048]{1,0:T(8,128)(2,1)S(1)}, bf16[1024,2048]{1,0:T(8,128)(2,1)S(1)}) custom-call(bf16[4096,2048]{1,0:T(8,128)(2,1)} %weight_ref.1, bf16[64,1024]{1,0:T(8,128)(2,1)S(1)} %get-tuple-element.17.x_ref, ...), custom_call_target="tpu_custom_call" | custom-call | flops 268435456 | bytes 12582912 | tf_op jit(solution)/shard_map/load/pallas_call | solution.py:392
  32.6 1.8 %collective-permute-start.6 = (bf16[32,1024]{1,0:T(8,128)(2,1)S(1)}, bf16[32,1024]{1,0:T(8,128)(2,1)S(1)}, u32[]{:S(2)}, u32[]{:S(2)}) collective-permute-start(bf16[32,1024]{1,0:T(8,128)(2,1)S(1)} %get-tuple-element.19), channel_id=1, source_target_pairs={{0,8},{4,12},{8,0},{12,4},{1,9},{5,13},{9,1},{13,5},{2,10},{6,14},... | collective-permute-start | bytes 196616 | tf_op jit(solution)/shard_map/ppermute | solution.py:144
  34.4 0.8 %project.4.acc_ref = f32[64,2048]{1,0:T(8,128)S(1)} custom-call(bf16[64,1024]{1,0:T(8,128)(2,1)S(1)} %collective-permute-done.8.x_ref, bf16[1024,2048]{1,0:T(8,128)(2,1)S(1)} %get-tuple-element.22.w_ref, f32[64,2048]{1,0:T(8,128)S(1)} %get-tuple-element.23.acc_ref), custom_call_target="tpu_custom_call" | custom-call | flops 268435456 | bytes 4194304 | tf_op jit(solution)/shard_map/project/pallas_call | solution.py:422
  35.3 0.8 %project.5.acc_ref = f32[64,2048]{1,0:T(8,128)S(1)} custom-call(bf16[64,1024]{1,0:T(8,128)(2,1)S(1)} %collective-permute-done.7.x_ref, bf16[1024,2048]{1,0:T(8,128)(2,1)S(1)} %get-tuple-element.21.w_ref, f32[64,2048]{1,0:T(8,128)S(1)} %project.4.acc_ref), custom_call_target="tpu_custom_call" | custom-call | flops 268435456 | bytes 4194304 | tf_op jit(solution)/shard_map/project/pallas_call | solution.py:422
  36.1 0.4 collective-permute-done.9.x_ref
  36.5 0.8 %project.7 = bf16[32,2048]{1,0:T(8,128)(2,1)S(1)} custom-call(bf16[32,1024]{1,0:T(8,128)(2,1)S(1)} %collective-permute-done.9.x_ref, bf16[1024,2048]{1,0:T(8,128)(2,1)S(1)} %get-tuple-element.20.w_ref, f32[64,2048]{1,0:T(8,128)S(1)} %project.5.acc_ref), custom_call_target="tpu_custom_call" | custom-call | flops 134217728 | bytes 4194304 | tf_op jit(solution)/shard_map/project/pallas_call | solution.py:422
  37.3 0.9 %collective-permute-start.10 = (bf16[32,2048]{1,0:T(8,128)(2,1)S(1)}, bf16[32,2048]{1,0:T(8,128)(2,1)S(1)}, u32[]{:S(2)}, u32[]{:S(2)}) collective-permute-start(bf16[32,2048]{1,0:T(8,128)(2,1)S(1)} %project.7), channel_id=1, source_target_pairs={{0,2},{2,0},{1,3},{3,1},{4,6},{6,4},{5,7},{7,5},{8,10},{10,8},{9,1... | collective-permute-start | bytes 393224 | tf_op jit(solution)/shard_map/ppermute | solution.py:144
  38.5 0.8 %project.6.refs_0_ = f32[32,2048]{1,0:T(8,128)S(1)} custom-call(bf16[32,1024]{1,0:T(8,128)(2,1)S(1)} %settle.3.x_ref, bf16[1024,2048]{1,0:T(8,128)(2,1)S(1)} %get-tuple-element.20.w_ref, f32[64,2048]{1,0:T(8,128)S(1)} %project.5.acc_ref), custom_call_target="tpu_custom_call" | custom-call | flops 134217728 | bytes 4194304 | tf_op jit(solution)/shard_map/project/pallas_call | solution.py:422
  39.4 2.9 %collective-permute-done.10.refs_1_ = bf16[32,2048]{1,0:T(8,128)(2,1)S(1)} collective-permute-done((bf16[32,2048]{1,0:T(8,128)(2,1)S(1)}, bf16[32,2048]{1,0:T(8,128)(2,1)S(1)}, u32[]{:S(2)}, u32[]{:S(2)}) %collective-permute-start.10) | collective-permute-done | bytes 131104 | tf_op jit(solution)/shard_map/ppermute | solution.py:144
  42.3 0.7 %add.30 = bf16[1,32,2048]{2,1,0:T(8,128)(2,1)} custom-call(f32[32,2048]{1,0:T(8,128)S(1)} %project.6.refs_0_, bf16[32,2048]{1,0:T(8,128)(2,1)S(1)} %collective-permute-done.10.refs_1_), custom_call_target="tpu_custom_call" | custom-call | bytes 524288 | tf_op jit(solution)/shard_map/add/pallas_call | solution.py:446
  (19 shorter events, 0.9 us)
Async XLA Ops:
  1.1 14.1 %collective-permute-start.2 = (bf16[512,128]{1,0:T(8,128)(2,1)S(1)}, bf16[512,128]{1,0:T(8,128)(2,1)S(1)}, u32[]{:S(2)}, u32[]{:S(2)}) collective-permute-start(bf16[512,128]{1,0:T(8,128)(2,1)S(1)} %pad_maximum_fusion.2), channel_id=1, source_target_pairs={{0,8},{4,12},{8,0},{12,4},{1,9},{5,13},{9,1},{13,5},{2,10},{6,14},... | collective-permute-start | bytes 393224 | tf_op jit(solution)/shard_map/ppermute | solution.py:144
  5.2 10.0 %collective-permute-start.3 = (bf16[512,128]{1,0:T(8,128)(2,1)S(1)}, bf16[512,128]{1,0:T(8,128)(2,1)S(1)}, u32[]{:S(2)}, u32[]{:S(2)}) collective-permute-start(bf16[512,128]{1,0:T(8,128)(2,1)S(1)} %pad_maximum_fusion.3), channel_id=1, source_target_pairs={{0,12},{4,8},{8,4},{12,0},{1,13},{5,9},{9,5},{13,1},{2,14},{6,10},... | collective-permute-start | bytes 393224 | tf_op jit(solution)/shard_map/ppermute | solution.py:144
  6.6 9.6 %collective-permute-start = (bf16[512,128]{1,0:T(8,128)(2,1)S(1)}, bf16[512,128]{1,0:T(8,128)(2,1)S(1)}, u32[]{:S(2)}, u32[]{:S(2)}) collective-permute-start(bf16[512,128]{1,0:T(8,128)(2,1)S(1)} %pad_maximum_fusion.1), channel_id=1, source_target_pairs={{0,4},{4,0},{8,12},{12,8},{1,5},{5,1},{9,13},{13,9},{2,6},{6,2},{1... | collective-permute-start | bytes 393224 | tf_op jit(solution)/shard_map/ppermute | solution.py:144
  8.5 12.7 %all-to-all-start = ((bf16[8,8,1280]{2,1,0:T(8,128)(2,1)}), bf16[8,8,1280]{2,1,0:T(8,128)(2,1)S(1)}, u32[]{:S(2)}, u32[]{:S(2)}) async-start(bf16[8,8,1280]{2,1,0:T(8,128)(2,1)} %bitcast.6), calls=%async_computation | async-start | bytes 327680 | tf_op jit(solution)/shard_map/all_to_all | solution.py:478
  13.7 3.6 %copy-start = (s32[1,64]{1,0:T(1,128)S(1)}, s32[1,64]{1,0:T(1,128)}, u32[]{:S(2)}) copy-start(s32[1,64]{1,0:T(1,128)} %visible_ref.1) | copy-start | bytes 772
  15.2 2.2 %collective-permute-start.4 = (bf16[512,128]{1,0:T(8,128)(2,1)S(1)}, bf16[512,128]{1,0:T(8,128)(2,1)S(1)}, u32[]{:S(2)}, u32[]{:S(2)}) collective-permute-start(bf16[512,128]{1,0:T(8,128)(2,1)S(1)} %get-tuple-element.15.refs_2_), channel_id=1, source_target_pairs={{0,1},{1,0},{2,3},{3,2},{4,5},{5,4},{6,7},{7,6},{8,9},{9,8},{10,11... | collective-permute-start | bytes 393224 | tf_op jit(solution)/shard_map/ppermute | solution.py:144
  15.2 2.2 %collective-permute-start.5 = (bf16[512,128]{1,0:T(8,128)(2,1)S(1)}, bf16[512,128]{1,0:T(8,128)(2,1)S(1)}, u32[]{:S(2)}, u32[]{:S(2)}) collective-permute-start(bf16[512,128]{1,0:T(8,128)(2,1)S(1)} %get-tuple-element.16.refs_4_), channel_id=1, source_target_pairs={{0,1},{1,0},{2,3},{3,2},{4,5},{5,4},{6,7},{7,6},{8,9},{9,8},{10,11... | collective-permute-start | bytes 393224 | tf_op jit(solution)/shard_map/ppermute | solution.py:144
  16.2 1.3 %collective-permute-start.1 = (bf16[512,128]{1,0:T(8,128)(2,1)S(1)}, bf16[512,128]{1,0:T(8,128)(2,1)S(1)}, u32[]{:S(2)}, u32[]{:S(2)}) collective-permute-start(bf16[512,128]{1,0:T(8,128)(2,1)S(1)} %collective-permute-done.refs_0_), channel_id=1, source_target_pairs={{0,1},{1,0},{2,3},{3,2},{4,5},{5,4},{6,7},{7,6},{8,9},{9,8},{10,11... | collective-permute-start | bytes 393224 | tf_op jit(solution)/shard_map/ppermute | solution.py:144
  23.4 11.0 %collective-permute-start.8 = (bf16[64,1024]{1,0:T(8,128)(2,1)S(1)}, bf16[64,1024]{1,0:T(8,128)(2,1)S(1)}, u32[]{:S(2)}, u32[]{:S(2)}) collective-permute-start(bf16[64,1024]{1,0:T(8,128)(2,1)S(1)} %get-tuple-element.17.x_ref), channel_id=1, source_target_pairs={{0,12},{4,8},{8,4},{12,0},{1,13},{5,9},{9,5},{13,1},{2,14},{6,10},... | collective-permute-start | bytes 393224 | tf_op jit(solution)/shard_map/ppermute | solution.py:144
  26.5 8.8 %collective-permute-start.7 = (bf16[64,1024]{1,0:T(8,128)(2,1)S(1)}, bf16[64,1024]{1,0:T(8,128)(2,1)S(1)}, u32[]{:S(2)}, u32[]{:S(2)}) collective-permute-start(bf16[64,1024]{1,0:T(8,128)(2,1)S(1)} %get-tuple-element.17.x_ref), channel_id=1, source_target_pairs={{0,4},{4,0},{8,12},{12,8},{1,5},{5,1},{9,13},{13,9},{2,6},{6,2},{1... | collective-permute-start | bytes 393224 | tf_op jit(solution)/shard_map/ppermute | solution.py:144
  26.7 9.8 %collective-permute-start.9 = (bf16[32,1024]{1,0:T(8,128)(2,1)S(1)}, bf16[32,1024]{1,0:T(8,128)(2,1)S(1)}, u32[]{:S(2)}, u32[]{:S(2)}) collective-permute-start(bf16[32,1024]{1,0:T(8,128)(2,1)S(1)} %get-tuple-element.24), channel_id=1, source_target_pairs={{0,8},{4,12},{8,0},{12,4},{1,9},{5,13},{9,1},{13,5},{2,10},{6,14},... | collective-permute-start | bytes 196616 | tf_op jit(solution)/shard_map/ppermute | solution.py:144
  32.6 5.9 %collective-permute-start.6 = (bf16[32,1024]{1,0:T(8,128)(2,1)S(1)}, bf16[32,1024]{1,0:T(8,128)(2,1)S(1)}, u32[]{:S(2)}, u32[]{:S(2)}) collective-permute-start(bf16[32,1024]{1,0:T(8,128)(2,1)S(1)} %get-tuple-element.19), channel_id=1, source_target_pairs={{0,8},{4,12},{8,0},{12,4},{1,9},{5,13},{9,1},{13,5},{2,10},{6,14},... | collective-permute-start | bytes 196616 | tf_op jit(solution)/shard_map/ppermute | solution.py:144
  37.3 5.0 %collective-permute-start.10 = (bf16[32,2048]{1,0:T(8,128)(2,1)S(1)}, bf16[32,2048]{1,0:T(8,128)(2,1)S(1)}, u32[]{:S(2)}, u32[]{:S(2)}) collective-permute-start(bf16[32,2048]{1,0:T(8,128)(2,1)S(1)} %project.7), channel_id=1, source_target_pairs={{0,2},{2,0},{1,3},{3,1},{4,6},{6,4},{5,7},{7,5},{8,10},{10,8},{9,1... | collective-permute-start | bytes 393224 | tf_op jit(solution)/shard_map/ppermute | solution.py:144

commit v5 on v4

--- a/solution.py
+++ b/solution.py
@@ -142,6 +142,12 @@
 
 def swap(array, axis, mask):
     return lax.ppermute(array, axis, [(i, i ^ mask) for i in range(lax.axis_size(axis))])
+
+
+def swap_by_core(array, mask):
+    count = 2 * lax.axis_size("seq")
+    pairs = [(i, i ^ (2 * (mask + i % 2))) for i in range(count)]
+    return lax.ppermute(array, ("seq", "rep"), pairs)
 
 
 def tile_at(index, width):
@@ -276,8 +282,8 @@
         finish(at, jnp.dot(x_ref[...], w_ref[:, at], preferred_element_type=jnp.float32))
 
 
-def attend_kernel(heads, masks, block_rows, rows_ref, lengths_ref, own_ref, *refs):
-    pieces = 2 * len(masks)
+def attend_kernel(heads, far_masks, block_rows, rows_ref, lengths_ref, own_ref, *refs):
+    pieces = 2 * len(far_masks) + 2
     piece_refs, weight_ref = refs[:pieces], refs[pieces]
     out_ref, theirs_ref, tile_ref, sems = refs[pieces + 1 :]
     seq, tp, rep = lax.axis_index("seq"), lax.axis_index("tp"), lax.axis_index("rep")
@@ -290,13 +296,18 @@
         half = block_rows // 2
         lane = lax.broadcasted_iota(jnp.int32, (1, half), 1)
         blocks = []
-        for core in range(2):
-            rows = slice(core * half, (core + 1) * half)
-            values = slice(block_rows + core * half, block_rows + (core + 1) * half)
-            blocks.append((own_ref, rows, values, seq * block_rows + core * half + lane))
-        for i, ref in enumerate(piece_refs):
-            mask, core = masks[i // 2], (rep if i % 2 == 0 else 1 - rep)
-            first = (seq ^ mask) * block_rows + core * half
+
+        def whole(ref, mask):
+            for first in (0, half):
+                rows, values = slice(first, first + half), slice(block_rows + first, block_rows + first + half)
+                blocks.append((ref, rows, values, (seq ^ mask) * block_rows + first + lane))
+
+        whole(own_ref, 0)
+        for i, ref in enumerate(piece_refs[:-2]):
+            core = rep if i % 2 == 0 else 1 - rep
+            whole(ref, far_masks[i // 2] + core)
+        for ref, core in zip(piece_refs[-2:], (rep, 1 - rep)):
+            first = (seq ^ 1) * block_rows + core * half
             blocks.append((ref, slice(0, half), slice(half, 2 * half), first + lane))
         width = heads * HEAD_WIDTH
         fresh_key = rows_ref[:, width : width + HEAD_WIDTH].astype(jnp.float32)
@@ -347,13 +358,13 @@
         copy.wait()
 
 
-def attend(heads, masks, query_rows, lengths, own, pieces, weight):
+def attend(heads, far_masks, query_rows, lengths, own, pieces, weight):
     tokens = query_rows.shape[0]
     block_rows = own.shape[0] // 2
-    work = tokens * heads * block_rows * (1 + len(masks))
+    work = tokens * heads * block_rows * 2 * (1 + len(far_masks))
     depth = heads * HEAD_WIDTH
     return pl.pallas_call(
-        functools.partial(attend_kernel, heads, masks, block_rows),
+        functools.partial(attend_kernel, heads, far_masks, block_rows),
         out_shape=[
             jax.ShapeDtypeStruct((tokens, depth), jnp.bfloat16),
             jax.ShapeDtypeStruct((tokens // 2, depth), jnp.bfloat16),
@@ -471,27 +482,23 @@
             ]
         )
 
-    pieces = [cut(rep * half_rows, half_rows, seq ^ mask) for mask in masks]
+    far_masks = masks[1::2]
+    far = [swap_by_core(cut(0, 2 * half_rows, seq ^ (m + rep)), m) for m in far_masks]
+    near = swap(cut(rep * half_rows, half_rows, seq ^ 1), "seq", 1)
     own = cut(0, 2 * half_rows, seq)
-    near = masks.index(1)
-    mine = [swap(piece, "seq", mask) for piece, mask in zip(pieces, masks)]
     query_rows = lax.all_to_all(
         pack_queries(rows, 1 + len(masks)), ("seq", "tp"), split_axis=0, concat_axis=0, tiled=True
     )
     lengths = spread_lengths(visible)
-    far = settle([piece for piece, mask in zip(mine, masks) if mask != 1], SETTLE_FIRST)
-    mine = [*far[:near], mine[near], *far[near:]]
-    other = [swap(piece, "rep", 1) for piece in mine]
-
-    pieces = [piece for pair in zip(mine, other) for piece in pair]
-    context, theirs, tile = attend(heads, masks, query_rows, lengths, own, pieces, out_weight)
+    far = settle(far, SETTLE_FIRST)
+    pieces = [piece for mine in (*far, near) for piece in (mine, swap(mine, "rep", 1))]
+    context, theirs, tile = attend(heads, far_masks, query_rows, lengths, own, pieces, out_weight)
 
     order = masks[-1:] + masks[:-1]
-    far = order[-1]
     chunks = [swap(context, "seq", mask) for mask in order[:-1]]
-    first = swap(theirs, "seq", far)
+    first = swap(theirs, "seq", order[-1])
     acc, ours, *tiles = load(out_weight, context, tile, order)
-    (second,) = settle([swap(ours, "seq", far)], SETTLE_LAST)
+    (second,) = settle([swap(ours, "seq", order[-1])], SETTLE_LAST)
     for chunk, tile in zip(chunks, tiles):
         acc = project(chunk, tile, acc)
     got = swap(project(first, tiles[-1], acc, 1, jnp.bfloat16), "tp", 1)

time: 43.3 us -> 42.8 us (0.988)
  starting transfers between devices: 18.6 us -> 17.3 us
  local copies, waits for them, and re-layouts: 2.03 us -> 2.83 us
    ppermute x0 -> x1, waiting for transfers between devices: none -> 5.24 us  [swap_by_core(): return lax.ppermute(array, ('seq', 'rep'), pairs)]
    ppermute x0 -> x1, starting transfers between devices: none -> 4.1 us  [swap_by_core(): return lax.ppermute(array, ('seq', 'rep'), pairs)]
    ppermute x11 -> x8, starting transfers between devices: 13.5 us -> 9.76 us  [swap(): lax.ppermute(array, axis, [(i, i ^ mask) for i in range(lax.axis_size(axi...]
    all_to_all x1, waiting for transfers between devices: 3.64 us -> 0.53 us  [shards_by_head(): lax.all_to_all(pack_queries(rows, 1 + len(masks)), ('seq', 'tp'), split_a...]
    ppermute x11 -> x8, waiting for transfers between devices: 5.89 us -> 3.74 us  [swap(): lax.ppermute(array, axis, [(i, i ^ mask) for i in range(lax.axis_size(axi...]
    all_to_all x1, starting transfers between devices: 5.12 us -> 3.39 us  [shards_by_head(): lax.all_to_all(pack_queries(rows, 1 + len(masks)), ('seq', 'tp'), split_a...]
    dynamic_slice x2 -> x3, local copies, waits for them, and re-layouts: 2.02 us -> 2.83 us  [cut(): lax.dynamic_slice(table, (first, head * HEAD_WIDTH), (count, HEAD_WIDTH))]
  transfers between devices with their start and end apart: 12 -> 10, of which waited for: 7 -> 5; matrix products, arithmetic and copies ran while one was open for 2% -> 4% of each run, Pallas kernels for 23% -> 23%
where the time goes in v5:
time: 42.8 us; the launch traced here: 42.4 us
  starting transfers between devices  17.3 us (40%)
  Pallas kernels  12.7 us (30%)
  waiting for transfers between devices  9.5 us (22%)
  local copies, waits for them, and re-layouts  2.83 us (7%)
    ppermute x8, starting transfers between devices, swap(): lax.ppermute(array, axis, [(i, i ^ mask) for i in range(lax.axis_size(axi...  9.76 us
    ppermute x1, waiting for transfers between devices, swap_by_core(): return lax.ppermute(array, ('seq', 'rep'), pairs)  5.24 us
    pallas_call x1, Pallas kernels, load(): pl.pallas_call(functools.partial(load_kernel, masks), out_shape=[jax.Shap...  4.71 us
    ppermute x1, starting transfers between devices, swap_by_core(): return lax.ppermute(array, ('seq', 'rep'), pairs)  4.1 us
    ppermute x8, waiting for transfers between devices, swap(): lax.ppermute(array, axis, [(i, i ^ mask) for i in range(lax.axis_size(axi...  3.74 us
    all_to_all x1, starting transfers between devices, shards_by_head(): lax.all_to_all(pack_queries(rows, 1 + len(masks)), ('seq', 'tp'), split_a...  3.39 us
    pallas_call x4, Pallas kernels, project(): pl.pallas_call(functools.partial(project_kernel, side), out_shape=jax.Sha...  3.35 us
    dynamic_slice x3, local copies, waits for them, and re-layouts, cut(): lax.dynamic_slice(table, (first, head * HEAD_WIDTH), (count, HEAD_WIDTH))  2.83 us
  transfers between devices with their start and end apart: 10, of which 5 were waited for; matrix products, arithmetic and copies ran while one was open for 4% of the time, Pallas kernels for 23%

profile of v5, /device:TPU:0, one launch (start us, length us, event | category | flops | bytes accessed | tf_op | source)
XLA Modules:
  0.0 42.4 jit_solution(10916559097502146537)
XLA Ops:
  0.0 1.1 %constant_dynamic-slice_fusion = (bf16[512,128]{1,0:T(8,128)(2,1)S(1)}, bf16[512,128]{1,0:T(8,128)(2,1)S(1)}, bf16[512,128]{1,0:T(8,128)(2,1)S(1)}, bf16[512,128]{1,0:T(8,128)(2,1)S(1)}) fusion(bf16[512,512]{1,0:T(8,128)(2,1)} %param.12, s32[]{:T(128)S(6)} %select_n.17, s32[]{:T(128)S(6)} %select_n.16, bf16[512,512]{1,0:T(8,128)(2,1)} %param.11), kind=kLoop, calls=%fused_computation.3 | loop fusion | bytes 1048584 | tf_op jit(solution)/shard_map/dynamic_slice | solution.py:480
  1.2 4.1 %collective-permute-start = (bf16[1024,128]{1,0:T(8,128)(2,1)S(1)}, bf16[1024,128]{1,0:T(8,128)(2,1)S(1)}, u32[]{:S(2)}, u32[]{:S(2)}) collective-permute-start(bf16[1024,128]{1,0:T(8,128)(2,1)S(1)} %pad_maximum_fusion.1), channel_id=1, source_target_pairs={{0,8},{1,13},{4,12},{5,9},{8,0},{9,5},{12,4},{13,1},{2,10},{3,15},... | collective-permute-start | bytes 786440 | tf_op jit(solution)/shard_map/ppermute | solution.py:150
  5.3 0.8 %dynamic_slice.22 = bf16[256,128]{1,0:T(8,128)(2,1)S(1)} dynamic-slice(bf16[512,512]{1,0:T(8,128)(2,1)} %param.11, s32[]{:T(128)S(6)} %select_n.18, s32[]{:T(128)S(6)} %select_n.19), dynamic_slice_sizes={256,128} | dynamic-slice | bytes 131076 | tf_op jit(solution)/shard_map/dynamic_slice | solution.py:480
  6.1 0.8 %dynamic_slice.23 = bf16[256,128]{1,0:T(8,128)(2,1)S(1)} dynamic-slice(bf16[512,512]{1,0:T(8,128)(2,1)} %param.12, s32[]{:T(128)S(6)} %select_n.18, s32[]{:T(128)S(6)} %select_n.19), dynamic_slice_sizes={256,128} | dynamic-slice | bytes 131076 | tf_op jit(solution)/shard_map/dynamic_slice | solution.py:480
  7.0 1.6 %collective-permute-start.2 = (bf16[512,128]{1,0:T(8,128)(2,1)S(1)}, bf16[512,128]{1,0:T(8,128)(2,1)S(1)}, u32[]{:S(2)}, u32[]{:S(2)}) collective-permute-start(bf16[512,128]{1,0:T(8,128)(2,1)S(1)} %pad_maximum_fusion.2), channel_id=1, source_target_pairs={{0,4},{4,0},{8,12},{12,8},{1,5},{5,1},{9,13},{13,9},{2,6},{6,2},{1... | collective-permute-start | bytes 393224 | tf_op jit(solution)/shard_map/ppermute | solution.py:144
  8.6 1.6 %pack_queries.1 = bf16[64,1280]{1,0:T(8,128)(2,1)} custom-call(bf16[8,8192]{1,0:T(8,128)(2,1)} %bitcast.7, bf16[8,1024]{1,0:T(8,128)(2,1)} %bitcast.8, bf16[8,1024]{1,0:T(8,128)(2,1)} %bitcast.9), custom_call_target="tpu_custom_call" | custom-call | bytes 524288 | tf_op jit(solution)/shard_map/pack_queries/pallas_call | solution.py:205
  10.2 3.4 %all-to-all-start = ((bf16[8,8,1280]{2,1,0:T(8,128)(2,1)}), bf16[8,8,1280]{2,1,0:T(8,128)(2,1)S(1)}, u32[]{:S(2)}, u32[]{:S(2)}) async-start(bf16[8,8,1280]{2,1,0:T(8,128)(2,1)} %bitcast.6), calls=%async_computation | async-start | bytes 327680 | tf_op jit(solution)/shard_map/all_to_all | solution.py:489
  13.6 5.2 %collective-permute-done.refs_0_ = bf16[1024,128]{1,0:T(8,128)(2,1)S(1)} collective-permute-done((bf16[1024,128]{1,0:T(8,128)(2,1)S(1)}, bf16[1024,128]{1,0:T(8,128)(2,1)S(1)}, u32[]{:S(2)}, u32[]{:S(2)}) %collective-permute-start) | collective-permute-done | bytes 262176 | tf_op jit(solution)/shard_map/ppermute | solution.py:150
  18.9 0.5 %collective-permute-start.3 = (bf16[512,128]{1,0:T(8,128)(2,1)S(1)}, bf16[512,128]{1,0:T(8,128)(2,1)S(1)}, u32[]{:S(2)}, u32[]{:S(2)}) collective-permute-start(bf16[512,128]{1,0:T(8,128)(2,1)S(1)} %collective-permute-done.2.refs_2_), channel_id=1, source_target_pairs={{0,1},{1,0},{2,3},{3,2},{4,5},{5,4},{6,7},{7,6},{8,9},{9,8},{10,11... | collective-permute-start | bytes 393224 | tf_op jit(solution)/shard_map/ppermute | solution.py:144
  19.5 1.1 %collective-permute-done.3.refs_3_ = bf16[512,128]{1,0:T(8,128)(2,1)S(1)} collective-permute-done((bf16[512,128]{1,0:T(8,128)(2,1)S(1)}, bf16[512,128]{1,0:T(8,128)(2,1)S(1)}, u32[]{:S(2)}, u32[]{:S(2)}) %collective-permute-start.3) | collective-permute-done | bytes 131104 | tf_op jit(solution)/shard_map/ppermute | solution.py:144
  20.6 0.5 %all-to-all-done = bf16[8,8,1280]{2,1,0:T(8,128)(2,1)S(1)} async-done(((bf16[8,8,1280]{2,1,0:T(8,128)(2,1)}), bf16[8,8,1280]{2,1,0:T(8,128)(2,1)S(1)}, u32[]{:S(2)}, u32[]{:S(2)}) %all-to-all-start) | async-done | bytes 163872 | tf_op jit(solution)/shard_map/all_to_all | solution.py:489
  21.1 2.2 %attend.1 = (bf16[64,1024]{1,0:T(8,128)(2,1)S(1)}, bf16[32,1024]{1,0:T(8,128)(2,1)S(1)}, bf16[1024,2048]{1,0:T(8,128)(2,1)S(1)}) custom-call(bf16[64,1280]{1,0:T(8,128)(2,1)S(1)} %bitcast.5, s32[64,128]{1,0:T(8,128)S(1)} %spread_lengths.1.lengths_ref, bf16[1024,128]{1,0:T(8,128)(2,1)S(1)} %pad_maximum_fusion.own_ref, bf16[1024,128]{1,0:T(8,128)(2,1)S(1)} %settle.2.refs_0_, ...), custom_call_target="tpu_custom_call" | custom-call | flops 805306368 | bytes 1048576 | tf_op jit(solution)/shard_map/attend/pallas_call | solution.py:366
  23.4 3.1 %collective-permute-start.6 = (bf16[64,1024]{1,0:T(8,128)(2,1)S(1)}, bf16[64,1024]{1,0:T(8,128)(2,1)S(1)}, u32[]{:S(2)}, u32[]{:S(2)}) collective-permute-start(bf16[64,1024]{1,0:T(8,128)(2,1)S(1)} %get-tuple-element.13.x_ref), channel_id=1, source_target_pairs={{0,12},{4,8},{8,4},{12,0},{1,13},{5,9},{9,5},{13,1},{2,14},{6,10},... | collective-permute-start | bytes 393224 | tf_op jit(solution)/shard_map/ppermute | solution.py:144
  26.5 1.3 %collective-permute-start.7 = (bf16[32,1024]{1,0:T(8,128)(2,1)S(1)}, bf16[32,1024]{1,0:T(8,128)(2,1)S(1)}, u32[]{:S(2)}, u32[]{:S(2)}) collective-permute-start(bf16[32,1024]{1,0:T(8,128)(2,1)S(1)} %get-tuple-element.20), channel_id=1, source_target_pairs={{0,8},{4,12},{8,0},{12,4},{1,9},{5,13},{9,1},{13,5},{2,10},{6,14},... | collective-permute-start | bytes 196616 | tf_op jit(solution)/shard_map/ppermute | solution.py:144
  27.8 4.7 %load.1 = (f32[64,2048]{1,0:T(8,128)S(1)}, bf16[32,1024]{1,0:T(8,128)(2,1)S(1)}, bf16[1024,2048]{1,0:T(8,128)(2,1)S(1)}, bf16[1024,2048]{1,0:T(8,128)(2,1)S(1)}, bf16[1024,2048]{1,0:T(8,128)(2,1)S(1)}) custom-call(bf16[4096,2048]{1,0:T(8,128)(2,1)} %weight_ref.1, bf16[64,1024]{1,0:T(8,128)(2,1)S(1)} %get-tuple-element.13.x_ref, ...), custom_call_target="tpu_custom_call" | custom-call | flops 268435456 | bytes 12582912 | tf_op jit(solution)/shard_map/load/pallas_call | solution.py:403
  32.5 1.7 %collective-permute-start.4 = (bf16[32,1024]{1,0:T(8,128)(2,1)S(1)}, bf16[32,1024]{1,0:T(8,128)(2,1)S(1)}, u32[]{:S(2)}, u32[]{:S(2)}) collective-permute-start(bf16[32,1024]{1,0:T(8,128)(2,1)S(1)} %get-tuple-element.15), channel_id=1, source_target_pairs={{0,8},{4,12},{8,0},{12,4},{1,9},{5,13},{9,1},{13,5},{2,10},{6,14},... | collective-permute-start | bytes 196616 | tf_op jit(solution)/shard_map/ppermute | solution.py:144
  34.2 0.8 %project.4.acc_ref = f32[64,2048]{1,0:T(8,128)S(1)} custom-call(bf16[64,1024]{1,0:T(8,128)(2,1)S(1)} %collective-permute-done.6.x_ref, bf16[1024,2048]{1,0:T(8,128)(2,1)S(1)} %get-tuple-element.18.w_ref, f32[64,2048]{1,0:T(8,128)S(1)} %get-tuple-element.19.acc_ref), custom_call_target="tpu_custom_call" | custom-call | flops 268435456 | bytes 4194304 | tf_op jit(solution)/shard_map/project/pallas_call | solution.py:433
  35.1 0.8 %project.5.acc_ref = f32[64,2048]{1,0:T(8,128)S(1)} custom-call(bf16[64,1024]{1,0:T(8,128)(2,1)S(1)} %collective-permute-done.5.x_ref, bf16[1024,2048]{1,0:T(8,128)(2,1)S(1)} %get-tuple-element.17.w_ref, f32[64,2048]{1,0:T(8,128)S(1)} %project.4.acc_ref), custom_call_target="tpu_custom_call" | custom-call | flops 268435456 | bytes 4194304 | tf_op jit(solution)/shard_map/project/pallas_call | solution.py:433
  35.9 0.8 %project.7 = bf16[32,2048]{1,0:T(8,128)(2,1)S(1)} custom-call(bf16[32,1024]{1,0:T(8,128)(2,1)S(1)} %collective-permute-done.7.x_ref, bf16[1024,2048]{1,0:T(8,128)(2,1)S(1)} %get-tuple-element.16.w_ref, f32[64,2048]{1,0:T(8,128)S(1)} %project.5.acc_ref), custom_call_target="tpu_custom_call" | custom-call | flops 134217728 | bytes 4194304 | tf_op jit(solution)/shard_map/project/pallas_call | solution.py:433
  36.8 1.5 %collective-permute-start.8 = (bf16[32,2048]{1,0:T(8,128)(2,1)S(1)}, bf16[32,2048]{1,0:T(8,128)(2,1)S(1)}, u32[]{:S(2)}, u32[]{:S(2)}) collective-permute-start(bf16[32,2048]{1,0:T(8,128)(2,1)S(1)} %project.7), channel_id=1, source_target_pairs={{0,2},{2,0},{1,3},{3,1},{4,6},{6,4},{5,7},{7,5},{8,10},{10,8},{9,1... | collective-permute-start | bytes 393224 | tf_op jit(solution)/shard_map/ppermute | solution.py:144
  38.3 0.2 collective-permute-done.4.refs_0_
  38.5 0.8 %project.6.refs_0_ = f32[32,2048]{1,0:T(8,128)S(1)} custom-call(bf16[32,1024]{1,0:T(8,128)(2,1)S(1)} %settle.3.x_ref, bf16[1024,2048]{1,0:T(8,128)(2,1)S(1)} %get-tuple-element.16.w_ref, f32[64,2048]{1,0:T(8,128)S(1)} %project.5.acc_ref), custom_call_target="tpu_custom_call" | custom-call | flops 134217728 | bytes 4194304 | tf_op jit(solution)/shard_map/project/pallas_call | solution.py:433
  39.3 2.4 %collective-permute-done.8.refs_1_ = bf16[32,2048]{1,0:T(8,128)(2,1)S(1)} collective-permute-done((bf16[32,2048]{1,0:T(8,128)(2,1)S(1)}, bf16[32,2048]{1,0:T(8,128)(2,1)S(1)}, u32[]{:S(2)}, u32[]{:S(2)}) %collective-permute-start.8) | collective-permute-done | bytes 131104 | tf_op jit(solution)/shard_map/ppermute | solution.py:144
  41.7 0.7 %add.21 = bf16[1,32,2048]{2,1,0:T(8,128)(2,1)} custom-call(f32[32,2048]{1,0:T(8,128)S(1)} %project.6.refs_0_, bf16[32,2048]{1,0:T(8,128)(2,1)S(1)} %collective-permute-done.8.refs_1_), custom_call_target="tpu_custom_call" | custom-call | bytes 524288 | tf_op jit(solution)/shard_map/add/pallas_call | solution.py:457
  (15 shorter events, 0.2 us)
Async XLA Ops:
  1.2 17.7 %collective-permute-start = (bf16[1024,128]{1,0:T(8,128)(2,1)S(1)}, bf16[1024,128]{1,0:T(8,128)(2,1)S(1)}, u32[]{:S(2)}, u32[]{:S(2)}) collective-permute-start(bf16[1024,128]{1,0:T(8,128)(2,1)S(1)} %pad_maximum_fusion.1), channel_id=1, source_target_pairs={{0,8},{1,13},{4,12},{5,9},{8,0},{9,5},{12,4},{13,1},{2,10},{3,15},... | collective-permute-start | bytes 786440 | tf_op jit(solution)/shard_map/ppermute | solution.py:150
  7.0 11.9 %collective-permute-start.2 = (bf16[512,128]{1,0:T(8,128)(2,1)S(1)}, bf16[512,128]{1,0:T(8,128)(2,1)S(1)}, u32[]{:S(2)}, u32[]{:S(2)}) collective-permute-start(bf16[512,128]{1,0:T(8,128)(2,1)S(1)} %pad_maximum_fusion.2), channel_id=1, source_target_pairs={{0,4},{4,0},{8,12},{12,8},{1,5},{5,1},{9,13},{13,9},{2,6},{6,2},{1... | collective-permute-start | bytes 393224 | tf_op jit(solution)/shard_map/ppermute | solution.py:144
  10.2 10.9 %all-to-all-start = ((bf16[8,8,1280]{2,1,0:T(8,128)(2,1)}), bf16[8,8,1280]{2,1,0:T(8,128)(2,1)S(1)}, u32[]{:S(2)}, u32[]{:S(2)}) async-start(bf16[8,8,1280]{2,1,0:T(8,128)(2,1)} %bitcast.6), calls=%async_computation | async-start | bytes 327680 | tf_op jit(solution)/shard_map/all_to_all | solution.py:489
  13.6 5.8 %copy-start = (s32[1,64]{1,0:T(1,128)S(1)}, s32[1,64]{1,0:T(1,128)}, u32[]{:S(2)}) copy-start(s32[1,64]{1,0:T(1,128)} %visible_ref.1) | copy-start | bytes 772
  18.9 2.3 %collective-permute-start.1 = (bf16[1024,128]{1,0:T(8,128)(2,1)S(1)}, bf16[1024,128]{1,0:T(8,128)(2,1)S(1)}, u32[]{:S(2)}, u32[]{:S(2)}) collective-permute-start(bf16[1024,128]{1,0:T(8,128)(2,1)S(1)} %settle.2.refs_0_), channel_id=1, source_target_pairs={{0,1},{1,0},{2,3},{3,2},{4,5},{5,4},{6,7},{7,6},{8,9},{9,8},{10,11... | collective-permute-start | bytes 786440 | tf_op jit(solution)/shard_map/ppermute | solution.py:144
  18.9 1.7 %collective-permute-start.3 = (bf16[512,128]{1,0:T(8,128)(2,1)S(1)}, bf16[512,128]{1,0:T(8,128)(2,1)S(1)}, u32[]{:S(2)}, u32[]{:S(2)}) collective-permute-start(bf16[512,128]{1,0:T(8,128)(2,1)S(1)} %collective-permute-done.2.refs_2_), channel_id=1, source_target_pairs={{0,1},{1,0},{2,3},{3,2},{4,5},{5,4},{6,7},{7,6},{8,9},{9,8},{10,11... | collective-permute-start | bytes 393224 | tf_op jit(solution)/shard_map/ppermute | solution.py:144
  23.4 10.8 %collective-permute-start.6 = (bf16[64,1024]{1,0:T(8,128)(2,1)S(1)}, bf16[64,1024]{1,0:T(8,128)(2,1)S(1)}, u32[]{:S(2)}, u32[]{:S(2)}) collective-permute-start(bf16[64,1024]{1,0:T(8,128)(2,1)S(1)} %get-tuple-element.13.x_ref), channel_id=1, source_target_pairs={{0,12},{4,8},{8,4},{12,0},{1,13},{5,9},{9,5},{13,1},{2,14},{6,10},... | collective-permute-start | bytes 393224 | tf_op jit(solution)/shard_map/ppermute | solution.py:144
  26.5 8.6 %collective-permute-start.5 = (bf16[64,1024]{1,0:T(8,128)(2,1)S(1)}, bf16[64,1024]{1,0:T(8,128)(2,1)S(1)}, u32[]{:S(2)}, u32[]{:S(2)}) collective-permute-start(bf16[64,1024]{1,0:T(8,128)(2,1)S(1)} %get-tuple-element.13.x_ref), channel_id=1, source_target_pairs={{0,4},{4,0},{8,12},{12,8},{1,5},{5,1},{9,13},{13,9},{2,6},{6,2},{1... | collective-permute-start | bytes 393224 | tf_op jit(solution)/shard_map/ppermute | solution.py:144
  26.5 9.4 %collective-permute-start.7 = (bf16[32,1024]{1,0:T(8,128)(2,1)S(1)}, bf16[32,1024]{1,0:T(8,128)(2,1)S(1)}, u32[]{:S(2)}, u32[]{:S(2)}) collective-permute-start(bf16[32,1024]{1,0:T(8,128)(2,1)S(1)} %get-tuple-element.20), channel_id=1, source_target_pairs={{0,8},{4,12},{8,0},{12,4},{1,9},{5,13},{9,1},{13,5},{2,10},{6,14},... | collective-permute-start | bytes 196616 | tf_op jit(solution)/shard_map/ppermute | solution.py:144
  32.5 5.9 %collective-permute-start.4 = (bf16[32,1024]{1,0:T(8,128)(2,1)S(1)}, bf16[32,1024]{1,0:T(8,128)(2,1)S(1)}, u32[]{:S(2)}, u32[]{:S(2)}) collective-permute-start(bf16[32,1024]{1,0:T(8,128)(2,1)S(1)} %get-tuple-element.15), channel_id=1, source_target_pairs={{0,8},{4,12},{8,0},{12,4},{1,9},{5,13},{9,1},{13,5},{2,10},{6,14},... | collective-permute-start | bytes 196616 | tf_op jit(solution)/shard_map/ppermute | solution.py:144
  36.8 5.0 %collective-permute-start.8 = (bf16[32,2048]{1,0:T(8,128)(2,1)S(1)}, bf16[32,2048]{1,0:T(8,128)(2,1)S(1)}, u32[]{:S(2)}, u32[]{:S(2)}) collective-permute-start(bf16[32,2048]{1,0:T(8,128)(2,1)S(1)} %project.7), channel_id=1, source_target_pairs={{0,2},{2,0},{1,3},{3,1},{4,6},{6,4},{5,7},{7,5},{8,10},{10,8},{9,1... | collective-permute-start | bytes 393224 | tf_op jit(solution)/shard_map/ppermute | solution.py:144

commit v6 on v5

--- a/solution.py
+++ b/solution.py
@@ -379,13 +379,12 @@
     )(query_rows, lengths, own, *pieces, weight)
 
 
-def load_kernel(masks, weight_ref, x_ref, first_ref, acc_ref, ours_ref, *refs):
+def load_kernel(masks, weight_ref, x_ref, first_ref, acc_ref, *refs):
     tile_refs, sems = refs[:-1], refs[-1]
     tp = lax.axis_index("tp")
     copies = tile_copies(masks, weight_ref, tile_refs, sems)
     for copy in copies:
         copy.start()
-    ours_ref[...] = half_of(x_ref[...], tp)
 
     def finish(at, part):
         acc_ref[:, at] = part
@@ -404,11 +403,10 @@
         functools.partial(load_kernel, masks),
         out_shape=[
             jax.ShapeDtypeStruct((tokens, columns), jnp.float32),
-            jax.ShapeDtypeStruct((tokens // 2, depth), jnp.bfloat16),
         ]
         + [jax.ShapeDtypeStruct(tile.shape, tile.dtype)] * len(masks),
         in_specs=[hbm(), vmem(), vmem()],
-        out_specs=[vmem()] * (2 + len(masks)),
+        out_specs=[vmem()] * (1 + len(masks)),
         scratch_shapes=[pltpu.SemaphoreType.DMA((FETCHES * len(masks),))],
         compiler_params=params(LOAD_BYTES),
         cost_estimate=cost(2 * tokens * depth * columns, len(masks) * depth * columns * 2),
@@ -416,8 +414,12 @@
     )(weight, context, tile)
 
 
-def project_kernel(side, x_ref, w_ref, acc_ref, out_ref):
+def project_kernel(side, pass_on, x_ref, w_ref, acc_ref, *refs):
     tp = lax.axis_index("tp")
+    out_ref = refs[-1]
+    if pass_on:
+        out_ref = refs[1]
+        refs[2][...] = half_of(refs[0][...], tp)
 
     def finish(at, part):
         acc = acc_ref[:, at]
@@ -428,17 +430,22 @@
     multiply(x_ref, w_ref, finish)
 
 
-def project(context, tile, acc, side=None, dtype=jnp.float32):
+def project(context, tile, acc, side=None, dtype=jnp.float32, pass_on=None):
     tokens, columns = context.shape[0], tile.shape[1]
-    return pl.pallas_call(
-        functools.partial(project_kernel, side),
-        out_shape=jax.ShapeDtypeStruct((tokens, columns), dtype),
-        in_specs=[vmem()] * 3,
-        out_specs=vmem(),
+    shapes = [jax.ShapeDtypeStruct((tokens, columns), dtype)]
+    operands = [context, tile, acc]
+    if pass_on is not None:
+        operands.append(pass_on)
+        shapes.append(jax.ShapeDtypeStruct((tokens // 2, pass_on.shape[1]), pass_on.dtype))
+    return pl.pallas_call(
+        functools.partial(project_kernel, side, pass_on is not None),
+        out_shape=shapes,
+        in_specs=[vmem()] * len(operands),
+        out_specs=[vmem()] * len(shapes),
         compiler_params=params(PROJECT_BYTES),
         cost_estimate=cost(2 * context.size * columns, 2 * tile.size),
         name="project",
-    )(context, tile, acc)
+    )(*operands)
 
 
 def add_kernel(*refs):
@@ -497,12 +504,15 @@
     order = masks[-1:] + masks[:-1]
     chunks = [swap(context, "seq", mask) for mask in order[:-1]]
     first = swap(theirs, "seq", order[-1])
-    acc, ours, *tiles = load(out_weight, context, tile, order)
-    (second,) = settle([swap(ours, "seq", order[-1])], SETTLE_LAST)
-    for chunk, tile in zip(chunks, tiles):
-        acc = project(chunk, tile, acc)
-    got = swap(project(first, tiles[-1], acc, 1, jnp.bfloat16), "tp", 1)
-    return add([project(second, tiles[-1], acc, 0)], [got])
+    acc, *tiles = load(out_weight, context, tile, order)
+    for i, (chunk, tile) in enumerate(zip(chunks, tiles)):
+        acc, *ours = project(chunk, tile, acc, pass_on=context if i == 0 else None)
+        if i == 0:
+            (second,) = settle([swap(ours[0], "seq", order[-1])], SETTLE_LAST)
+    (sums,) = project(first, tiles[-1], acc, 1, jnp.bfloat16)
+    got = swap(sums, "tp", 1)
+    (kept,) = project(second, tiles[-1], acc, 0)
+    return add([kept], [got])
 
 
 def solution(mesh):

time: 42.8 us -> 42.7 us (level)
  no operation moved by 1% of the time
where the time goes in v6:
time: 42.7 us; the launch traced here: 42.4 us
  starting transfers between devices  17.3 us (41%)
  Pallas kernels  12.6 us (30%)
  waiting for transfers between devices  9.5 us (22%)
  local copies, waits for them, and re-layouts  2.83 us (7%)
    ppermute x8, starting transfers between devices, swap(): lax.ppermute(array, axis, [(i, i ^ mask) for i in range(lax.axis_size(axi...  9.77 us
    ppermute x1, waiting for transfers between devices, swap_by_core(): return lax.ppermute(array, ('seq', 'rep'), pairs)  5.24 us
    pallas_call x1, Pallas kernels, load(): pl.pallas_call(functools.partial(load_kernel, masks), out_shape=[jax.Shap...  4.71 us
    ppermute x1, starting transfers between devices, swap_by_core(): return lax.ppermute(array, ('seq', 'rep'), pairs)  4.1 us
    ppermute x8, waiting for transfers between devices, swap(): lax.ppermute(array, axis, [(i, i ^ mask) for i in range(lax.axis_size(axi...  3.73 us
    all_to_all x1, starting transfers between devices, shards_by_head(): lax.all_to_all(pack_queries(rows, 1 + len(masks)), ('seq', 'tp'), split_a...  3.39 us
    pallas_call x4, Pallas kernels, project(): pl.pallas_call(functools.partial(project_kernel, side, pass_on is not Non...  3.35 us
    dynamic_slice x3, local copies, waits for them, and re-layouts, cut(): lax.dynamic_slice(table, (first, head * HEAD_WIDTH), (count, HEAD_WIDTH))  2.83 us
  transfers between devices with their start and end apart: 10, of which 5 were waited for; matrix products, arithmetic and copies ran while one was open for 4% of the time, Pallas kernels for 23%

profile of v6, /device:TPU:0, one launch (start us, length us, event | category | flops | bytes accessed | tf_op | source)
XLA Modules:
  0.0 42.4 jit_solution(15185538058985837460)
XLA Ops:
  0.0 1.1 %constant_dynamic-slice_fusion = (bf16[512,128]{1,0:T(8,128)(2,1)S(1)}, bf16[512,128]{1,0:T(8,128)(2,1)S(1)}, bf16[512,128]{1,0:T(8,128)(2,1)S(1)}, bf16[512,128]{1,0:T(8,128)(2,1)S(1)}) fusion(bf16[512,512]{1,0:T(8,128)(2,1)} %param.12, s32[]{:T(128)S(6)} %select_n.17, s32[]{:T(128)S(6)} %select_n.16, bf16[512,512]{1,0:T(8,128)(2,1)} %param.11), kind=kLoop, calls=%fused_computation.3 | loop fusion | bytes 1048584 | tf_op jit(solution)/shard_map/dynamic_slice | solution.py:487
  1.2 4.1 %collective-permute-start = (bf16[1024,128]{1,0:T(8,128)(2,1)S(1)}, bf16[1024,128]{1,0:T(8,128)(2,1)S(1)}, u32[]{:S(2)}, u32[]{:S(2)}) collective-permute-start(bf16[1024,128]{1,0:T(8,128)(2,1)S(1)} %pad_maximum_fusion.1), channel_id=1, source_target_pairs={{0,8},{1,13},{4,12},{5,9},{8,0},{9,5},{12,4},{13,1},{2,10},{3,15},... | collective-permute-start | bytes 786440 | tf_op jit(solution)/shard_map/ppermute | solution.py:150
  5.3 0.8 %dynamic_slice.22 = bf16[256,128]{1,0:T(8,128)(2,1)S(1)} dynamic-slice(bf16[512,512]{1,0:T(8,128)(2,1)} %param.11, s32[]{:T(128)S(6)} %select_n.18, s32[]{:T(128)S(6)} %select_n.19), dynamic_slice_sizes={256,128} | dynamic-slice | bytes 131076 | tf_op jit(solution)/shard_map/dynamic_slice | solution.py:487
  6.1 0.8 %dynamic_slice.23 = bf16[256,128]{1,0:T(8,128)(2,1)S(1)} dynamic-slice(bf16[512,512]{1,0:T(8,128)(2,1)} %param.12, s32[]{:T(128)S(6)} %select_n.18, s32[]{:T(128)S(6)} %select_n.19), dynamic_slice_sizes={256,128} | dynamic-slice | bytes 131076 | tf_op jit(solution)/shard_map/dynamic_slice | solution.py:487
  7.0 1.6 %collective-permute-start.2 = (bf16[512,128]{1,0:T(8,128)(2,1)S(1)}, bf16[512,128]{1,0:T(8,128)(2,1)S(1)}, u32[]{:S(2)}, u32[]{:S(2)}) collective-permute-start(bf16[512,128]{1,0:T(8,128)(2,1)S(1)} %pad_maximum_fusion.2), channel_id=1, source_target_pairs={{0,4},{4,0},{8,12},{12,8},{1,5},{5,1},{9,13},{13,9},{2,6},{6,2},{1... | collective-permute-start | bytes 393224 | tf_op jit(solution)/shard_map/ppermute | solution.py:144
  8.6 1.6 %pack_queries.1 = bf16[64,1280]{1,0:T(8,128)(2,1)} custom-call(bf16[8,8192]{1,0:T(8,128)(2,1)} %bitcast.7, bf16[8,1024]{1,0:T(8,128)(2,1)} %bitcast.8, bf16[8,1024]{1,0:T(8,128)(2,1)} %bitcast.9), custom_call_target="tpu_custom_call" | custom-call | bytes 524288 | tf_op jit(solution)/shard_map/pack_queries/pallas_call | solution.py:205
  10.2 3.4 %all-to-all-start = ((bf16[8,8,1280]{2,1,0:T(8,128)(2,1)}), bf16[8,8,1280]{2,1,0:T(8,128)(2,1)S(1)}, u32[]{:S(2)}, u32[]{:S(2)}) async-start(bf16[8,8,1280]{2,1,0:T(8,128)(2,1)} %bitcast.6), calls=%async_computation | async-start | bytes 327680 | tf_op jit(solution)/shard_map/all_to_all | solution.py:496
  13.6 5.2 %collective-permute-done.refs_0_ = bf16[1024,128]{1,0:T(8,128)(2,1)S(1)} collective-permute-done((bf16[1024,128]{1,0:T(8,128)(2,1)S(1)}, bf16[1024,128]{1,0:T(8,128)(2,1)S(1)}, u32[]{:S(2)}, u32[]{:S(2)}) %collective-permute-start) | collective-permute-done | bytes 262176 | tf_op jit(solution)/shard_map/ppermute | solution.py:150
  18.9 0.5 %collective-permute-start.3 = (bf16[512,128]{1,0:T(8,128)(2,1)S(1)}, bf16[512,128]{1,0:T(8,128)(2,1)S(1)}, u32[]{:S(2)}, u32[]{:S(2)}) collective-permute-start(bf16[512,128]{1,0:T(8,128)(2,1)S(1)} %collective-permute-done.2.refs_2_), channel_id=1, source_target_pairs={{0,1},{1,0},{2,3},{3,2},{4,5},{5,4},{6,7},{7,6},{8,9},{9,8},{10,11... | collective-permute-start | bytes 393224 | tf_op jit(solution)/shard_map/ppermute | solution.py:144
  19.5 1.1 %collective-permute-done.3.refs_3_ = bf16[512,128]{1,0:T(8,128)(2,1)S(1)} collective-permute-done((bf16[512,128]{1,0:T(8,128)(2,1)S(1)}, bf16[512,128]{1,0:T(8,128)(2,1)S(1)}, u32[]{:S(2)}, u32[]{:S(2)}) %collective-permute-start.3) | collective-permute-done | bytes 131104 | tf_op jit(solution)/shard_map/ppermute | solution.py:144
  20.6 0.5 %all-to-all-done = bf16[8,8,1280]{2,1,0:T(8,128)(2,1)S(1)} async-done(((bf16[8,8,1280]{2,1,0:T(8,128)(2,1)}), bf16[8,8,1280]{2,1,0:T(8,128)(2,1)S(1)}, u32[]{:S(2)}, u32[]{:S(2)}) %all-to-all-start) | async-done | bytes 163872 | tf_op jit(solution)/shard_map/all_to_all | solution.py:496
  21.1 2.2 %attend.1 = (bf16[64,1024]{1,0:T(8,128)(2,1)S(1)}, bf16[32,1024]{1,0:T(8,128)(2,1)S(1)}, bf16[1024,2048]{1,0:T(8,128)(2,1)S(1)}) custom-call(bf16[64,1280]{1,0:T(8,128)(2,1)S(1)} %bitcast.5, s32[64,128]{1,0:T(8,128)S(1)} %spread_lengths.1.lengths_ref, bf16[1024,128]{1,0:T(8,128)(2,1)S(1)} %pad_maximum_fusion.own_ref, bf16[1024,128]{1,0:T(8,128)(2,1)S(1)} %settle.2.refs_0_, ...), custom_call_target="tpu_custom_call" | custom-call | flops 805306368 | bytes 1048576 | tf_op jit(solution)/shard_map/attend/pallas_call | solution.py:366
  23.4 3.1 %collective-permute-start.4 = (bf16[64,1024]{1,0:T(8,128)(2,1)S(1)}, bf16[64,1024]{1,0:T(8,128)(2,1)S(1)}, u32[]{:S(2)}, u32[]{:S(2)}) collective-permute-start(bf16[64,1024]{1,0:T(8,128)(2,1)S(1)} %get-tuple-element.14.x_ref.refs_0_), channel_id=1, source_target_pairs={{0,12},{4,8},{8,4},{12,0},{1,13},{5,9},{9,5},{13,1},{2,14},{6,10},... | collective-permute-start | bytes 393224 | tf_op jit(solution)/shard_map/ppermute | solution.py:144
  26.5 1.3 %collective-permute-start.7 = (bf16[32,1024]{1,0:T(8,128)(2,1)S(1)}, bf16[32,1024]{1,0:T(8,128)(2,1)S(1)}, u32[]{:S(2)}, u32[]{:S(2)}) collective-permute-start(bf16[32,1024]{1,0:T(8,128)(2,1)S(1)} %get-tuple-element.22), channel_id=1, source_target_pairs={{0,8},{4,12},{8,0},{12,4},{1,9},{5,13},{9,1},{13,5},{2,10},{6,14},... | collective-permute-start | bytes 196616 | tf_op jit(solution)/shard_map/ppermute | solution.py:144
  27.8 4.7 %load.1 = (f32[64,2048]{1,0:T(8,128)S(1)}, bf16[1024,2048]{1,0:T(8,128)(2,1)S(1)}, bf16[1024,2048]{1,0:T(8,128)(2,1)S(1)}, bf16[1024,2048]{1,0:T(8,128)(2,1)S(1)}) custom-call(bf16[4096,2048]{1,0:T(8,128)(2,1)} %weight_ref.1, bf16[64,1024]{1,0:T(8,128)(2,1)S(1)} %get-tuple-element.14.x_ref.refs_0_, bf16[1024,2048]{1,0:T(8,128)(2,1)S(1)} %get-tuple-element.15.first_ref), custom_call_target="tpu_custom_call" | custom-call | flops 268435456 | bytes 12582912 | tf_op jit(solution)/shard_map/load/pallas_call | solution.py:402
  32.5 0.8 %project.4 = (f32[64,2048]{1,0:T(8,128)S(1)}, bf16[32,1024]{1,0:T(8,128)(2,1)S(1)}) custom-call(bf16[64,1024]{1,0:T(8,128)(2,1)S(1)} %collective-permute-done.4.x_ref, bf16[1024,2048]{1,0:T(8,128)(2,1)S(1)} %get-tuple-element.16.w_ref, f32[64,2048]{1,0:T(8,128)S(1)} %get-tuple-element.17.acc_ref, bf16[64,1024]{1,0:T(8,128)(2,1)S(1)} %get-tuple-element.14.x_ref.refs_0_), custom_call_target="tpu_custom_call" | custom-call | flops 268435456 | bytes 4194304 | tf_op jit(solution)/shard_map/project/pallas_call | solution.py:440
  33.4 1.7 %collective-permute-start.5 = (bf16[32,1024]{1,0:T(8,128)(2,1)S(1)}, bf16[32,1024]{1,0:T(8,128)(2,1)S(1)}, u32[]{:S(2)}, u32[]{:S(2)}) collective-permute-start(bf16[32,1024]{1,0:T(8,128)(2,1)S(1)} %get-tuple-element.18), channel_id=1, source_target_pairs={{0,8},{4,12},{8,0},{12,4},{1,9},{5,13},{9,1},{13,5},{2,10},{6,14},... | collective-permute-start | bytes 196616 | tf_op jit(solution)/shard_map/ppermute | solution.py:144
  35.1 0.8 %project.5.acc_ref = f32[64,2048]{1,0:T(8,128)S(1)} custom-call(bf16[64,1024]{1,0:T(8,128)(2,1)S(1)} %collective-permute-done.6.x_ref, bf16[1024,2048]{1,0:T(8,128)(2,1)S(1)} %get-tuple-element.20.w_ref, f32[64,2048]{1,0:T(8,128)S(1)} %get-tuple-element.21.acc_ref), custom_call_target="tpu_custom_call" | custom-call | flops 268435456 | bytes 4194304 | tf_op jit(solution)/shard_map/project/pallas_call | solution.py:440
  35.9 0.8 %project.7 = bf16[32,2048]{1,0:T(8,128)(2,1)S(1)} custom-call(bf16[32,1024]{1,0:T(8,128)(2,1)S(1)} %collective-permute-done.7.x_ref, bf16[1024,2048]{1,0:T(8,128)(2,1)S(1)} %get-tuple-element.19.w_ref, f32[64,2048]{1,0:T(8,128)S(1)} %project.5.acc_ref), custom_call_target="tpu_custom_call" | custom-call | flops 134217728 | bytes 4194304 | tf_op jit(solution)/shard_map/project/pallas_call | solution.py:440
  36.8 1.5 %collective-permute-start.8 = (bf16[32,2048]{1,0:T(8,128)(2,1)S(1)}, bf16[32,2048]{1,0:T(8,128)(2,1)S(1)}, u32[]{:S(2)}, u32[]{:S(2)}) collective-permute-start(bf16[32,2048]{1,0:T(8,128)(2,1)S(1)} %project.7), channel_id=1, source_target_pairs={{0,2},{2,0},{1,3},{3,1},{4,6},{6,4},{5,7},{7,5},{8,10},{10,8},{9,1... | collective-permute-start | bytes 393224 | tf_op jit(solution)/shard_map/ppermute | solution.py:144
  38.2 1.1 %collective-permute-done.5.refs_0_ = bf16[32,1024]{1,0:T(8,128)(2,1)S(1)} collective-permute-done((bf16[32,1024]{1,0:T(8,128)(2,1)S(1)}, bf16[32,1024]{1,0:T(8,128)(2,1)S(1)}, u32[]{:S(2)}, u32[]{:S(2)}) %collective-permute-start.5) | collective-permute-done | bytes 65568 | tf_op jit(solution)/shard_map/ppermute | solution.py:144
  39.3 0.8 %project.6.refs_0_ = f32[32,2048]{1,0:T(8,128)S(1)} custom-call(bf16[32,1024]{1,0:T(8,128)(2,1)S(1)} %settle.3.x_ref, bf16[1024,2048]{1,0:T(8,128)(2,1)S(1)} %get-tuple-element.19.w_ref, f32[64,2048]{1,0:T(8,128)S(1)} %project.5.acc_ref), custom_call_target="tpu_custom_call" | custom-call | flops 134217728 | bytes 4194304 | tf_op jit(solution)/shard_map/project/pallas_call | solution.py:440
  40.2 1.6 %collective-permute-done.8.refs_1_ = bf16[32,2048]{1,0:T(8,128)(2,1)S(1)} collective-permute-done((bf16[32,2048]{1,0:T(8,128)(2,1)S(1)}, bf16[32,2048]{1,0:T(8,128)(2,1)S(1)}, u32[]{:S(2)}, u32[]{:S(2)}) %collective-permute-start.8) | collective-permute-done | bytes 131104 | tf_op jit(solution)/shard_map/ppermute | solution.py:144
  41.7 0.7 %add.21 = bf16[1,32,2048]{2,1,0:T(8,128)(2,1)} custom-call(f32[32,2048]{1,0:T(8,128)S(1)} %project.6.refs_0_, bf16[32,2048]{1,0:T(8,128)(2,1)S(1)} %collective-permute-done.8.refs_1_), custom_call_target="tpu_custom_call" | custom-call | bytes 524288 | tf_op jit(solution)/shard_map/add/pallas_call | solution.py:464
  (15 shorter events, 0.2 us)
Async XLA Ops:
  1.2 17.7 %collective-permute-start = (bf16[1024,128]{1,0:T(8,128)(2,1)S(1)}, bf16[1024,128]{1,0:T(8,128)(2,1)S(1)}, u32[]{:S(2)}, u32[]{:S(2)}) collective-permute-start(bf16[1024,128]{1,0:T(8,128)(2,1)S(1)} %pad_maximum_fusion.1), channel_id=1, source_target_pairs={{0,8},{1,13},{4,12},{5,9},{8,0},{9,5},{12,4},{13,1},{2,10},{3,15},... | collective-permute-start | bytes 786440 | tf_op jit(solution)/shard_map/ppermute | solution.py:150
  7.0 11.9 %collective-permute-start.2 = (bf16[512,128]{1,0:T(8,128)(2,1)S(1)}, bf16[512,128]{1,0:T(8,128)(2,1)S(1)}, u32[]{:S(2)}, u32[]{:S(2)}) collective-permute-start(bf16[512,128]{1,0:T(8,128)(2,1)S(1)} %pad_maximum_fusion.2), channel_id=1, source_target_pairs={{0,4},{4,0},{8,12},{12,8},{1,5},{5,1},{9,13},{13,9},{2,6},{6,2},{1... | collective-permute-start | bytes 393224 | tf_op jit(solution)/shard_map/ppermute | solution.py:144
  10.2 10.9 %all-to-all-start = ((bf16[8,8,1280]{2,1,0:T(8,128)(2,1)}), bf16[8,8,1280]{2,1,0:T(8,128)(2,1)S(1)}, u32[]{:S(2)}, u32[]{:S(2)}) async-start(bf16[8,8,1280]{2,1,0:T(8,128)(2,1)} %bitcast.6), calls=%async_computation | async-start | bytes 327680 | tf_op jit(solution)/shard_map/all_to_all | solution.py:496
  13.6 5.8 %copy-start = (s32[1,64]{1,0:T(1,128)S(1)}, s32[1,64]{1,0:T(1,128)}, u32[]{:S(2)}) copy-start(s32[1,64]{1,0:T(1,128)} %visible_ref.1) | copy-start | bytes 772
  18.9 2.3 %collective-permute-start.1 = (bf16[1024,128]{1,0:T(8,128)(2,1)S(1)}, bf16[1024,128]{1,0:T(8,128)(2,1)S(1)}, u32[]{:S(2)}, u32[]{:S(2)}) collective-permute-start(bf16[1024,128]{1,0:T(8,128)(2,1)S(1)} %settle.2.refs_0_), channel_id=1, source_target_pairs={{0,1},{1,0},{2,3},{3,2},{4,5},{5,4},{6,7},{7,6},{8,9},{9,8},{10,11... | collective-permute-start | bytes 786440 | tf_op jit(solution)/shard_map/ppermute | solution.py:144
  18.9 1.7 %collective-permute-start.3 = (bf16[512,128]{1,0:T(8,128)(2,1)S(1)}, bf16[512,128]{1,0:T(8,128)(2,1)S(1)}, u32[]{:S(2)}, u32[]{:S(2)}) collective-permute-start(bf16[512,128]{1,0:T(8,128)(2,1)S(1)} %collective-permute-done.2.refs_2_), channel_id=1, source_target_pairs={{0,1},{1,0},{2,3},{3,2},{4,5},{5,4},{6,7},{7,6},{8,9},{9,8},{10,11... | collective-permute-start | bytes 393224 | tf_op jit(solution)/shard_map/ppermute | solution.py:144
  23.4 9.2 %collective-permute-start.4 = (bf16[64,1024]{1,0:T(8,128)(2,1)S(1)}, bf16[64,1024]{1,0:T(8,128)(2,1)S(1)}, u32[]{:S(2)}, u32[]{:S(2)}) collective-permute-start(bf16[64,1024]{1,0:T(8,128)(2,1)S(1)} %get-tuple-element.14.x_ref.refs_0_), channel_id=1, source_target_pairs={{0,12},{4,8},{8,4},{12,0},{1,13},{5,9},{9,5},{13,1},{2,14},{6,10},... | collective-permute-start | bytes 393224 | tf_op jit(solution)/shard_map/ppermute | solution.py:144
  26.5 8.6 %collective-permute-start.6 = (bf16[64,1024]{1,0:T(8,128)(2,1)S(1)}, bf16[64,1024]{1,0:T(8,128)(2,1)S(1)}, u32[]{:S(2)}, u32[]{:S(2)}) collective-permute-start(bf16[64,1024]{1,0:T(8,128)(2,1)S(1)} %get-tuple-element.14.x_ref.refs_0_), channel_id=1, source_target_pairs={{0,4},{4,0},{8,12},{12,8},{1,5},{5,1},{9,13},{13,9},{2,6},{6,2},{1... | collective-permute-start | bytes 393224 | tf_op jit(solution)/shard_map/ppermute | solution.py:144
  26.5 9.4 %collective-permute-start.7 = (bf16[32,1024]{1,0:T(8,128)(2,1)S(1)}, bf16[32,1024]{1,0:T(8,128)(2,1)S(1)}, u32[]{:S(2)}, u32[]{:S(2)}) collective-permute-start(bf16[32,1024]{1,0:T(8,128)(2,1)S(1)} %get-tuple-element.22), channel_id=1, source_target_pairs={{0,8},{4,12},{8,0},{12,4},{1,9},{5,13},{9,1},{13,5},{2,10},{6,14},... | collective-permute-start | bytes 196616 | tf_op jit(solution)/shard_map/ppermute | solution.py:144
  33.4 5.9 %collective-permute-start.5 = (bf16[32,1024]{1,0:T(8,128)(2,1)S(1)}, bf16[32,1024]{1,0:T(8,128)(2,1)S(1)}, u32[]{:S(2)}, u32[]{:S(2)}) collective-permute-start(bf16[32,1024]{1,0:T(8,128)(2,1)S(1)} %get-tuple-element.18), channel_id=1, source_target_pairs={{0,8},{4,12},{8,0},{12,4},{1,9},{5,13},{9,1},{13,5},{2,10},{6,14},... | collective-permute-start | bytes 196616 | tf_op jit(solution)/shard_map/ppermute | solution.py:144
  36.8 5.0 %collective-permute-start.8 = (bf16[32,2048]{1,0:T(8,128)(2,1)S(1)}, bf16[32,2048]{1,0:T(8,128)(2,1)S(1)}, u32[]{:S(2)}, u32[]{:S(2)}) collective-permute-start(bf16[32,2048]{1,0:T(8,128)(2,1)S(1)} %project.7), channel_id=1, source_target_pairs={{0,2},{2,0},{1,3},{3,1},{4,6},{6,4},{5,7},{7,5},{8,10},{10,8},{9,1... | collective-permute-start | bytes 393224 | tf_op jit(solution)/shard_map/ppermute | solution.py:144

commit v7 on v6

--- a/solution.py
+++ b/solution.py
@@ -130,8 +130,8 @@
 
 EXPONENT = SCALE * math.log2(math.e)
 VMEM_BYTES = 20 * 2**20
-UNIT_ROWS = 128
-FETCHES = 4
+UNIT_ROWS = 256
+FETCHES = 1
 SETTLE_FIRST = 10**11
 SETTLE_LAST = 10**10
 PACK_BYTES = 56 * 2**20
@@ -536,7 +536,7 @@
             and seq_count in (4, 8)
             and sizes["tp"] == 2
             and sizes["rep"] == 2
-            and args[0].shape[2] // args[1].shape[2] % 2 == 0
+            and args[0].shape[2] // args[1].shape[2] % 4 == 0
         )
         return (shards_by_head if by_head else shards_any)(*args)
 

time: 42.7 us -> 42.7 us (level)
  no operation moved by 1% of the time
where the time goes in v7:
time: 42.7 us; the launch traced here: 42.4 us
  starting transfers between devices  17.3 us (41%)
  Pallas kernels  12.6 us (30%)
  waiting for transfers between devices  9.5 us (22%)
  local copies, waits for them, and re-layouts  2.83 us (7%)
    ppermute x8, starting transfers between devices, swap(): lax.ppermute(array, axis, [(i, i ^ mask) for i in range(lax.axis_size(axi...  9.76 us
    ppermute x1, waiting for transfers between devices, swap_by_core(): return lax.ppermute(array, ('seq', 'rep'), pairs)  5.24 us
    pallas_call x1, Pallas kernels, load(): pl.pallas_call(functools.partial(load_kernel, masks), out_shape=[jax.Shap...  4.69 us
    ppermute x1, starting transfers between devices, swap_by_core(): return lax.ppermute(array, ('seq', 'rep'), pairs)  4.1 us
    ppermute x8, waiting for transfers between devices, swap(): lax.ppermute(array, axis, [(i, i ^ mask) for i in range(lax.axis_size(axi...  3.73 us
    all_to_all x1, starting transfers between devices, shards_by_head(): lax.all_to_all(pack_queries(rows, 1 + len(masks)), ('seq', 'tp'), split_a...  3.39 us
    pallas_call x4, Pallas kernels, project(): pl.pallas_call(functools.partial(project_kernel, side, pass_on is not Non...  3.35 us
    dynamic_slice x3, local copies, waits for them, and re-layouts, cut(): lax.dynamic_slice(table, (first, head * HEAD_WIDTH), (count, HEAD_WIDTH))  2.83 us
  transfers between devices with their start and end apart: 10, of which 5 were waited for; matrix products, arithmetic and copies ran while one was open for 4% of the time, Pallas kernels for 23%

profile of v7, /device:TPU:0, one launch (start us, length us, event | category | flops | bytes accessed | tf_op | source)
XLA Modules:
  0.0 42.4 jit_solution(17750621882413496847)
XLA Ops:
  0.0 1.1 %constant_dynamic-slice_fusion = (bf16[512,128]{1,0:T(8,128)(2,1)S(1)}, bf16[512,128]{1,0:T(8,128)(2,1)S(1)}, bf16[512,128]{1,0:T(8,128)(2,1)S(1)}, bf16[512,128]{1,0:T(8,128)(2,1)S(1)}) fusion(bf16[512,512]{1,0:T(8,128)(2,1)} %param.12, s32[]{:T(128)S(6)} %select_n.17, s32[]{:T(128)S(6)} %select_n.16, bf16[512,512]{1,0:T(8,128)(2,1)} %param.11), kind=kLoop, calls=%fused_computation.3 | loop fusion | bytes 1048584 | tf_op jit(solution)/shard_map/dynamic_slice | solution.py:487
  1.2 4.1 %collective-permute-start = (bf16[1024,128]{1,0:T(8,128)(2,1)S(1)}, bf16[1024,128]{1,0:T(8,128)(2,1)S(1)}, u32[]{:S(2)}, u32[]{:S(2)}) collective-permute-start(bf16[1024,128]{1,0:T(8,128)(2,1)S(1)} %pad_maximum_fusion.1), channel_id=1, source_target_pairs={{0,8},{1,13},{4,12},{5,9},{8,0},{9,5},{12,4},{13,1},{2,10},{3,15},... | collective-permute-start | bytes 786440 | tf_op jit(solution)/shard_map/ppermute | solution.py:150
  5.3 0.8 %dynamic_slice.22 = bf16[256,128]{1,0:T(8,128)(2,1)S(1)} dynamic-slice(bf16[512,512]{1,0:T(8,128)(2,1)} %param.11, s32[]{:T(128)S(6)} %select_n.18, s32[]{:T(128)S(6)} %select_n.19), dynamic_slice_sizes={256,128} | dynamic-slice | bytes 131076 | tf_op jit(solution)/shard_map/dynamic_slice | solution.py:487
  6.1 0.8 %dynamic_slice.23 = bf16[256,128]{1,0:T(8,128)(2,1)S(1)} dynamic-slice(bf16[512,512]{1,0:T(8,128)(2,1)} %param.12, s32[]{:T(128)S(6)} %select_n.18, s32[]{:T(128)S(6)} %select_n.19), dynamic_slice_sizes={256,128} | dynamic-slice | bytes 131076 | tf_op jit(solution)/shard_map/dynamic_slice | solution.py:487
  7.0 1.6 %collective-permute-start.2 = (bf16[512,128]{1,0:T(8,128)(2,1)S(1)}, bf16[512,128]{1,0:T(8,128)(2,1)S(1)}, u32[]{:S(2)}, u32[]{:S(2)}) collective-permute-start(bf16[512,128]{1,0:T(8,128)(2,1)S(1)} %pad_maximum_fusion.2), channel_id=1, source_target_pairs={{0,4},{4,0},{8,12},{12,8},{1,5},{5,1},{9,13},{13,9},{2,6},{6,2},{1... | collective-permute-start | bytes 393224 | tf_op jit(solution)/shard_map/ppermute | solution.py:144
  8.6 1.6 %pack_queries.1 = bf16[64,1280]{1,0:T(8,128)(2,1)} custom-call(bf16[8,8192]{1,0:T(8,128)(2,1)} %bitcast.7, bf16[8,1024]{1,0:T(8,128)(2,1)} %bitcast.8, bf16[8,1024]{1,0:T(8,128)(2,1)} %bitcast.9), custom_call_target="tpu_custom_call" | custom-call | bytes 524288 | tf_op jit(solution)/shard_map/pack_queries/pallas_call | solution.py:205
  10.2 3.4 %all-to-all-start = ((bf16[8,8,1280]{2,1,0:T(8,128)(2,1)}), bf16[8,8,1280]{2,1,0:T(8,128)(2,1)S(1)}, u32[]{:S(2)}, u32[]{:S(2)}) async-start(bf16[8,8,1280]{2,1,0:T(8,128)(2,1)} %bitcast.6), calls=%async_computation | async-start | bytes 327680 | tf_op jit(solution)/shard_map/all_to_all | solution.py:496
  13.6 5.2 %collective-permute-done.refs_0_ = bf16[1024,128]{1,0:T(8,128)(2,1)S(1)} collective-permute-done((bf16[1024,128]{1,0:T(8,128)(2,1)S(1)}, bf16[1024,128]{1,0:T(8,128)(2,1)S(1)}, u32[]{:S(2)}, u32[]{:S(2)}) %collective-permute-start) | collective-permute-done | bytes 262176 | tf_op jit(solution)/shard_map/ppermute | solution.py:150
  18.9 0.5 %collective-permute-start.3 = (bf16[512,128]{1,0:T(8,128)(2,1)S(1)}, bf16[512,128]{1,0:T(8,128)(2,1)S(1)}, u32[]{:S(2)}, u32[]{:S(2)}) collective-permute-start(bf16[512,128]{1,0:T(8,128)(2,1)S(1)} %collective-permute-done.2.refs_2_), channel_id=1, source_target_pairs={{0,1},{1,0},{2,3},{3,2},{4,5},{5,4},{6,7},{7,6},{8,9},{9,8},{10,11... | collective-permute-start | bytes 393224 | tf_op jit(solution)/shard_map/ppermute | solution.py:144
  19.5 1.1 %collective-permute-done.3.refs_3_ = bf16[512,128]{1,0:T(8,128)(2,1)S(1)} collective-permute-done((bf16[512,128]{1,0:T(8,128)(2,1)S(1)}, bf16[512,128]{1,0:T(8,128)(2,1)S(1)}, u32[]{:S(2)}, u32[]{:S(2)}) %collective-permute-start.3) | collective-permute-done | bytes 131104 | tf_op jit(solution)/shard_map/ppermute | solution.py:144
  20.6 0.5 %all-to-all-done = bf16[8,8,1280]{2,1,0:T(8,128)(2,1)S(1)} async-done(((bf16[8,8,1280]{2,1,0:T(8,128)(2,1)}), bf16[8,8,1280]{2,1,0:T(8,128)(2,1)S(1)}, u32[]{:S(2)}, u32[]{:S(2)}) %all-to-all-start) | async-done | bytes 163872 | tf_op jit(solution)/shard_map/all_to_all | solution.py:496
  21.1 2.2 %attend.1 = (bf16[64,1024]{1,0:T(8,128)(2,1)S(1)}, bf16[32,1024]{1,0:T(8,128)(2,1)S(1)}, bf16[1024,2048]{1,0:T(8,128)(2,1)S(1)}) custom-call(bf16[64,1280]{1,0:T(8,128)(2,1)S(1)} %bitcast.5, s32[64,128]{1,0:T(8,128)S(1)} %spread_lengths.1.lengths_ref, bf16[1024,128]{1,0:T(8,128)(2,1)S(1)} %pad_maximum_fusion.own_ref, bf16[1024,128]{1,0:T(8,128)(2,1)S(1)} %settle.2.refs_0_, ...), custom_call_target="tpu_custom_call" | custom-call | flops 805306368 | bytes 1048576 | tf_op jit(solution)/shard_map/attend/pallas_call | solution.py:366
  23.3 3.1 %collective-permute-start.4 = (bf16[64,1024]{1,0:T(8,128)(2,1)S(1)}, bf16[64,1024]{1,0:T(8,128)(2,1)S(1)}, u32[]{:S(2)}, u32[]{:S(2)}) collective-permute-start(bf16[64,1024]{1,0:T(8,128)(2,1)S(1)} %get-tuple-element.14.x_ref.refs_0_), channel_id=1, source_target_pairs={{0,12},{4,8},{8,4},{12,0},{1,13},{5,9},{9,5},{13,1},{2,14},{6,10},... | collective-permute-start | bytes 393224 | tf_op jit(solution)/shard_map/ppermute | solution.py:144
  26.5 1.3 %collective-permute-start.7 = (bf16[32,1024]{1,0:T(8,128)(2,1)S(1)}, bf16[32,1024]{1,0:T(8,128)(2,1)S(1)}, u32[]{:S(2)}, u32[]{:S(2)}) collective-permute-start(bf16[32,1024]{1,0:T(8,128)(2,1)S(1)} %get-tuple-element.22), channel_id=1, source_target_pairs={{0,8},{4,12},{8,0},{12,4},{1,9},{5,13},{9,1},{13,5},{2,10},{6,14},... | collective-permute-start | bytes 196616 | tf_op jit(solution)/shard_map/ppermute | solution.py:144
  27.8 4.7 %load.1 = (f32[64,2048]{1,0:T(8,128)S(1)}, bf16[1024,2048]{1,0:T(8,128)(2,1)S(1)}, bf16[1024,2048]{1,0:T(8,128)(2,1)S(1)}, bf16[1024,2048]{1,0:T(8,128)(2,1)S(1)}) custom-call(bf16[4096,2048]{1,0:T(8,128)(2,1)} %weight_ref.1, bf16[64,1024]{1,0:T(8,128)(2,1)S(1)} %get-tuple-element.14.x_ref.refs_0_, bf16[1024,2048]{1,0:T(8,128)(2,1)S(1)} %get-tuple-element.15.first_ref), custom_call_target="tpu_custom_call" | custom-call | flops 268435456 | bytes 12582912 | tf_op jit(solution)/shard_map/load/pallas_call | solution.py:402
  32.5 0.8 %project.4 = (f32[64,2048]{1,0:T(8,128)S(1)}, bf16[32,1024]{1,0:T(8,128)(2,1)S(1)}) custom-call(bf16[64,1024]{1,0:T(8,128)(2,1)S(1)} %collective-permute-done.4.x_ref, bf16[1024,2048]{1,0:T(8,128)(2,1)S(1)} %get-tuple-element.16.w_ref, f32[64,2048]{1,0:T(8,128)S(1)} %get-tuple-element.17.acc_ref, bf16[64,1024]{1,0:T(8,128)(2,1)S(1)} %get-tuple-element.14.x_ref.refs_0_), custom_call_target="tpu_custom_call" | custom-call | flops 268435456 | bytes 4194304 | tf_op jit(solution)/shard_map/project/pallas_call | solution.py:440
  33.4 1.7 %collective-permute-start.5 = (bf16[32,1024]{1,0:T(8,128)(2,1)S(1)}, bf16[32,1024]{1,0:T(8,128)(2,1)S(1)}, u32[]{:S(2)}, u32[]{:S(2)}) collective-permute-start(bf16[32,1024]{1,0:T(8,128)(2,1)S(1)} %get-tuple-element.18), channel_id=1, source_target_pairs={{0,8},{4,12},{8,0},{12,4},{1,9},{5,13},{9,1},{13,5},{2,10},{6,14},... | collective-permute-start | bytes 196616 | tf_op jit(solution)/shard_map/ppermute | solution.py:144
  35.0 0.8 %project.5.acc_ref = f32[64,2048]{1,0:T(8,128)S(1)} custom-call(bf16[64,1024]{1,0:T(8,128)(2,1)S(1)} %collective-permute-done.6.x_ref, bf16[1024,2048]{1,0:T(8,128)(2,1)S(1)} %get-tuple-element.20.w_ref, f32[64,2048]{1,0:T(8,128)S(1)} %get-tuple-element.21.acc_ref), custom_call_target="tpu_custom_call" | custom-call | flops 268435456 | bytes 4194304 | tf_op jit(solution)/shard_map/project/pallas_call | solution.py:440
  35.9 0.8 %project.7 = bf16[32,2048]{1,0:T(8,128)(2,1)S(1)} custom-call(bf16[32,1024]{1,0:T(8,128)(2,1)S(1)} %collective-permute-done.7.x_ref, bf16[1024,2048]{1,0:T(8,128)(2,1)S(1)} %get-tuple-element.19.w_ref, f32[64,2048]{1,0:T(8,128)S(1)} %project.5.acc_ref), custom_call_target="tpu_custom_call" | custom-call | flops 134217728 | bytes 4194304 | tf_op jit(solution)/shard_map/project/pallas_call | solution.py:440
  36.7 1.5 %collective-permute-start.8 = (bf16[32,2048]{1,0:T(8,128)(2,1)S(1)}, bf16[32,2048]{1,0:T(8,128)(2,1)S(1)}, u32[]{:S(2)}, u32[]{:S(2)}) collective-permute-start(bf16[32,2048]{1,0:T(8,128)(2,1)S(1)} %project.7), channel_id=1, source_target_pairs={{0,2},{2,0},{1,3},{3,1},{4,6},{6,4},{5,7},{7,5},{8,10},{10,8},{9,1... | collective-permute-start | bytes 393224 | tf_op jit(solution)/shard_map/ppermute | solution.py:144
  38.2 1.1 %collective-permute-done.5.refs_0_ = bf16[32,1024]{1,0:T(8,128)(2,1)S(1)} collective-permute-done((bf16[32,1024]{1,0:T(8,128)(2,1)S(1)}, bf16[32,1024]{1,0:T(8,128)(2,1)S(1)}, u32[]{:S(2)}, u32[]{:S(2)}) %collective-permute-start.5) | collective-permute-done | bytes 65568 | tf_op jit(solution)/shard_map/ppermute | solution.py:144
  39.3 0.8 %project.6.refs_0_ = f32[32,2048]{1,0:T(8,128)S(1)} custom-call(bf16[32,1024]{1,0:T(8,128)(2,1)S(1)} %settle.3.x_ref, bf16[1024,2048]{1,0:T(8,128)(2,1)S(1)} %get-tuple-element.19.w_ref, f32[64,2048]{1,0:T(8,128)S(1)} %project.5.acc_ref), custom_call_target="tpu_custom_call" | custom-call | flops 134217728 | bytes 4194304 | tf_op jit(solution)/shard_map/project/pallas_call | solution.py:440
  40.1 1.6 %collective-permute-done.8.refs_1_ = bf16[32,2048]{1,0:T(8,128)(2,1)S(1)} collective-permute-done((bf16[32,2048]{1,0:T(8,128)(2,1)S(1)}, bf16[32,2048]{1,0:T(8,128)(2,1)S(1)}, u32[]{:S(2)}, u32[]{:S(2)}) %collective-permute-start.8) | collective-permute-done | bytes 131104 | tf_op jit(solution)/shard_map/ppermute | solution.py:144
  41.7 0.7 %add.21 = bf16[1,32,2048]{2,1,0:T(8,128)(2,1)} custom-call(f32[32,2048]{1,0:T(8,128)S(1)} %project.6.refs_0_, bf16[32,2048]{1,0:T(8,128)(2,1)S(1)} %collective-permute-done.8.refs_1_), custom_call_target="tpu_custom_call" | custom-call | bytes 524288 | tf_op jit(solution)/shard_map/add/pallas_call | solution.py:464
  (15 shorter events, 0.2 us)
Async XLA Ops:
  1.2 17.7 %collective-permute-start = (bf16[1024,128]{1,0:T(8,128)(2,1)S(1)}, bf16[1024,128]{1,0:T(8,128)(2,1)S(1)}, u32[]{:S(2)}, u32[]{:S(2)}) collective-permute-start(bf16[1024,128]{1,0:T(8,128)(2,1)S(1)} %pad_maximum_fusion.1), channel_id=1, source_target_pairs={{0,8},{1,13},{4,12},{5,9},{8,0},{9,5},{12,4},{13,1},{2,10},{3,15},... | collective-permute-start | bytes 786440 | tf_op jit(solution)/shard_map/ppermute | solution.py:150
  7.0 11.9 %collective-permute-start.2 = (bf16[512,128]{1,0:T(8,128)(2,1)S(1)}, bf16[512,128]{1,0:T(8,128)(2,1)S(1)}, u32[]{:S(2)}, u32[]{:S(2)}) collective-permute-start(bf16[512,128]{1,0:T(8,128)(2,1)S(1)} %pad_maximum_fusion.2), channel_id=1, source_target_pairs={{0,4},{4,0},{8,12},{12,8},{1,5},{5,1},{9,13},{13,9},{2,6},{6,2},{1... | collective-permute-start | bytes 393224 | tf_op jit(solution)/shard_map/ppermute | solution.py:144
  10.2 10.9 %all-to-all-start = ((bf16[8,8,1280]{2,1,0:T(8,128)(2,1)}), bf16[8,8,1280]{2,1,0:T(8,128)(2,1)S(1)}, u32[]{:S(2)}, u32[]{:S(2)}) async-start(bf16[8,8,1280]{2,1,0:T(8,128)(2,1)} %bitcast.6), calls=%async_computation | async-start | bytes 327680 | tf_op jit(solution)/shard_map/all_to_all | solution.py:496
  13.6 5.8 %copy-start = (s32[1,64]{1,0:T(1,128)S(1)}, s32[1,64]{1,0:T(1,128)}, u32[]{:S(2)}) copy-start(s32[1,64]{1,0:T(1,128)} %visible_ref.1) | copy-start | bytes 772
  18.9 2.3 %collective-permute-start.1 = (bf16[1024,128]{1,0:T(8,128)(2,1)S(1)}, bf16[1024,128]{1,0:T(8,128)(2,1)S(1)}, u32[]{:S(2)}, u32[]{:S(2)}) collective-permute-start(bf16[1024,128]{1,0:T(8,128)(2,1)S(1)} %settle.2.refs_0_), channel_id=1, source_target_pairs={{0,1},{1,0},{2,3},{3,2},{4,5},{5,4},{6,7},{7,6},{8,9},{9,8},{10,11... | collective-permute-start | bytes 786440 | tf_op jit(solution)/shard_map/ppermute | solution.py:144
  18.9 1.7 %collective-permute-start.3 = (bf16[512,128]{1,0:T(8,128)(2,1)S(1)}, bf16[512,128]{1,0:T(8,128)(2,1)S(1)}, u32[]{:S(2)}, u32[]{:S(2)}) collective-permute-start(bf16[512,128]{1,0:T(8,128)(2,1)S(1)} %collective-permute-done.2.refs_2_), channel_id=1, source_target_pairs={{0,1},{1,0},{2,3},{3,2},{4,5},{5,4},{6,7},{7,6},{8,9},{9,8},{10,11... | collective-permute-start | bytes 393224 | tf_op jit(solution)/shard_map/ppermute | solution.py:144
  23.3 9.2 %collective-permute-start.4 = (bf16[64,1024]{1,0:T(8,128)(2,1)S(1)}, bf16[64,1024]{1,0:T(8,128)(2,1)S(1)}, u32[]{:S(2)}, u32[]{:S(2)}) collective-permute-start(bf16[64,1024]{1,0:T(8,128)(2,1)S(1)} %get-tuple-element.14.x_ref.refs_0_), channel_id=1, source_target_pairs={{0,12},{4,8},{8,4},{12,0},{1,13},{5,9},{9,5},{13,1},{2,14},{6,10},... | collective-permute-start | bytes 393224 | tf_op jit(solution)/shard_map/ppermute | solution.py:144
  26.5 8.6 %collective-permute-start.6 = (bf16[64,1024]{1,0:T(8,128)(2,1)S(1)}, bf16[64,1024]{1,0:T(8,128)(2,1)S(1)}, u32[]{:S(2)}, u32[]{:S(2)}) collective-permute-start(bf16[64,1024]{1,0:T(8,128)(2,1)S(1)} %get-tuple-element.14.x_ref.refs_0_), channel_id=1, source_target_pairs={{0,4},{4,0},{8,12},{12,8},{1,5},{5,1},{9,13},{13,9},{2,6},{6,2},{1... | collective-permute-start | bytes 393224 | tf_op jit(solution)/shard_map/ppermute | solution.py:144
  26.5 9.4 %collective-permute-start.7 = (bf16[32,1024]{1,0:T(8,128)(2,1)S(1)}, bf16[32,1024]{1,0:T(8,128)(2,1)S(1)}, u32[]{:S(2)}, u32[]{:S(2)}) collective-permute-start(bf16[32,1024]{1,0:T(8,128)(2,1)S(1)} %get-tuple-element.22), channel_id=1, source_target_pairs={{0,8},{4,12},{8,0},{12,4},{1,9},{5,13},{9,1},{13,5},{2,10},{6,14},... | collective-permute-start | bytes 196616 | tf_op jit(solution)/shard_map/ppermute | solution.py:144
  33.4 5.9 %collective-permute-start.5 = (bf16[32,1024]{1,0:T(8,128)(2,1)S(1)}, bf16[32,1024]{1,0:T(8,128)(2,1)S(1)}, u32[]{:S(2)}, u32[]{:S(2)}) collective-permute-start(bf16[32,1024]{1,0:T(8,128)(2,1)S(1)} %get-tuple-element.18), channel_id=1, source_target_pairs={{0,8},{4,12},{8,0},{12,4},{1,9},{5,13},{9,1},{13,5},{2,10},{6,14},... | collective-permute-start | bytes 196616 | tf_op jit(solution)/shard_map/ppermute | solution.py:144
  36.7 5.0 %collective-permute-start.8 = (bf16[32,2048]{1,0:T(8,128)(2,1)S(1)}, bf16[32,2048]{1,0:T(8,128)(2,1)S(1)}, u32[]{:S(2)}, u32[]{:S(2)}) collective-permute-start(bf16[32,2048]{1,0:T(8,128)(2,1)S(1)} %project.7), channel_id=1, source_target_pairs={{0,2},{2,0},{1,3},{3,1},{4,6},{6,4},{5,7},{7,5},{8,10},{10,8},{9,1... | collective-permute-start | bytes 393224 | tf_op jit(solution)/shard_map/ppermute | solution.py:144

commit v8 on v7

--- a/solution.py
+++ b/solution.py
@@ -276,7 +276,7 @@
 
 def multiply(x_ref, w_ref, finish):
     columns = w_ref.shape[1]
-    width = math.gcd(columns, 512)
+    width = math.gcd(columns, 2048)
     for start in range(0, columns, width):
         at = slice(start, start + width)
         finish(at, jnp.dot(x_ref[...], w_ref[:, at], preferred_element_type=jnp.float32))

time: 42.7 us -> 42.7 us (level)
  no operation moved by 1% of the time
where the time goes in v8:
time: 42.7 us; the launch traced here: 42.4 us
  starting transfers between devices  17.3 us (41%)
  Pallas kernels  12.6 us (30%)
  waiting for transfers between devices  9.51 us (22%)
  local copies, waits for them, and re-layouts  2.83 us (7%)
    ppermute x8, starting transfers between devices, swap(): lax.ppermute(array, axis, [(i, i ^ mask) for i in range(lax.axis_size(axi...  9.77 us
    ppermute x1, waiting for transfers between devices, swap_by_core(): return lax.ppermute(array, ('seq', 'rep'), pairs)  5.24 us
    pallas_call x1, Pallas kernels, load(): pl.pallas_call(functools.partial(load_kernel, masks), out_shape=[jax.Shap...  4.69 us
    ppermute x1, starting transfers between devices, swap_by_core(): return lax.ppermute(array, ('seq', 'rep'), pairs)  4.1 us
    ppermute x8, waiting for transfers between devices, swap(): lax.ppermute(array, axis, [(i, i ^ mask) for i in range(lax.axis_size(axi...  3.74 us
    all_to_all x1, starting transfers between devices, shards_by_head(): lax.all_to_all(pack_queries(rows, 1 + len(masks)), ('seq', 'tp'), split_a...  3.39 us
    pallas_call x4, Pallas kernels, project(): pl.pallas_call(functools.partial(project_kernel, side, pass_on is not Non...  3.33 us
    dynamic_slice x3, local copies, waits for them, and re-layouts, cut(): lax.dynamic_slice(table, (first, head * HEAD_WIDTH), (count, HEAD_WIDTH))  2.83 us
  transfers between devices with their start and end apart: 10, of which 5 were waited for; matrix products, arithmetic and copies ran while one was open for 4% of the time, Pallas kernels for 23%

profile of v8, /device:TPU:0, one launch (start us, length us, event | category | flops | bytes accessed | tf_op | source)
XLA Modules:
  0.0 42.4 jit_solution(16635733663456573516)
XLA Ops:
  0.0 1.1 %constant_dynamic-slice_fusion = (bf16[512,128]{1,0:T(8,128)(2,1)S(1)}, bf16[512,128]{1,0:T(8,128)(2,1)S(1)}, bf16[512,128]{1,0:T(8,128)(2,1)S(1)}, bf16[512,128]{1,0:T(8,128)(2,1)S(1)}) fusion(bf16[512,512]{1,0:T(8,128)(2,1)} %param.12, s32[]{:T(128)S(6)} %select_n.17, s32[]{:T(128)S(6)} %select_n.16, bf16[512,512]{1,0:T(8,128)(2,1)} %param.11), kind=kLoop, calls=%fused_computation.3 | loop fusion | bytes 1048584 | tf_op jit(solution)/shard_map/dynamic_slice | solution.py:487
  1.2 4.1 %collective-permute-start = (bf16[1024,128]{1,0:T(8,128)(2,1)S(1)}, bf16[1024,128]{1,0:T(8,128)(2,1)S(1)}, u32[]{:S(2)}, u32[]{:S(2)}) collective-permute-start(bf16[1024,128]{1,0:T(8,128)(2,1)S(1)} %pad_maximum_fusion.1), channel_id=1, source_target_pairs={{0,8},{1,13},{4,12},{5,9},{8,0},{9,5},{12,4},{13,1},{2,10},{3,15},... | collective-permute-start | bytes 786440 | tf_op jit(solution)/shard_map/ppermute | solution.py:150
  5.3 0.8 %dynamic_slice.22 = bf16[256,128]{1,0:T(8,128)(2,1)S(1)} dynamic-slice(bf16[512,512]{1,0:T(8,128)(2,1)} %param.11, s32[]{:T(128)S(6)} %select_n.18, s32[]{:T(128)S(6)} %select_n.19), dynamic_slice_sizes={256,128} | dynamic-slice | bytes 131076 | tf_op jit(solution)/shard_map/dynamic_slice | solution.py:487
  6.1 0.8 %dynamic_slice.23 = bf16[256,128]{1,0:T(8,128)(2,1)S(1)} dynamic-slice(bf16[512,512]{1,0:T(8,128)(2,1)} %param.12, s32[]{:T(128)S(6)} %select_n.18, s32[]{:T(128)S(6)} %select_n.19), dynamic_slice_sizes={256,128} | dynamic-slice | bytes 131076 | tf_op jit(solution)/shard_map/dynamic_slice | solution.py:487
  7.0 1.6 %collective-permute-start.2 = (bf16[512,128]{1,0:T(8,128)(2,1)S(1)}, bf16[512,128]{1,0:T(8,128)(2,1)S(1)}, u32[]{:S(2)}, u32[]{:S(2)}) collective-permute-start(bf16[512,128]{1,0:T(8,128)(2,1)S(1)} %pad_maximum_fusion.2), channel_id=1, source_target_pairs={{0,4},{4,0},{8,12},{12,8},{1,5},{5,1},{9,13},{13,9},{2,6},{6,2},{1... | collective-permute-start | bytes 393224 | tf_op jit(solution)/shard_map/ppermute | solution.py:144
  8.6 1.6 %pack_queries.1 = bf16[64,1280]{1,0:T(8,128)(2,1)} custom-call(bf16[8,8192]{1,0:T(8,128)(2,1)} %bitcast.7, bf16[8,1024]{1,0:T(8,128)(2,1)} %bitcast.8, bf16[8,1024]{1,0:T(8,128)(2,1)} %bitcast.9), custom_call_target="tpu_custom_call" | custom-call | bytes 524288 | tf_op jit(solution)/shard_map/pack_queries/pallas_call | solution.py:205
  10.2 3.4 %all-to-all-start = ((bf16[8,8,1280]{2,1,0:T(8,128)(2,1)}), bf16[8,8,1280]{2,1,0:T(8,128)(2,1)S(1)}, u32[]{:S(2)}, u32[]{:S(2)}) async-start(bf16[8,8,1280]{2,1,0:T(8,128)(2,1)} %bitcast.6), calls=%async_computation | async-start | bytes 327680 | tf_op jit(solution)/shard_map/all_to_all | solution.py:496
  13.6 5.2 %collective-permute-done.refs_0_ = bf16[1024,128]{1,0:T(8,128)(2,1)S(1)} collective-permute-done((bf16[1024,128]{1,0:T(8,128)(2,1)S(1)}, bf16[1024,128]{1,0:T(8,128)(2,1)S(1)}, u32[]{:S(2)}, u32[]{:S(2)}) %collective-permute-start) | collective-permute-done | bytes 262176 | tf_op jit(solution)/shard_map/ppermute | solution.py:150
  18.9 0.5 %collective-permute-start.3 = (bf16[512,128]{1,0:T(8,128)(2,1)S(1)}, bf16[512,128]{1,0:T(8,128)(2,1)S(1)}, u32[]{:S(2)}, u32[]{:S(2)}) collective-permute-start(bf16[512,128]{1,0:T(8,128)(2,1)S(1)} %collective-permute-done.2.refs_2_), channel_id=1, source_target_pairs={{0,1},{1,0},{2,3},{3,2},{4,5},{5,4},{6,7},{7,6},{8,9},{9,8},{10,11... | collective-permute-start | bytes 393224 | tf_op jit(solution)/shard_map/ppermute | solution.py:144
  19.5 1.1 %collective-permute-done.3.refs_3_ = bf16[512,128]{1,0:T(8,128)(2,1)S(1)} collective-permute-done((bf16[512,128]{1,0:T(8,128)(2,1)S(1)}, bf16[512,128]{1,0:T(8,128)(2,1)S(1)}, u32[]{:S(2)}, u32[]{:S(2)}) %collective-permute-start.3) | collective-permute-done | bytes 131104 | tf_op jit(solution)/shard_map/ppermute | solution.py:144
  20.6 0.5 %all-to-all-done = bf16[8,8,1280]{2,1,0:T(8,128)(2,1)S(1)} async-done(((bf16[8,8,1280]{2,1,0:T(8,128)(2,1)}), bf16[8,8,1280]{2,1,0:T(8,128)(2,1)S(1)}, u32[]{:S(2)}, u32[]{:S(2)}) %all-to-all-start) | async-done | bytes 163872 | tf_op jit(solution)/shard_map/all_to_all | solution.py:496
  21.1 2.2 %attend.1 = (bf16[64,1024]{1,0:T(8,128)(2,1)S(1)}, bf16[32,1024]{1,0:T(8,128)(2,1)S(1)}, bf16[1024,2048]{1,0:T(8,128)(2,1)S(1)}) custom-call(bf16[64,1280]{1,0:T(8,128)(2,1)S(1)} %bitcast.5, s32[64,128]{1,0:T(8,128)S(1)} %spread_lengths.1.lengths_ref, bf16[1024,128]{1,0:T(8,128)(2,1)S(1)} %pad_maximum_fusion.own_ref, bf16[1024,128]{1,0:T(8,128)(2,1)S(1)} %settle.2.refs_0_, ...), custom_call_target="tpu_custom_call" | custom-call | flops 805306368 | bytes 1048576 | tf_op jit(solution)/shard_map/attend/pallas_call | solution.py:366
  23.3 3.1 %collective-permute-start.4 = (bf16[64,1024]{1,0:T(8,128)(2,1)S(1)}, bf16[64,1024]{1,0:T(8,128)(2,1)S(1)}, u32[]{:S(2)}, u32[]{:S(2)}) collective-permute-start(bf16[64,1024]{1,0:T(8,128)(2,1)S(1)} %get-tuple-element.14.x_ref.refs_0_), channel_id=1, source_target_pairs={{0,12},{4,8},{8,4},{12,0},{1,13},{5,9},{9,5},{13,1},{2,14},{6,10},... | collective-permute-start | bytes 393224 | tf_op jit(solution)/shard_map/ppermute | solution.py:144
  26.5 1.3 %collective-permute-start.7 = (bf16[32,1024]{1,0:T(8,128)(2,1)S(1)}, bf16[32,1024]{1,0:T(8,128)(2,1)S(1)}, u32[]{:S(2)}, u32[]{:S(2)}) collective-permute-start(bf16[32,1024]{1,0:T(8,128)(2,1)S(1)} %get-tuple-element.22), channel_id=1, source_target_pairs={{0,8},{4,12},{8,0},{12,4},{1,9},{5,13},{9,1},{13,5},{2,10},{6,14},... | collective-permute-start | bytes 196616 | tf_op jit(solution)/shard_map/ppermute | solution.py:144
  27.8 4.7 %load.1 = (f32[64,2048]{1,0:T(8,128)S(1)}, bf16[1024,2048]{1,0:T(8,128)(2,1)S(1)}, bf16[1024,2048]{1,0:T(8,128)(2,1)S(1)}, bf16[1024,2048]{1,0:T(8,128)(2,1)S(1)}) custom-call(bf16[4096,2048]{1,0:T(8,128)(2,1)} %weight_ref.1, bf16[64,1024]{1,0:T(8,128)(2,1)S(1)} %get-tuple-element.14.x_ref.refs_0_, bf16[1024,2048]{1,0:T(8,128)(2,1)S(1)} %get-tuple-element.15.first_ref), custom_call_target="tpu_custom_call" | custom-call | flops 268435456 | bytes 12582912 | tf_op jit(solution)/shard_map/load/pallas_call | solution.py:402
  32.5 0.8 %project.4 = (f32[64,2048]{1,0:T(8,128)S(1)}, bf16[32,1024]{1,0:T(8,128)(2,1)S(1)}) custom-call(bf16[64,1024]{1,0:T(8,128)(2,1)S(1)} %collective-permute-done.4.x_ref, bf16[1024,2048]{1,0:T(8,128)(2,1)S(1)} %get-tuple-element.16.w_ref, f32[64,2048]{1,0:T(8,128)S(1)} %get-tuple-element.17.acc_ref, bf16[64,1024]{1,0:T(8,128)(2,1)S(1)} %get-tuple-element.14.x_ref.refs_0_), custom_call_target="tpu_custom_call" | custom-call | flops 268435456 | bytes 4194304 | tf_op jit(solution)/shard_map/project/pallas_call | solution.py:440
  33.4 1.7 %collective-permute-start.5 = (bf16[32,1024]{1,0:T(8,128)(2,1)S(1)}, bf16[32,1024]{1,0:T(8,128)(2,1)S(1)}, u32[]{:S(2)}, u32[]{:S(2)}) collective-permute-start(bf16[32,1024]{1,0:T(8,128)(2,1)S(1)} %get-tuple-element.18), channel_id=1, source_target_pairs={{0,8},{4,12},{8,0},{12,4},{1,9},{5,13},{9,1},{13,5},{2,10},{6,14},... | collective-permute-start | bytes 196616 | tf_op jit(solution)/shard_map/ppermute | solution.py:144
  35.0 0.8 %project.5.acc_ref = f32[64,2048]{1,0:T(8,128)S(1)} custom-call(bf16[64,1024]{1,0:T(8,128)(2,1)S(1)} %collective-permute-done.6.x_ref, bf16[1024,2048]{1,0:T(8,128)(2,1)S(1)} %get-tuple-element.20.w_ref, f32[64,2048]{1,0:T(8,128)S(1)} %get-tuple-element.21.acc_ref), custom_call_target="tpu_custom_call" | custom-call | flops 268435456 | bytes 4194304 | tf_op jit(solution)/shard_map/project/pallas_call | solution.py:440
  35.9 0.8 %project.7 = bf16[32,2048]{1,0:T(8,128)(2,1)S(1)} custom-call(bf16[32,1024]{1,0:T(8,128)(2,1)S(1)} %collective-permute-done.7.x_ref, bf16[1024,2048]{1,0:T(8,128)(2,1)S(1)} %get-tuple-element.19.w_ref, f32[64,2048]{1,0:T(8,128)S(1)} %project.5.acc_ref), custom_call_target="tpu_custom_call" | custom-call | flops 134217728 | bytes 4194304 | tf_op jit(solution)/shard_map/project/pallas_call | solution.py:440
  36.7 1.5 %collective-permute-start.8 = (bf16[32,2048]{1,0:T(8,128)(2,1)S(1)}, bf16[32,2048]{1,0:T(8,128)(2,1)S(1)}, u32[]{:S(2)}, u32[]{:S(2)}) collective-permute-start(bf16[32,2048]{1,0:T(8,128)(2,1)S(1)} %project.7), channel_id=1, source_target_pairs={{0,2},{2,0},{1,3},{3,1},{4,6},{6,4},{5,7},{7,5},{8,10},{10,8},{9,1... | collective-permute-start | bytes 393224 | tf_op jit(solution)/shard_map/ppermute | solution.py:144
  38.2 1.1 %collective-permute-done.5.refs_0_ = bf16[32,1024]{1,0:T(8,128)(2,1)S(1)} collective-permute-done((bf16[32,1024]{1,0:T(8,128)(2,1)S(1)}, bf16[32,1024]{1,0:T(8,128)(2,1)S(1)}, u32[]{:S(2)}, u32[]{:S(2)}) %collective-permute-start.5) | collective-permute-done | bytes 65568 | tf_op jit(solution)/shard_map/ppermute | solution.py:144
  39.3 0.8 %project.6.refs_0_ = f32[32,2048]{1,0:T(8,128)S(1)} custom-call(bf16[32,1024]{1,0:T(8,128)(2,1)S(1)} %settle.3.x_ref, bf16[1024,2048]{1,0:T(8,128)(2,1)S(1)} %get-tuple-element.19.w_ref, f32[64,2048]{1,0:T(8,128)S(1)} %project.5.acc_ref), custom_call_target="tpu_custom_call" | custom-call | flops 134217728 | bytes 4194304 | tf_op jit(solution)/shard_map/project/pallas_call | solution.py:440
  40.1 1.6 %collective-permute-done.8.refs_1_ = bf16[32,2048]{1,0:T(8,128)(2,1)S(1)} collective-permute-done((bf16[32,2048]{1,0:T(8,128)(2,1)S(1)}, bf16[32,2048]{1,0:T(8,128)(2,1)S(1)}, u32[]{:S(2)}, u32[]{:S(2)}) %collective-permute-start.8) | collective-permute-done | bytes 131104 | tf_op jit(solution)/shard_map/ppermute | solution.py:144
  41.7 0.7 %add.21 = bf16[1,32,2048]{2,1,0:T(8,128)(2,1)} custom-call(f32[32,2048]{1,0:T(8,128)S(1)} %project.6.refs_0_, bf16[32,2048]{1,0:T(8,128)(2,1)S(1)} %collective-permute-done.8.refs_1_), custom_call_target="tpu_custom_call" | custom-call | bytes 524288 | tf_op jit(solution)/shard_map/add/pallas_call | solution.py:464
  (15 shorter events, 0.2 us)
Async XLA Ops:
  1.2 17.7 %collective-permute-start = (bf16[1024,128]{1,0:T(8,128)(2,1)S(1)}, bf16[1024,128]{1,0:T(8,128)(2,1)S(1)}, u32[]{:S(2)}, u32[]{:S(2)}) collective-permute-start(bf16[1024,128]{1,0:T(8,128)(2,1)S(1)} %pad_maximum_fusion.1), channel_id=1, source_target_pairs={{0,8},{1,13},{4,12},{5,9},{8,0},{9,5},{12,4},{13,1},{2,10},{3,15},... | collective-permute-start | bytes 786440 | tf_op jit(solution)/shard_map/ppermute | solution.py:150
  7.0 11.9 %collective-permute-start.2 = (bf16[512,128]{1,0:T(8,128)(2,1)S(1)}, bf16[512,128]{1,0:T(8,128)(2,1)S(1)}, u32[]{:S(2)}, u32[]{:S(2)}) collective-permute-start(bf16[512,128]{1,0:T(8,128)(2,1)S(1)} %pad_maximum_fusion.2), channel_id=1, source_target_pairs={{0,4},{4,0},{8,12},{12,8},{1,5},{5,1},{9,13},{13,9},{2,6},{6,2},{1... | collective-permute-start | bytes 393224 | tf_op jit(solution)/shard_map/ppermute | solution.py:144
  10.2 10.9 %all-to-all-start = ((bf16[8,8,1280]{2,1,0:T(8,128)(2,1)}), bf16[8,8,1280]{2,1,0:T(8,128)(2,1)S(1)}, u32[]{:S(2)}, u32[]{:S(2)}) async-start(bf16[8,8,1280]{2,1,0:T(8,128)(2,1)} %bitcast.6), calls=%async_computation | async-start | bytes 327680 | tf_op jit(solution)/shard_map/all_to_all | solution.py:496
  13.6 5.8 %copy-start = (s32[1,64]{1,0:T(1,128)S(1)}, s32[1,64]{1,0:T(1,128)}, u32[]{:S(2)}) copy-start(s32[1,64]{1,0:T(1,128)} %visible_ref.1) | copy-start | bytes 772
  18.9 2.3 %collective-permute-start.1 = (bf16[1024,128]{1,0:T(8,128)(2,1)S(1)}, bf16[1024,128]{1,0:T(8,128)(2,1)S(1)}, u32[]{:S(2)}, u32[]{:S(2)}) collective-permute-start(bf16[1024,128]{1,0:T(8,128)(2,1)S(1)} %settle.2.refs_0_), channel_id=1, source_target_pairs={{0,1},{1,0},{2,3},{3,2},{4,5},{5,4},{6,7},{7,6},{8,9},{9,8},{10,11... | collective-permute-start | bytes 786440 | tf_op jit(solution)/shard_map/ppermute | solution.py:144
  18.9 1.7 %collective-permute-start.3 = (bf16[512,128]{1,0:T(8,128)(2,1)S(1)}, bf16[512,128]{1,0:T(8,128)(2,1)S(1)}, u32[]{:S(2)}, u32[]{:S(2)}) collective-permute-start(bf16[512,128]{1,0:T(8,128)(2,1)S(1)} %collective-permute-done.2.refs_2_), channel_id=1, source_target_pairs={{0,1},{1,0},{2,3},{3,2},{4,5},{5,4},{6,7},{7,6},{8,9},{9,8},{10,11... | collective-permute-start | bytes 393224 | tf_op jit(solution)/shard_map/ppermute | solution.py:144
  23.3 9.2 %collective-permute-start.4 = (bf16[64,1024]{1,0:T(8,128)(2,1)S(1)}, bf16[64,1024]{1,0:T(8,128)(2,1)S(1)}, u32[]{:S(2)}, u32[]{:S(2)}) collective-permute-start(bf16[64,1024]{1,0:T(8,128)(2,1)S(1)} %get-tuple-element.14.x_ref.refs_0_), channel_id=1, source_target_pairs={{0,12},{4,8},{8,4},{12,0},{1,13},{5,9},{9,5},{13,1},{2,14},{6,10},... | collective-permute-start | bytes 393224 | tf_op jit(solution)/shard_map/ppermute | solution.py:144
  26.5 8.6 %collective-permute-start.6 = (bf16[64,1024]{1,0:T(8,128)(2,1)S(1)}, bf16[64,1024]{1,0:T(8,128)(2,1)S(1)}, u32[]{:S(2)}, u32[]{:S(2)}) collective-permute-start(bf16[64,1024]{1,0:T(8,128)(2,1)S(1)} %get-tuple-element.14.x_ref.refs_0_), channel_id=1, source_target_pairs={{0,4},{4,0},{8,12},{12,8},{1,5},{5,1},{9,13},{13,9},{2,6},{6,2},{1... | collective-permute-start | bytes 393224 | tf_op jit(solution)/shard_map/ppermute | solution.py:144
  26.5 9.4 %collective-permute-start.7 = (bf16[32,1024]{1,0:T(8,128)(2,1)S(1)}, bf16[32,1024]{1,0:T(8,128)(2,1)S(1)}, u32[]{:S(2)}, u32[]{:S(2)}) collective-permute-start(bf16[32,1024]{1,0:T(8,128)(2,1)S(1)} %get-tuple-element.22), channel_id=1, source_target_pairs={{0,8},{4,12},{8,0},{12,4},{1,9},{5,13},{9,1},{13,5},{2,10},{6,14},... | collective-permute-start | bytes 196616 | tf_op jit(solution)/shard_map/ppermute | solution.py:144
  33.4 5.9 %collective-permute-start.5 = (bf16[32,1024]{1,0:T(8,128)(2,1)S(1)}, bf16[32,1024]{1,0:T(8,128)(2,1)S(1)}, u32[]{:S(2)}, u32[]{:S(2)}) collective-permute-start(bf16[32,1024]{1,0:T(8,128)(2,1)S(1)} %get-tuple-element.18), channel_id=1, source_target_pairs={{0,8},{4,12},{8,0},{12,4},{1,9},{5,13},{9,1},{13,5},{2,10},{6,14},... | collective-permute-start | bytes 196616 | tf_op jit(solution)/shard_map/ppermute | solution.py:144
  36.7 5.0 %collective-permute-start.8 = (bf16[32,2048]{1,0:T(8,128)(2,1)S(1)}, bf16[32,2048]{1,0:T(8,128)(2,1)S(1)}, u32[]{:S(2)}, u32[]{:S(2)}) collective-permute-start(bf16[32,2048]{1,0:T(8,128)(2,1)S(1)} %project.7), channel_id=1, source_target_pairs={{0,2},{2,0},{1,3},{3,1},{4,6},{6,4},{5,7},{7,5},{8,10},{10,8},{9,1... | collective-permute-start | bytes 393224 | tf_op jit(solution)/shard_map/ppermute | solution.py:144

commit v9 on v7

--- a/solution.py
+++ b/solution.py
@@ -131,7 +131,7 @@
 EXPONENT = SCALE * math.log2(math.e)
 VMEM_BYTES = 20 * 2**20
 UNIT_ROWS = 256
-FETCHES = 1
+FETCHES = 2
 SETTLE_FIRST = 10**11
 SETTLE_LAST = 10**10
 PACK_BYTES = 56 * 2**20

time: 42.7 us -> 42.8 us (level)
  no operation moved by 1% of the time
where the time goes in v9:
time: 42.8 us; the launch traced here: 42.4 us
  starting transfers between devices  17.3 us (40%)
  Pallas kernels  12.7 us (30%)
  waiting for transfers between devices  9.5 us (22%)
  local copies, waits for them, and re-layouts  2.83 us (7%)
    ppermute x8, starting transfers between devices, swap(): lax.ppermute(array, axis, [(i, i ^ mask) for i in range(lax.axis_size(axi...  9.77 us
    ppermute x1, waiting for transfers between devices, swap_by_core(): return lax.ppermute(array, ('seq', 'rep'), pairs)  5.24 us
    pallas_call x1, Pallas kernels, load(): pl.pallas_call(functools.partial(load_kernel, masks), out_shape=[jax.Shap...  4.71 us
    ppermute x1, starting transfers between devices, swap_by_core(): return lax.ppermute(array, ('seq', 'rep'), pairs)  4.1 us
    ppermute x8, waiting for transfers between devices, swap(): lax.ppermute(array, axis, [(i, i ^ mask) for i in range(lax.axis_size(axi...  3.73 us
    all_to_all x1, starting transfers between devices, shards_by_head(): lax.all_to_all(pack_queries(rows, 1 + len(masks)), ('seq', 'tp'), split_a...  3.39 us
    pallas_call x4, Pallas kernels, project(): pl.pallas_call(functools.partial(project_kernel, side, pass_on is not Non...  3.35 us
    dynamic_slice x3, local copies, waits for them, and re-layouts, cut(): lax.dynamic_slice(table, (first, head * HEAD_WIDTH), (count, HEAD_WIDTH))  2.83 us
  transfers between devices with their start and end apart: 10, of which 5 were waited for; matrix products, arithmetic and copies ran while one was open for 4% of the time, Pallas kernels for 23%

profile of v9, /device:TPU:0, one launch (start us, length us, event | category | flops | bytes accessed | tf_op | source)
XLA Modules:
  0.0 42.4 jit_solution(6468040682529985516)
XLA Ops:
  0.0 1.1 %constant_dynamic-slice_fusion = (bf16[512,128]{1,0:T(8,128)(2,1)S(1)}, bf16[512,128]{1,0:T(8,128)(2,1)S(1)}, bf16[512,128]{1,0:T(8,128)(2,1)S(1)}, bf16[512,128]{1,0:T(8,128)(2,1)S(1)}) fusion(bf16[512,512]{1,0:T(8,128)(2,1)} %param.12, s32[]{:T(128)S(6)} %select_n.17, s32[]{:T(128)S(6)} %select_n.16, bf16[512,512]{1,0:T(8,128)(2,1)} %param.11), kind=kLoop, calls=%fused_computation.3 | loop fusion | bytes 1048584 | tf_op jit(solution)/shard_map/dynamic_slice | solution.py:487
  1.2 4.1 %collective-permute-start = (bf16[1024,128]{1,0:T(8,128)(2,1)S(1)}, bf16[1024,128]{1,0:T(8,128)(2,1)S(1)}, u32[]{:S(2)}, u32[]{:S(2)}) collective-permute-start(bf16[1024,128]{1,0:T(8,128)(2,1)S(1)} %pad_maximum_fusion.1), channel_id=1, source_target_pairs={{0,8},{1,13},{4,12},{5,9},{8,0},{9,5},{12,4},{13,1},{2,10},{3,15},... | collective-permute-start | bytes 786440 | tf_op jit(solution)/shard_map/ppermute | solution.py:150
  5.3 0.8 %dynamic_slice.22 = bf16[256,128]{1,0:T(8,128)(2,1)S(1)} dynamic-slice(bf16[512,512]{1,0:T(8,128)(2,1)} %param.11, s32[]{:T(128)S(6)} %select_n.18, s32[]{:T(128)S(6)} %select_n.19), dynamic_slice_sizes={256,128} | dynamic-slice | bytes 131076 | tf_op jit(solution)/shard_map/dynamic_slice | solution.py:487
  6.1 0.8 %dynamic_slice.23 = bf16[256,128]{1,0:T(8,128)(2,1)S(1)} dynamic-slice(bf16[512,512]{1,0:T(8,128)(2,1)} %param.12, s32[]{:T(128)S(6)} %select_n.18, s32[]{:T(128)S(6)} %select_n.19), dynamic_slice_sizes={256,128} | dynamic-slice | bytes 131076 | tf_op jit(solution)/shard_map/dynamic_slice | solution.py:487
  7.0 1.6 %collective-permute-start.2 = (bf16[512,128]{1,0:T(8,128)(2,1)S(1)}, bf16[512,128]{1,0:T(8,128)(2,1)S(1)}, u32[]{:S(2)}, u32[]{:S(2)}) collective-permute-start(bf16[512,128]{1,0:T(8,128)(2,1)S(1)} %pad_maximum_fusion.2), channel_id=1, source_target_pairs={{0,4},{4,0},{8,12},{12,8},{1,5},{5,1},{9,13},{13,9},{2,6},{6,2},{1... | collective-permute-start | bytes 393224 | tf_op jit(solution)/shard_map/ppermute | solution.py:144
  8.6 1.6 %pack_queries.1 = bf16[64,1280]{1,0:T(8,128)(2,1)} custom-call(bf16[8,8192]{1,0:T(8,128)(2,1)} %bitcast.7, bf16[8,1024]{1,0:T(8,128)(2,1)} %bitcast.8, bf16[8,1024]{1,0:T(8,128)(2,1)} %bitcast.9), custom_call_target="tpu_custom_call" | custom-call | bytes 524288 | tf_op jit(solution)/shard_map/pack_queries/pallas_call | solution.py:205
  10.2 3.4 %all-to-all-start = ((bf16[8,8,1280]{2,1,0:T(8,128)(2,1)}), bf16[8,8,1280]{2,1,0:T(8,128)(2,1)S(1)}, u32[]{:S(2)}, u32[]{:S(2)}) async-start(bf16[8,8,1280]{2,1,0:T(8,128)(2,1)} %bitcast.6), calls=%async_computation | async-start | bytes 327680 | tf_op jit(solution)/shard_map/all_to_all | solution.py:496
  13.6 5.2 %collective-permute-done.refs_0_ = bf16[1024,128]{1,0:T(8,128)(2,1)S(1)} collective-permute-done((bf16[1024,128]{1,0:T(8,128)(2,1)S(1)}, bf16[1024,128]{1,0:T(8,128)(2,1)S(1)}, u32[]{:S(2)}, u32[]{:S(2)}) %collective-permute-start) | collective-permute-done | bytes 262176 | tf_op jit(solution)/shard_map/ppermute | solution.py:150
  18.9 0.5 %collective-permute-start.3 = (bf16[512,128]{1,0:T(8,128)(2,1)S(1)}, bf16[512,128]{1,0:T(8,128)(2,1)S(1)}, u32[]{:S(2)}, u32[]{:S(2)}) collective-permute-start(bf16[512,128]{1,0:T(8,128)(2,1)S(1)} %collective-permute-done.2.refs_2_), channel_id=1, source_target_pairs={{0,1},{1,0},{2,3},{3,2},{4,5},{5,4},{6,7},{7,6},{8,9},{9,8},{10,11... | collective-permute-start | bytes 393224 | tf_op jit(solution)/shard_map/ppermute | solution.py:144
  19.5 1.1 %collective-permute-done.3.refs_3_ = bf16[512,128]{1,0:T(8,128)(2,1)S(1)} collective-permute-done((bf16[512,128]{1,0:T(8,128)(2,1)S(1)}, bf16[512,128]{1,0:T(8,128)(2,1)S(1)}, u32[]{:S(2)}, u32[]{:S(2)}) %collective-permute-start.3) | collective-permute-done | bytes 131104 | tf_op jit(solution)/shard_map/ppermute | solution.py:144
  20.6 0.5 %all-to-all-done = bf16[8,8,1280]{2,1,0:T(8,128)(2,1)S(1)} async-done(((bf16[8,8,1280]{2,1,0:T(8,128)(2,1)}), bf16[8,8,1280]{2,1,0:T(8,128)(2,1)S(1)}, u32[]{:S(2)}, u32[]{:S(2)}) %all-to-all-start) | async-done | bytes 163872 | tf_op jit(solution)/shard_map/all_to_all | solution.py:496
  21.1 2.2 %attend.1 = (bf16[64,1024]{1,0:T(8,128)(2,1)S(1)}, bf16[32,1024]{1,0:T(8,128)(2,1)S(1)}, bf16[1024,2048]{1,0:T(8,128)(2,1)S(1)}) custom-call(bf16[64,1280]{1,0:T(8,128)(2,1)S(1)} %bitcast.5, s32[64,128]{1,0:T(8,128)S(1)} %spread_lengths.1.lengths_ref, bf16[1024,128]{1,0:T(8,128)(2,1)S(1)} %pad_maximum_fusion.own_ref, bf16[1024,128]{1,0:T(8,128)(2,1)S(1)} %settle.2.refs_0_, ...), custom_call_target="tpu_custom_call" | custom-call | flops 805306368 | bytes 1048576 | tf_op jit(solution)/shard_map/attend/pallas_call | solution.py:366
  23.4 3.1 %collective-permute-start.4 = (bf16[64,1024]{1,0:T(8,128)(2,1)S(1)}, bf16[64,1024]{1,0:T(8,128)(2,1)S(1)}, u32[]{:S(2)}, u32[]{:S(2)}) collective-permute-start(bf16[64,1024]{1,0:T(8,128)(2,1)S(1)} %get-tuple-element.14.x_ref.refs_0_), channel_id=1, source_target_pairs={{0,12},{4,8},{8,4},{12,0},{1,13},{5,9},{9,5},{13,1},{2,14},{6,10},... | collective-permute-start | bytes 393224 | tf_op jit(solution)/shard_map/ppermute | solution.py:144
  26.5 1.3 %collective-permute-start.7 = (bf16[32,1024]{1,0:T(8,128)(2,1)S(1)}, bf16[32,1024]{1,0:T(8,128)(2,1)S(1)}, u32[]{:S(2)}, u32[]{:S(2)}) collective-permute-start(bf16[32,1024]{1,0:T(8,128)(2,1)S(1)} %get-tuple-element.22), channel_id=1, source_target_pairs={{0,8},{4,12},{8,0},{12,4},{1,9},{5,13},{9,1},{13,5},{2,10},{6,14},... | collective-permute-start | bytes 196616 | tf_op jit(solution)/shard_map/ppermute | solution.py:144
  27.8 4.7 %load.1 = (f32[64,2048]{1,0:T(8,128)S(1)}, bf16[1024,2048]{1,0:T(8,128)(2,1)S(1)}, bf16[1024,2048]{1,0:T(8,128)(2,1)S(1)}, bf16[1024,2048]{1,0:T(8,128)(2,1)S(1)}) custom-call(bf16[4096,2048]{1,0:T(8,128)(2,1)} %weight_ref.1, bf16[64,1024]{1,0:T(8,128)(2,1)S(1)} %get-tuple-element.14.x_ref.refs_0_, bf16[1024,2048]{1,0:T(8,128)(2,1)S(1)} %get-tuple-element.15.first_ref), custom_call_target="tpu_custom_call" | custom-call | flops 268435456 | bytes 12582912 | tf_op jit(solution)/shard_map/load/pallas_call | solution.py:402
  32.6 0.8 %project.4 = (f32[64,2048]{1,0:T(8,128)S(1)}, bf16[32,1024]{1,0:T(8,128)(2,1)S(1)}) custom-call(bf16[64,1024]{1,0:T(8,128)(2,1)S(1)} %collective-permute-done.4.x_ref, bf16[1024,2048]{1,0:T(8,128)(2,1)S(1)} %get-tuple-element.16.w_ref, f32[64,2048]{1,0:T(8,128)S(1)} %get-tuple-element.17.acc_ref, bf16[64,1024]{1,0:T(8,128)(2,1)S(1)} %get-tuple-element.14.x_ref.refs_0_), custom_call_target="tpu_custom_call" | custom-call | flops 268435456 | bytes 4194304 | tf_op jit(solution)/shard_map/project/pallas_call | solution.py:440
  33.4 1.7 %collective-permute-start.5 = (bf16[32,1024]{1,0:T(8,128)(2,1)S(1)}, bf16[32,1024]{1,0:T(8,128)(2,1)S(1)}, u32[]{:S(2)}, u32[]{:S(2)}) collective-permute-start(bf16[32,1024]{1,0:T(8,128)(2,1)S(1)} %get-tuple-element.18), channel_id=1, source_target_pairs={{0,8},{4,12},{8,0},{12,4},{1,9},{5,13},{9,1},{13,5},{2,10},{6,14},... | collective-permute-start | bytes 196616 | tf_op jit(solution)/shard_map/ppermute | solution.py:144
  35.1 0.8 %project.5.acc_ref = f32[64,2048]{1,0:T(8,128)S(1)} custom-call(bf16[64,1024]{1,0:T(8,128)(2,1)S(1)} %collective-permute-done.6.x_ref, bf16[1024,2048]{1,0:T(8,128)(2,1)S(1)} %get-tuple-element.20.w_ref, f32[64,2048]{1,0:T(8,128)S(1)} %get-tuple-element.21.acc_ref), custom_call_target="tpu_custom_call" | custom-call | flops 268435456 | bytes 4194304 | tf_op jit(solution)/shard_map/project/pallas_call | solution.py:440
  36.0 0.8 %project.7 = bf16[32,2048]{1,0:T(8,128)(2,1)S(1)} custom-call(bf16[32,1024]{1,0:T(8,128)(2,1)S(1)} %collective-permute-done.7.x_ref, bf16[1024,2048]{1,0:T(8,128)(2,1)S(1)} %get-tuple-element.19.w_ref, f32[64,2048]{1,0:T(8,128)S(1)} %project.5.acc_ref), custom_call_target="tpu_custom_call" | custom-call | flops 134217728 | bytes 4194304 | tf_op jit(solution)/shard_map/project/pallas_call | solution.py:440
  36.8 1.5 %collective-permute-start.8 = (bf16[32,2048]{1,0:T(8,128)(2,1)S(1)}, bf16[32,2048]{1,0:T(8,128)(2,1)S(1)}, u32[]{:S(2)}, u32[]{:S(2)}) collective-permute-start(bf16[32,2048]{1,0:T(8,128)(2,1)S(1)} %project.7), channel_id=1, source_target_pairs={{0,2},{2,0},{1,3},{3,1},{4,6},{6,4},{5,7},{7,5},{8,10},{10,8},{9,1... | collective-permute-start | bytes 393224 | tf_op jit(solution)/shard_map/ppermute | solution.py:144
  38.3 1.1 %collective-permute-done.5.refs_0_ = bf16[32,1024]{1,0:T(8,128)(2,1)S(1)} collective-permute-done((bf16[32,1024]{1,0:T(8,128)(2,1)S(1)}, bf16[32,1024]{1,0:T(8,128)(2,1)S(1)}, u32[]{:S(2)}, u32[]{:S(2)}) %collective-permute-start.5) | collective-permute-done | bytes 65568 | tf_op jit(solution)/shard_map/ppermute | solution.py:144
  39.4 0.8 %project.6.refs_0_ = f32[32,2048]{1,0:T(8,128)S(1)} custom-call(bf16[32,1024]{1,0:T(8,128)(2,1)S(1)} %settle.3.x_ref, bf16[1024,2048]{1,0:T(8,128)(2,1)S(1)} %get-tuple-element.19.w_ref, f32[64,2048]{1,0:T(8,128)S(1)} %project.5.acc_ref), custom_call_target="tpu_custom_call" | custom-call | flops 134217728 | bytes 4194304 | tf_op jit(solution)/shard_map/project/pallas_call | solution.py:440
  40.2 1.6 %collective-permute-done.8.refs_1_ = bf16[32,2048]{1,0:T(8,128)(2,1)S(1)} collective-permute-done((bf16[32,2048]{1,0:T(8,128)(2,1)S(1)}, bf16[32,2048]{1,0:T(8,128)(2,1)S(1)}, u32[]{:S(2)}, u32[]{:S(2)}) %collective-permute-start.8) | collective-permute-done | bytes 131104 | tf_op jit(solution)/shard_map/ppermute | solution.py:144
  41.8 0.7 %add.21 = bf16[1,32,2048]{2,1,0:T(8,128)(2,1)} custom-call(f32[32,2048]{1,0:T(8,128)S(1)} %project.6.refs_0_, bf16[32,2048]{1,0:T(8,128)(2,1)S(1)} %collective-permute-done.8.refs_1_), custom_call_target="tpu_custom_call" | custom-call | bytes 524288 | tf_op jit(solution)/shard_map/add/pallas_call | solution.py:464
  (15 shorter events, 0.2 us)
Async XLA Ops:
  1.2 17.7 %collective-permute-start = (bf16[1024,128]{1,0:T(8,128)(2,1)S(1)}, bf16[1024,128]{1,0:T(8,128)(2,1)S(1)}, u32[]{:S(2)}, u32[]{:S(2)}) collective-permute-start(bf16[1024,128]{1,0:T(8,128)(2,1)S(1)} %pad_maximum_fusion.1), channel_id=1, source_target_pairs={{0,8},{1,13},{4,12},{5,9},{8,0},{9,5},{12,4},{13,1},{2,10},{3,15},... | collective-permute-start | bytes 786440 | tf_op jit(solution)/shard_map/ppermute | solution.py:150
  7.0 11.9 %collective-permute-start.2 = (bf16[512,128]{1,0:T(8,128)(2,1)S(1)}, bf16[512,128]{1,0:T(8,128)(2,1)S(1)}, u32[]{:S(2)}, u32[]{:S(2)}) collective-permute-start(bf16[512,128]{1,0:T(8,128)(2,1)S(1)} %pad_maximum_fusion.2), channel_id=1, source_target_pairs={{0,4},{4,0},{8,12},{12,8},{1,5},{5,1},{9,13},{13,9},{2,6},{6,2},{1... | collective-permute-start | bytes 393224 | tf_op jit(solution)/shard_map/ppermute | solution.py:144
  10.2 10.9 %all-to-all-start = ((bf16[8,8,1280]{2,1,0:T(8,128)(2,1)}), bf16[8,8,1280]{2,1,0:T(8,128)(2,1)S(1)}, u32[]{:S(2)}, u32[]{:S(2)}) async-start(bf16[8,8,1280]{2,1,0:T(8,128)(2,1)} %bitcast.6), calls=%async_computation | async-start | bytes 327680 | tf_op jit(solution)/shard_map/all_to_all | solution.py:496
  13.6 5.8 %copy-start = (s32[1,64]{1,0:T(1,128)S(1)}, s32[1,64]{1,0:T(1,128)}, u32[]{:S(2)}) copy-start(s32[1,64]{1,0:T(1,128)} %visible_ref.1) | copy-start | bytes 772
  18.9 2.3 %collective-permute-start.1 = (bf16[1024,128]{1,0:T(8,128)(2,1)S(1)}, bf16[1024,128]{1,0:T(8,128)(2,1)S(1)}, u32[]{:S(2)}, u32[]{:S(2)}) collective-permute-start(bf16[1024,128]{1,0:T(8,128)(2,1)S(1)} %settle.2.refs_0_), channel_id=1, source_target_pairs={{0,1},{1,0},{2,3},{3,2},{4,5},{5,4},{6,7},{7,6},{8,9},{9,8},{10,11... | collective-permute-start | bytes 786440 | tf_op jit(solution)/shard_map/ppermute | solution.py:144
  18.9 1.7 %collective-permute-start.3 = (bf16[512,128]{1,0:T(8,128)(2,1)S(1)}, bf16[512,128]{1,0:T(8,128)(2,1)S(1)}, u32[]{:S(2)}, u32[]{:S(2)}) collective-permute-start(bf16[512,128]{1,0:T(8,128)(2,1)S(1)} %collective-permute-done.2.refs_2_), channel_id=1, source_target_pairs={{0,1},{1,0},{2,3},{3,2},{4,5},{5,4},{6,7},{7,6},{8,9},{9,8},{10,11... | collective-permute-start | bytes 393224 | tf_op jit(solution)/shard_map/ppermute | solution.py:144
  23.4 9.2 %collective-permute-start.4 = (bf16[64,1024]{1,0:T(8,128)(2,1)S(1)}, bf16[64,1024]{1,0:T(8,128)(2,1)S(1)}, u32[]{:S(2)}, u32[]{:S(2)}) collective-permute-start(bf16[64,1024]{1,0:T(8,128)(2,1)S(1)} %get-tuple-element.14.x_ref.refs_0_), channel_id=1, source_target_pairs={{0,12},{4,8},{8,4},{12,0},{1,13},{5,9},{9,5},{13,1},{2,14},{6,10},... | collective-permute-start | bytes 393224 | tf_op jit(solution)/shard_map/ppermute | solution.py:144
  26.5 8.6 %collective-permute-start.6 = (bf16[64,1024]{1,0:T(8,128)(2,1)S(1)}, bf16[64,1024]{1,0:T(8,128)(2,1)S(1)}, u32[]{:S(2)}, u32[]{:S(2)}) collective-permute-start(bf16[64,1024]{1,0:T(8,128)(2,1)S(1)} %get-tuple-element.14.x_ref.refs_0_), channel_id=1, source_target_pairs={{0,4},{4,0},{8,12},{12,8},{1,5},{5,1},{9,13},{13,9},{2,6},{6,2},{1... | collective-permute-start | bytes 393224 | tf_op jit(solution)/shard_map/ppermute | solution.py:144
  26.5 9.4 %collective-permute-start.7 = (bf16[32,1024]{1,0:T(8,128)(2,1)S(1)}, bf16[32,1024]{1,0:T(8,128)(2,1)S(1)}, u32[]{:S(2)}, u32[]{:S(2)}) collective-permute-start(bf16[32,1024]{1,0:T(8,128)(2,1)S(1)} %get-tuple-element.22), channel_id=1, source_target_pairs={{0,8},{4,12},{8,0},{12,4},{1,9},{5,13},{9,1},{13,5},{2,10},{6,14},... | collective-permute-start | bytes 196616 | tf_op jit(solution)/shard_map/ppermute | solution.py:144
  33.4 5.9 %collective-permute-start.5 = (bf16[32,1024]{1,0:T(8,128)(2,1)S(1)}, bf16[32,1024]{1,0:T(8,128)(2,1)S(1)}, u32[]{:S(2)}, u32[]{:S(2)}) collective-permute-start(bf16[32,1024]{1,0:T(8,128)(2,1)S(1)} %get-tuple-element.18), channel_id=1, source_target_pairs={{0,8},{4,12},{8,0},{12,4},{1,9},{5,13},{9,1},{13,5},{2,10},{6,14},... | collective-permute-start | bytes 196616 | tf_op jit(solution)/shard_map/ppermute | solution.py:144
  36.8 5.0 %collective-permute-start.8 = (bf16[32,2048]{1,0:T(8,128)(2,1)S(1)}, bf16[32,2048]{1,0:T(8,128)(2,1)S(1)}, u32[]{:S(2)}, u32[]{:S(2)}) collective-permute-start(bf16[32,2048]{1,0:T(8,128)(2,1)S(1)} %project.7), channel_id=1, source_target_pairs={{0,2},{2,0},{1,3},{3,1},{4,6},{6,4},{5,7},{7,5},{8,10},{10,8},{9,1... | collective-permute-start | bytes 393224 | tf_op jit(solution)/shard_map/ppermute | solution.py:144
